TPU v7x, 32 devices: a whole 2x2x4 slice. The times are simulated.
32 devices in a mesh: stream: 2 (over core), dp: 16 (over z, y, x).
Axes of the slice: x: 2, y: 2, z: 4, core: 2. Of those that a mesh axis runs over, the one named last changes fastest.
Arguments:
- hidden: float32 [2, 8192, 768], P('stream', 'dp'), may hold values from -6 to 6
- features: bfloat16 [256, 257, 1408], P('dp'), may hold values from -6 to 6
- caption_lengths: int32 [16, 32], P('dp'), may hold values from 1 to 32, 512 in all within a row
- caption_image: int32 [16, 32], P('dp'), may hold values from 0 to 15, as said below
- out_grad: float32 [2, 8192, 768], P('stream', 'dp'), may hold values from -6 to 6
- attn_project: float32 [3, 768, 768], P(None, 'dp'), may hold values from -0.21875 to 0.21875
- attn_output: float32 [2, 768, 768], P(None, 'dp'), may hold values from -0.625 to 0.625
- cross_query: float32 [768, 768], P('dp'), may hold values from -0.21875 to 0.21875
- cross_vision: float32 [2, 1408, 768], P(None, 'dp'), may hold values from -0.15625 to 0.15625
- feed_expand: float32 [2, 3072, 768], P('stream', 'dp'), may hold values from -0.21875 to 0.21875
- feed_reduce: float32 [2, 3072, 768], P('stream', 'dp'), may hold values from -0.109375 to 0.109375
- norm_gains: float32 [4, 768], P(None, 'dp'), may hold values from 0.3 to 2.4, as said below
- first_project: float32 [3, 768, 768], P(None, 'dp'), may hold values from -0.00018310547 to 0.00018310547
- second_project: float32 [3, 768, 768], P(None, 'dp'), may hold values from 6.6041964e-11 to 2.6416785e-10
- first_output: float32 [2, 768, 768], P(None, 'dp'), may hold values from -0.00018310547 to 0.00018310547
- second_output: float32 [2, 768, 768], P(None, 'dp'), may hold values from 6.6041964e-11 to 2.6416785e-10
- first_query: float32 [768, 768], P('dp'), may hold values from -0.00018310547 to 0.00018310547
- second_query: float32 [768, 768], P('dp'), may hold values from 6.6041964e-11 to 2.6416785e-10
- first_vision: float32 [2, 1408, 768], P(None, 'dp'), may hold values from -0.00018310547 to 0.00018310547
- second_vision: float32 [2, 1408, 768], P(None, 'dp'), may hold values from 6.6041964e-11 to 2.6416785e-10
- first_expand: float32 [2, 3072, 768], P('stream', 'dp'), may hold values from -0.00018310547 to 0.00018310547
- second_expand: float32 [2, 3072, 768], P('stream', 'dp'), may hold values from 6.6041964e-11 to 2.6416785e-10
- first_reduce: float32 [2, 3072, 768], P('stream', 'dp'), may hold values from -0.00018310547 to 0.00018310547
- second_reduce: float32 [2, 3072, 768], P('stream', 'dp'), may hold values from 6.6041964e-11 to 2.6416785e-10
- first_gains: float32 [4, 768], P(None, 'dp'), may hold values from -0.0007324219 to 0.0007324219
- second_gains: float32 [4, 768], P(None, 'dp'), may hold values from 1.0566714e-09 to 4.2266857e-09
Outputs:
- layer_output: float32 [2, 8192, 768], P('stream', 'dp')
- hidden_grad: float32 [2, 8192, 768], P('stream', 'dp')
- grad_norm: float32 [], replicated
- rms_values: float32 [2, 4], replicated
- fresh_project: float32 [3, 768, 768], P(None, 'dp')
- mean_project: float32 [3, 768, 768], P(None, 'dp')
- square_project: float32 [3, 768, 768], P(None, 'dp')
- fresh_output: float32 [2, 768, 768], P(None, 'dp')
- mean_output: float32 [2, 768, 768], P(None, 'dp')
- square_output: float32 [2, 768, 768], P(None, 'dp')
- fresh_query: float32 [768, 768], P('dp')
- mean_query: float32 [768, 768], P('dp')
- square_query: float32 [768, 768], P('dp')
- fresh_vision: float32 [2, 1408, 768], P(None, 'dp')
- mean_vision: float32 [2, 1408, 768], P(None, 'dp')
- square_vision: float32 [2, 1408, 768], P(None, 'dp')
- fresh_expand: float32 [2, 3072, 768], P('stream', 'dp')
- mean_expand: float32 [2, 3072, 768], P('stream', 'dp')
- square_expand: float32 [2, 3072, 768], P('stream', 'dp')
- fresh_reduce: float32 [2, 3072, 768], P('stream', 'dp')
- mean_reduce: float32 [2, 3072, 768], P('stream', 'dp')
- square_reduce: float32 [2, 3072, 768], P('stream', 'dp')
- fresh_gains: float32 [4, 768], P(None, 'dp')
- mean_gains: float32 [4, 768], P(None, 'dp')
- square_gains: float32 [4, 768], P(None, 'dp')
- gain_grads: float32 [4, 768], P(None, 'dp')
- copy_project: bfloat16 [3, 768, 768], P(None, 'dp')
- copy_output: bfloat16 [2, 768, 768], P(None, 'dp')
- copy_query: bfloat16 [768, 768], P('dp')
- copy_vision: bfloat16 [2, 1408, 768], P(None, 'dp')
- copy_expand: bfloat16 [2, 3072, 768], P('stream', 'dp')
- copy_reduce: bfloat16 [2, 3072, 768], P('stream', 'dp')
Inputs may be any that keep to these rules, and one draw needn't show every extreme that they name: `caption_lengths`: one index of dp's caption lengths fill its 512 text rows exactly, and one caption of each index has 32 tokens. `caption_image`: never falls along one index's captions; every image of an index has 1 to 5 captions, and some image of every index has 5. `norm_gains`: positive gains.
All inputs are finite; a program needn't handle non-finite values.
Results may differ from a plain program's by a relative error of at most 0.023.
Values may be sent and summed in bfloat16 or wider, within the bound.
A program may use at most 256 MiB of HBM per device.

v0:
```python
import jax
import jax.numpy as jnp
from jax import lax
from jax.sharding import PartitionSpec as P

HEADS = 12
HD = 64
NQ = 32
STEP = 10


epsilon = 1e-06
masked_value = -1e30
beta_first = 0.9
beta_second = 0.999
rate_matrix = 0.05
rate_gains = 1.0
decay_rate = 0.01
adam_floor = 1e-08
clip_norm = 1.0


def shifted(block, axis, distance):
    devices = range(lax.axis_size(axis))
    route = [(i - distance, i) for i in devices if i - distance in devices]
    return lax.ppermute(block, axis, route)


def to_half(values):
    return values.astype(jnp.bfloat16)


def product(left, right):
    return jnp.dot(left, right, preferred_element_type=jnp.float32)


def left_product(left, right):
    return lax.dot_general(
        left, right, (((0,), (0,)), ((), ())), preferred_element_type=jnp.float32
    )


def right_product(left, right):
    return lax.dot_general(
        left, right, (((1,), (1,)), ((), ())), preferred_element_type=jnp.float32
    )


def norm_rows(values, gain):
    return values * lax.rsqrt(jnp.mean(values * values, axis=-1, keepdims=True) + epsilon) * gain


def exact_gelu(values):
    return jax.nn.gelu(values, approximate=False)


def square_rows(values):
    return jnp.sum(jnp.mean(values * values, axis=-1))


def layout(lengths, owners, row_count, per_image):
    caption_ends = jnp.cumsum(lengths)
    caption_starts = caption_ends - lengths
    row_index = jnp.arange(row_count, dtype=jnp.int32)
    inside = (row_index[:, None] >= caption_starts[None, :]) & (
        row_index[:, None] < caption_ends[None, :]
    )
    caption = jnp.sum(
        jnp.where(inside, jnp.arange(lengths.shape[0], dtype=jnp.int32)[None, :], 0), axis=1
    )
    text_image = jnp.sum(jnp.where(inside, owners[None, :], 0), axis=1)
    query_image = row_index // per_image
    query_allow = query_image[:, None] == query_image[None, :]
    own_caption = (caption[:, None] == caption[None, :]) & (
        row_index[None, :] <= row_index[:, None]
    )
    text_allow = jnp.concatenate([text_image[:, None] == query_image[None, :], own_caption], axis=1)
    return (query_allow, text_allow)


def attention_scores(query_rows, key_rows, allowed):
    batch_count, query_count, width_all = query_rows.shape
    query_heads = query_rows.reshape(batch_count, query_count, HEADS, HD)
    key_heads = key_rows.reshape(batch_count, key_rows.shape[1], HEADS, HD)
    scores = jnp.einsum(
        "bqhd,bkhd->bhqk", query_heads, key_heads, preferred_element_type=jnp.float32
    ) * HD ** (-0.5)
    if allowed is not None:
        scores = jnp.where(allowed[:, None], scores, masked_value)
    return (scores, query_heads, key_heads)


def attend(query_rows, key_rows, value_rows, allowed):
    scores, query_heads, key_heads = attention_scores(query_rows, key_rows, allowed)
    value_heads = value_rows.reshape(key_heads.shape)
    row_max = jnp.max(scores, axis=-1, keepdims=True)
    weights = jnp.exp(scores - row_max)
    denominator = jnp.sum(weights, axis=-1, keepdims=True)
    probability = to_half(weights / denominator)
    context = jnp.einsum(
        "bhqk,bkhd->bqhd", probability, value_heads, preferred_element_type=jnp.float32
    )
    return (context.reshape(query_rows.shape), (row_max + jnp.log(denominator))[..., 0])


def attend_back(query_rows, key_rows, value_rows, allowed, log_total, grad_context):
    scores, query_heads, key_heads = attention_scores(query_rows, key_rows, allowed)
    value_heads = value_rows.reshape(key_heads.shape)
    probability = jnp.exp(scores - log_total[..., None])
    grad_heads = grad_context.reshape(query_heads.shape)
    grad_prob = jnp.einsum(
        "bqhd,bkhd->bhqk", grad_heads, value_heads, preferred_element_type=jnp.float32
    )
    grad_value = jnp.einsum(
        "bhqk,bqhd->bkhd", to_half(probability), grad_heads, preferred_element_type=jnp.float32
    )
    grad_score = to_half(
        probability * (grad_prob - jnp.sum(grad_prob * probability, axis=-1, keepdims=True))
    )
    grad_query = jnp.einsum(
        "bhqk,bkhd->bqhd", grad_score, key_heads, preferred_element_type=jnp.float32
    ) * HD ** (-0.5)
    grad_key = jnp.einsum(
        "bhqk,bqhd->bkhd", grad_score, query_heads, preferred_element_type=jnp.float32
    ) * HD ** (-0.5)
    return (
        grad_query.reshape(query_rows.shape),
        grad_key.reshape(key_rows.shape),
        grad_value.reshape(value_rows.shape),
    )


def project_vision(feature_block, vision_weights):
    return to_half(
        jnp.einsum(
            "inv,kvd->kind", feature_block, vision_weights, preferred_element_type=jnp.float32
        )
    )


def vision_grad(feature_block, grad_pair):
    return jnp.einsum("inv,kind->kvd", feature_block, grad_pair, preferred_element_type=jnp.float32)


def adam_step(weight, gradient, first, second, factor, rate, decay):
    clipped = gradient * factor
    mean_new = beta_first * first + (1.0 - beta_first) * clipped
    square_new = beta_second * second + (1.0 - beta_second) * clipped * clipped
    corrected_mean = mean_new / (1.0 - beta_first**STEP)
    corrected_square = square_new / (1.0 - beta_second**STEP)
    fresh = weight - rate * (
        corrected_mean / (jnp.sqrt(corrected_square) + adam_floor) + decay * weight
    )
    return (fresh, mean_new, square_new)


def body(
    hidden,
    features,
    caption_lengths,
    caption_image,
    out_grad,
    attn_project,
    attn_output,
    cross_query,
    cross_vision,
    feed_expand,
    feed_reduce,
    norm_gains,
    first_project,
    second_project,
    first_output,
    second_output,
    first_query,
    second_query,
    first_vision,
    second_vision,
    first_expand,
    second_expand,
    first_reduce,
    second_reduce,
    first_gains,
    second_gains,
):
    stream = lax.axis_index("stream")
    full_project, full_output, full_query, full_vision, full_expand, full_reduce, full_gains = (
        lax.all_gather(to_half(attn_project), "dp", axis=1, tiled=True),
        lax.all_gather(to_half(attn_output), "dp", axis=1, tiled=True),
        lax.all_gather(to_half(cross_query), "dp", axis=0, tiled=True),
        lax.all_gather(to_half(cross_vision), "dp", axis=1, tiled=True),
        lax.all_gather(to_half(feed_expand), "dp", axis=1, tiled=True),
        lax.all_gather(to_half(feed_reduce), "dp", axis=1, tiled=True),
        lax.all_gather(to_half(norm_gains), "dp", axis=1, tiled=True),
    )
    gain_rows = full_gains.astype(jnp.float32)
    gain_self = gain_rows[0]
    gain_cross = gain_rows[1]
    gain_feed = lax.dynamic_index_in_dim(gain_rows, 2 + stream, 0, keepdims=False)
    source = hidden[0]
    row_count = source.shape[0]
    feature_width = source.shape[1]
    image_count = features.shape[0]
    query_allow, text_allow = layout(caption_lengths[0], caption_image[0], row_count, NQ)
    normed_self = to_half(norm_rows(source, gain_self))
    query_half = to_half(product(normed_self, full_project[0]))
    key_half = to_half(product(normed_self, full_project[1]))
    value_half = to_half(product(normed_self, full_project[2]))
    empty_half = jnp.zeros((row_count, feature_width), jnp.bfloat16)
    far_key, far_value = shifted((key_half, value_half), "stream", 1)
    text_keys = jnp.concatenate([far_key, key_half], axis=0)
    text_values = jnp.concatenate([far_value, value_half], axis=0)

    def self_query():
        return attend(query_half[None], key_half[None], value_half[None], query_allow[None])

    def self_text():
        return attend(query_half[None], text_keys[None], text_values[None], text_allow[None])

    context_self, total_self = lax.cond(stream == 0, self_query, self_text)
    context_half = to_half(context_self[0])
    branch_self = product(context_half, full_output[0])
    after_self = source + branch_self

    def cross_on():
        normed_cross = to_half(norm_rows(after_self, gain_cross))
        cross_half = to_half(product(normed_cross, full_query))
        vision_pair = project_vision(features, full_vision)
        context_cross, total_cross = attend(
            cross_half.reshape(image_count, NQ, feature_width), vision_pair[0], vision_pair[1], None
        )
        context_cross_half = to_half(context_cross.reshape(row_count, feature_width))
        branch = product(context_cross_half, full_output[1])
        return (branch, total_cross, vision_pair, normed_cross, cross_half, context_cross_half)

    def cross_off():
        return (
            jnp.zeros((row_count, feature_width), jnp.float32),
            jnp.zeros((image_count, HEADS, NQ), jnp.float32),
            jnp.zeros((2, image_count, features.shape[1], feature_width), jnp.bfloat16),
            empty_half,
            empty_half,
            empty_half,
        )

    branch_cross, total_cross, vision_pair, normed_cross, cross_half, context_cross_half = lax.cond(
        stream == 0, cross_on, cross_off
    )
    after_cross = after_self + branch_cross
    normed_feed = to_half(norm_rows(after_cross, gain_feed))
    before = right_product(normed_feed, full_expand[0])
    active_half = to_half(exact_gelu(before))
    branch_feed = product(active_half, full_reduce[0])
    result = after_cross + branch_feed
    grad_result = out_grad[0]
    grad_feed_half = to_half(grad_result)
    grad_reduce = left_product(active_half, grad_feed_half)
    grad_active = right_product(grad_feed_half, full_reduce[0])
    grad_before = to_half(jax.vjp(exact_gelu, before)[1](grad_active)[0])
    grad_expand = left_product(grad_before, normed_feed)
    grad_normed_feed = product(grad_before, full_expand[0])
    feed_in, grad_gain_feed = jax.vjp(norm_rows, after_cross, gain_feed)[1](grad_normed_feed)
    grad_cross = grad_result + feed_in

    def cross_back_on():
        grad_branch_half = to_half(grad_cross)
        grad_out_cross = left_product(context_cross_half, grad_branch_half)
        grad_context = to_half(right_product(grad_branch_half, full_output[1]))
        grad_cq, grad_ck, grad_cv = attend_back(
            cross_half.reshape(image_count, NQ, feature_width),
            vision_pair[0],
            vision_pair[1],
            None,
            total_cross,
            grad_context.reshape(image_count, NQ, feature_width),
        )
        grad_cq_half = to_half(grad_cq.reshape(row_count, feature_width))
        grad_pair = to_half(jnp.stack([grad_ck, grad_cv]))
        grad_cross_weight = left_product(normed_cross, grad_cq_half)
        grad_normed_cross = right_product(grad_cq_half, full_query)
        cross_in, grad_gain_cross = jax.vjp(norm_rows, after_self, gain_cross)[1](grad_normed_cross)
        vision_term = vision_grad(features, grad_pair)
        return (cross_in, grad_gain_cross, grad_out_cross, grad_cross_weight, vision_term)

    def cross_back_off():
        square_zero = jnp.zeros((feature_width, feature_width), jnp.float32)
        vision_term = jnp.zeros((2, features.shape[2], feature_width), jnp.float32)
        return (
            jnp.zeros((row_count, feature_width), jnp.float32),
            jnp.zeros((feature_width,), jnp.float32),
            square_zero,
            square_zero,
            vision_term,
        )

    cross_in, grad_gain_cross, grad_out_cross, grad_cross_weight, vision_term = lax.cond(
        stream == 0, cross_back_on, cross_back_off
    )
    grad_after_self = grad_cross + cross_in
    grad_branch_half = to_half(grad_after_self)
    grad_out_self = left_product(context_half, grad_branch_half)
    grad_context_self = to_half(right_product(grad_branch_half, full_output[0]))

    def self_back_query():
        grad_sq, grad_sk, grad_sv = attend_back(
            query_half[None],
            key_half[None],
            value_half[None],
            query_allow[None],
            total_self,
            grad_context_self[None],
        )
        empty_rows = jnp.zeros((row_count, feature_width), jnp.float32)
        return (grad_sq[0], grad_sk[0], grad_sv[0], empty_rows, empty_rows)

    def self_back_text():
        grad_sq, grad_sk, grad_sv = attend_back(
            query_half[None],
            text_keys[None],
            text_values[None],
            text_allow[None],
            total_self,
            grad_context_self[None],
        )
        return (
            grad_sq[0],
            grad_sk[0, row_count:],
            grad_sv[0, row_count:],
            grad_sk[0, :row_count],
            grad_sv[0, :row_count],
        )

    own_query, own_key, own_value, far_grad_key, far_grad_value = lax.cond(
        stream == 0, self_back_query, self_back_text
    )
    own_query = to_half(own_query)
    own_key = to_half(own_key)
    own_value = to_half(own_value)
    far_key_half = to_half(far_grad_key)
    far_value_half = to_half(far_grad_value)
    grad_normed = (
        right_product(own_query, full_project[0])
        + right_product(own_key, full_project[1])
        + right_product(own_value, full_project[2])
    )
    grad_key_weight = left_product(normed_self, own_key)
    grad_value_weight = left_product(normed_self, own_value)
    back_key, back_value = shifted((far_key_half, far_value_half), "stream", -1)
    grad_normed = (
        grad_normed
        + right_product(back_key, full_project[1])
        + right_product(back_value, full_project[2])
    )
    grad_key_weight = grad_key_weight + left_product(normed_self, back_key)
    grad_value_weight = grad_value_weight + left_product(normed_self, back_value)
    grad_project = jnp.stack(
        [left_product(normed_self, own_query), grad_key_weight, grad_value_weight]
    )
    source_in, grad_gain_self = jax.vjp(norm_rows, source, gain_self)[1](grad_normed)
    hidden_grad = grad_after_self + source_in
    zero_row = jnp.zeros_like(grad_gain_feed)
    gain_grads = jnp.stack(
        [
            grad_gain_self,
            grad_gain_cross,
            jnp.where(stream == 0, grad_gain_feed, zero_row),
            jnp.where(stream == 1, grad_gain_feed, zero_row),
        ]
    )
    shared_grads = (
        grad_project,
        jnp.stack([grad_out_self, grad_out_cross]),
        grad_cross_weight,
        vision_term,
        gain_grads,
    )
    (
        parts_project,
        parts_output,
        parts_query,
        parts_vision,
        parts_expand,
        parts_reduce,
        parts_gains,
    ) = (
        lax.psum_scatter(shared_grads[0], "dp", scatter_dimension=1, tiled=True),
        lax.psum_scatter(shared_grads[1], "dp", scatter_dimension=1, tiled=True),
        lax.psum_scatter(shared_grads[2], "dp", scatter_dimension=0, tiled=True),
        lax.psum_scatter(shared_grads[3], "dp", scatter_dimension=1, tiled=True),
        lax.psum_scatter(grad_expand[None], "dp", scatter_dimension=1, tiled=True),
        lax.psum_scatter(grad_reduce[None], "dp", scatter_dimension=1, tiled=True),
        lax.psum_scatter(shared_grads[4], "dp", scatter_dimension=1, tiled=True),
    )
    sum_project, sum_output, sum_query, sum_vision, sum_gains = (
        lax.psum(parts_project.astype(jnp.bfloat16), "stream").astype(jnp.float32),
        lax.psum(parts_output.astype(jnp.bfloat16), "stream").astype(jnp.float32),
        lax.psum(parts_query.astype(jnp.bfloat16), "stream").astype(jnp.float32),
        lax.psum(parts_vision.astype(jnp.bfloat16), "stream").astype(jnp.float32),
        lax.psum(parts_gains.astype(jnp.bfloat16), "stream").astype(jnp.float32),
    )
    shared_square = (
        jnp.sum(sum_project * sum_project)
        + jnp.sum(sum_output * sum_output)
        + jnp.sum(sum_query * sum_query)
        + jnp.sum(sum_vision * sum_vision)
        + jnp.sum(sum_gains * sum_gains)
    )
    local_square = (
        0.5 * shared_square
        + jnp.sum(parts_expand * parts_expand)
        + jnp.sum(parts_reduce * parts_reduce)
    )
    stat_row = jnp.stack(
        [
            square_rows(source),
            square_rows(branch_self),
            square_rows(branch_feed),
            square_rows(result),
        ]
    )
    stat_local = jnp.where(
        jnp.arange(2, dtype=jnp.int32)[:, None] == stream, stat_row[None, :], 0.0
    )
    total_square, stat_sums = lax.psum((local_square, stat_local), ("stream", "dp"))
    grad_norm = jnp.sqrt(total_square)
    rms_values = jnp.sqrt(stat_sums / (row_count * lax.axis_size("dp")))
    factor = clip_norm / jnp.maximum(grad_norm, clip_norm)
    clipped_gains = sum_gains * factor
    fresh_expand, mean_expand, square_expand = adam_step(
        feed_expand, parts_expand, first_expand, second_expand, factor, rate_matrix, decay_rate
    )
    fresh_reduce, mean_reduce, square_reduce = adam_step(
        feed_reduce, parts_reduce, first_reduce, second_reduce, factor, rate_matrix, decay_rate
    )
    weights_shared = (attn_project, attn_output, cross_query, cross_vision, norm_gains)
    firsts_shared = (first_project, first_output, first_query, first_vision, first_gains)
    seconds_shared = (second_project, second_output, second_query, second_vision, second_gains)
    summed_shared = (sum_project, sum_output, sum_query, sum_vision, sum_gains)
    updated = []
    for index in range(5):
        rate = rate_gains if index == 4 else rate_matrix
        decay = 0.0 if index == 4 else decay_rate
        weight = weights_shared[index]
        first = firsts_shared[index]
        second = seconds_shared[index]
        updated.append(adam_step(weight, summed_shared[index], first, second, factor, rate, decay))
    fresh_project, mean_project, square_project = updated[0]
    fresh_output, mean_output, square_output = updated[1]
    fresh_query, mean_query, square_query = updated[2]
    fresh_vision, mean_vision, square_vision = updated[3]
    fresh_gains, mean_gains, square_gains = updated[4]
    return (
        result[None],
        hidden_grad[None],
        grad_norm,
        rms_values,
        fresh_project,
        mean_project,
        square_project,
        fresh_output,
        mean_output,
        square_output,
        fresh_query,
        mean_query,
        square_query,
        fresh_vision,
        mean_vision,
        square_vision,
        fresh_expand,
        mean_expand,
        square_expand,
        fresh_reduce,
        mean_reduce,
        square_reduce,
        fresh_gains,
        mean_gains,
        square_gains,
        clipped_gains,
        to_half(fresh_project),
        to_half(fresh_output),
        to_half(fresh_query),
        to_half(fresh_vision),
        to_half(fresh_expand),
        to_half(fresh_reduce),
    )


def solution(mesh):
    return jax.shard_map(
        body,
        mesh=mesh,
        in_specs=(
            P("stream", "dp", None),
            P("dp", None, None),
            P("dp", None),
            P("dp", None),
            P("stream", "dp", None),
            P(None, "dp", None),
            P(None, "dp", None),
            P("dp", None),
            P(None, "dp", None),
            P("stream", "dp", None),
            P("stream", "dp", None),
            P(None, "dp"),
            P(None, "dp", None),
            P(None, "dp", None),
            P(None, "dp", None),
            P(None, "dp", None),
            P("dp", None),
            P("dp", None),
            P(None, "dp", None),
            P(None, "dp", None),
            P("stream", "dp", None),
            P("stream", "dp", None),
            P("stream", "dp", None),
            P("stream", "dp", None),
            P(None, "dp"),
            P(None, "dp"),
        ),
        out_specs=(
            P("stream", "dp", None),
            P("stream", "dp", None),
            P(),
            P(),
            P(None, "dp", None),
            P(None, "dp", None),
            P(None, "dp", None),
            P(None, "dp", None),
            P(None, "dp", None),
            P(None, "dp", None),
            P("dp", None),
            P("dp", None),
            P("dp", None),
            P(None, "dp", None),
            P(None, "dp", None),
            P(None, "dp", None),
            P("stream", "dp", None),
            P("stream", "dp", None),
            P("stream", "dp", None),
            P("stream", "dp", None),
            P("stream", "dp", None),
            P("stream", "dp", None),
            P(None, "dp"),
            P(None, "dp"),
            P(None, "dp"),
            P(None, "dp"),
            P(None, "dp", None),
            P(None, "dp", None),
            P("dp", None),
            P(None, "dp", None),
            P("stream", "dp", None),
            P("stream", "dp", None),
        ),
        check_vma=False,
    )
```

profile of v0, /device:TPU:0, one launch (start us, length us, event | category | flops | bytes accessed | tf_op | source)
XLA Modules:
  0.0 1814.9 jit_solution(10446482797198245968)
XLA Ops:
  18.2 42.4 %all-gather = bf16[16,48,4]{1,2,0:T(4,128)(2,1)S(1)} all-gather(bf16[1,48,4]{1,2,0:T(4,128)(2,1)S(1)} %convert_bitcast_fusion), channel_id=1, replica_groups=mesh['stream'=2,'dp'=16] {'dp'}, dimensions={0}, use_global_device_ids=true | all-gather | bytes 6528 | tf_op jit(solution)/shard_map/all_gather | solution.py:193
  63.8 21.6 %all-gather.8.cloned.1.call-done = bf16[3,768,768]{2,1,0:T(8,128)(2,1)} async-done(((bf16[3,48,768]{2,1,0:T(8,128)(2,1)}), bf16[3,768,768]{2,1,0:T(8,128)(2,1)}) %all-gather.8.cloned.1.call-update) | async-done | bytes 3538960 | tf_op jit(solution)/shard_map/all_gather | solution.py:187
  94.6 3.0 convolution_convert_fusion.7
  100.1 21.2 %conditional.6 = (f32[1,12,512]{2,1,0:T(8,128)S(1)}, bf16[512,768]{0,1:T(8,128)(2,1)S(1)}) conditional(s32[]{:T(128)} %convert_element_type.232, (pred[512,1024]{0,1:T(8,128)(4,1)}, bf16[512,768]{1,0:T(8,128)(2,1)}, bf16[1024,768]{1,0:T(8,128)(2,1)}, bf16[1024,768]{1,0:T(8,128)(2,1)}) %tuple.62, (pred[512,512]{0,1:T(8,128)(4,1)S(1)}, ...), branch_computations={%region_4.7_spmd, %region_7.10_spmd} | conditional | flops 1686497280 | bytes 96927784 | solution.py:219
  103.8 3.4 fusion.6
  112.9 8.4 fusion.9
  121.4 28.2 %all-gather.10.cloned.1.call-done = bf16[2,768,768]{2,1,0:T(8,128)(2,1)} async-done(((bf16[2,48,768]{2,1,0:T(8,128)(2,1)}), bf16[2,768,768]{2,1,0:T(8,128)(2,1)}) %all-gather.10.cloned.1.call-update) | async-done | bytes 2359312 | tf_op jit(solution)/shard_map/all_gather | solution.py:188
  149.6 3.0 multiply_reduce_fusion.10
  152.6 55.3 %all-gather.14.cloned.1.call-done = bf16[768,768]{1,0:T(8,128)(2,1)} async-done(((bf16[48,768]{1,0:T(8,128)(2,1)}), bf16[768,768]{1,0:T(8,128)(2,1)}) %all-gather.14.cloned.1.call-update) | async-done | bytes 1179664 | tf_op jit(solution)/shard_map/all_gather | solution.py:189
  207.9 79.1 %all-gather.12.cloned.1.call-done = bf16[2,1408,768]{2,1,0:T(8,128)(2,1)} async-done(((bf16[2,88,768]{2,1,0:T(8,128)(2,1)}), bf16[2,1408,768]{2,1,0:T(8,128)(2,1)}) %all-gather.12.cloned.1.call-update) | async-done | bytes 4325392 | tf_op jit(solution)/shard_map/all_gather | solution.py:190
  287.0 89.5 %conditional.7 = (f32[512,768]{1,0:T(8,128)}, f32[16,12,32]{2,1,0:T(8,128)S(1)}, bf16[2,16,257,768]{3,2,1,0:T(8,128)(2,1)}, bf16[512,768]{1,0:T(8,128)(2,1)}, bf...) conditional(s32[]{:T(128)} %convert_element_type.232, () %tuple.64, (bf16[2,1408,768]{2,1,0:T(8,128)(2,1)}, ...), branch_computations={%region_10.11_spmd, %region_11.15_spmd} | conditional | flops 19421405184 | bytes 209458352 | solution.py:245
  292.4 24.4 %fusion.31 = bf16[2,16,257,768]{3,2,1,0:T(8,128)(2,1)S(1)} fusion(bf16[16,257,1408]{2,0,1:T(8,128)(2,1)} %get-tuple-element.401, bf16[2,1408,768]{2,1,0:T(8,128)(2,1)} %get-tuple-element.106), kind=kOutput, calls=%fused_computation.50 | convolution fusion | flops 17792262144 | bytes 28536832 | tf_op jit(solution)/shard_map/cond/branch_1_fun/inv,kvd->kind/dot_general | solution.py:135
  316.9 5.4 fusion.152
  322.3 3.2 copy-done
  325.5 11.3 copy.247
  336.7 6.9 multiply_reduce_fusion.2
  347.2 11.2 copy.246
  358.5 8.5 fusion.40
  369.0 3.9 convert_element_type.174
  372.9 3.4 fusion.41
  379.4 19.7 %multiply_convert_fusion.9 = (bf16[512,3072]{1,0:T(8,128)(2,1)}, f32[512,3072]{1,0:T(8,128)}, f32[512,3072]{1,0:T(8,128)}) fusion(bf16[1,3072,768]{2,1,0:T(8,128)(2,1)} %all-gather.16.cloned.1.call-done, f32[512,768]{1,0:T(8,128)} %get-tuple-element.478, f32[768]{0:T(1024)S(1)} %copy-done.58, f32[512]{0:T(512)S(1)} %fusion.131), kind=kOutput, calls=%fused_computation.113 | convolution fusion | flops 2519334912 | bytes 22025216 | tf_op jit(solution)/shard_map/dot_general | solution.py:44
  399.1 52.7 %all-gather.18.cloned.1.call-done = bf16[1,3072,768]{2,1,0:T(8,128)(2,1)} async-done(((bf16[1,192,768]{2,1,0:T(8,128)(2,1)}), bf16[1,3072,768]{2,1,0:T(8,128)(2,1)}) %all-gather.18.cloned.1.call-update) | async-done | bytes 4718608 | tf_op jit(solution)/shard_map/all_gather | solution.py:192
  451.7 8.3 add_convert_fusion
  464.9 4.7 multiply_reduce_fusion.9
  470.0 176.3 %conditional.16 = (f32[512,768]{1,0:T(8,128)}, f32[768,768]{0,1:T(8,128)}, f32[2,1408,768]{1,2,0:T(8,128)}, f32[1,768]{1,0:T(1,128)S(1)}, f32[1,768,768]{2,1,0:T(8,128)}) conditional(s32[]{:T(128)} %convert_element_type.232, () %tuple.66, (bf16[512,768]{1,0:T(8,128)(2,1)}, bf16[2,16,257,768]{3,2,1,0:T(8,128)(2,1)}, f32[16,12,32]{2,1,0:T(8,128)S(1)}, ...), branch_computations={%region_17.18_spmd, %region_18.23_spmd} | conditional | flops 21254242304 | bytes 265626816 | solution.py:295
  470.3 21.1 %copy.270 = bf16[2,16,257,768]{2,3,1,0:T(8,128)(2,1)} copy(bf16[2,16,257,768]{3,2,1,0:T(8,128)(2,1)} %get-tuple-element.407) | data formatting | bytes 25264128 | tf_op jit(solution)/shard_map
  491.4 14.6 fusion.153
  506.0 3.8 reshape.498
  509.7 9.9 fusion.67
  521.4 3.8 reshape.499
  525.2 14.7 multiply_reduce_fusion.4
  539.9 8.2 multiply_convert_fusion.7
  548.1 8.5 fusion.60
  558.7 3.9 convert_element_type.180
  566.7 9.3 multiply_convert_fusion.6
  576.1 11.5 copy.255
  587.6 10.8 convolution_convert_fusion.2
  598.5 11.4 copy.256
  609.9 30.7 %fusion.52 = f32[2,1408,768]{1,2,0:T(8,128)} fusion(bf16[16,257,1408]{2,0,1:T(8,128)(2,1)} %get-tuple-element.415, bf16[1,16,257,768]{3,2,1,0:T(8,128)(2,1)} %copy.256, bf16[1,16,257,768]{3,2,1,0:T(8,128)(2,1)} %copy.255), kind=kOutput, calls=%fused_computation.82 | convolution fusion | flops 17792262144 | bytes 32862208 | tf_op jit(solution)/shard_map/cond/branch_1_fun/inv,kind->kvd/dot_general | solution.py:142
  642.9 3.3 convolution_bitcast_fusion
  646.4 3.0 copy.281
  653.6 4.2 pad_maximum_fusion.1
  657.8 3.1 convolution_convert_fusion.4
  660.9 51.4 %conditional.17 = (bf16[512,768]{0,1:T(8,128)(2,1)}, bf16[512,768]{0,1:T(8,128)(2,1)}, bf16[512,768]{0,1:T(8,128)(2,1)}, bf16[512,768]{0,1:T(8,128)(2,1)}, bf16[512,768]{0,1:T(8,128)(2,1)}) conditional(s32[]{:T(128)} %convert_element_type.232, (pred[512,1024]{0,1:T(8,128)(4,1)}, bf16[512,768]{1,0:T(8,128)(2,1)}, bf16[1024,768]{1,0:T(8,128)(2,1)}, ...), branch_computations={%region_23.25_spmd, %region_25.27_spmd} | conditional | flops 4123256832 | bytes 274587776
  670.9 6.4 fusion.160
  679.7 13.6 multiply_reduce_fusion.1
  693.4 7.1 multiply_convert_fusion.2
  700.5 2.9 multiply_convert_fusion.3
  705.4 5.0 fusion.24
  733.1 3.4 pad_maximum_fusion
  736.5 9.4 copy.282
  747.7 28.7 %reduce-scatter.14.cloned.1.call-done = f32[48,768]{1,0:T(8,128)} async-done(((f32[768,768]{1,0:T(8,128)}), f32[48,768]{1,0:T(8,128)}) %reduce-scatter.14.cloned.1.call-update) | async-done | bytes 147472 | tf_op jit(solution)/shard_map/reduce_scatter | solution.py:387
  777.9 141.4 %reduce-scatter.12.cloned.1.call-done = f32[2,48,768]{2,1,0:T(8,128)} async-done(((f32[2,768,768]{2,1,0:T(8,128)}), f32[2,48,768]{2,1,0:T(8,128)}) %reduce-scatter.12.cloned.1.call-update) | async-done | bytes 294928 | tf_op jit(solution)/shard_map/reduce_scatter | solution.py:386
  921.0 154.0 %reduce-scatter.10.cloned.1.call-done = f32[3,48,768]{2,1,0:T(8,128)} async-done(((f32[3,768,768]{2,1,0:T(8,128)}), f32[3,48,768]{2,1,0:T(8,128)}) %reduce-scatter.10.cloned.1.call-update) | async-done | bytes 442384 | tf_op jit(solution)/shard_map/reduce_scatter | solution.py:385
  1076.7 168.0 %reduce-scatter.16.cloned.1.call-done = f32[2,88,768]{2,1,0:T(8,128)} async-done(((f32[2,1408,768]{2,1,0:T(8,128)}), f32[2,88,768]{2,1,0:T(8,128)}) %reduce-scatter.16.cloned.1.call-update) | async-done | bytes 540688 | tf_op jit(solution)/shard_map/reduce_scatter | solution.py:388
  1246.8 8.3 convolution_bitcast_fusion.3
  1256.5 8.2 convolution_bitcast_fusion.2
  1270.0 100.8 %reduce-scatter.22.cloned.1.call-done = f32[48,4]{1,0:T(8,128)} async-done(((f32[768,4]{1,0:T(8,128)}), f32[48,4]{1,0:T(8,128)}) %reduce-scatter.22.cloned.1.call-update) | async-done | bytes 784
  1374.7 18.0 all-reduce.4.cloned.1.call-done
  1402.4 169.3 %reduce-scatter.18.cloned.1.call-done = f32[1,192,768]{2,1,0:T(8,128)} async-done(((f32[1,3072,768]{2,1,0:T(8,128)}), f32[1,192,768]{2,1,0:T(8,128)}) %reduce-scatter.18.cloned.1.call-update) | async-done | bytes 589840 | tf_op jit(solution)/shard_map/reduce_scatter | solution.py:389
  1574.2 172.9 %reduce-scatter.20.cloned.1.call-done = f32[1,192,768]{2,1,0:T(8,128)} async-done(((f32[1,3072,768]{2,1,0:T(8,128)}), f32[1,192,768]{2,1,0:T(8,128)}) %reduce-scatter.20.cloned.1.call-update) | async-done | bytes 589840 | tf_op jit(solution)/shard_map/reduce_scatter | solution.py:390
  1749.5 3.0 fusion.92
  1752.5 39.2 %all-reduce = (f32[]{:T(128)}, f32[2,4]{1,0:T(2,128)S(1)}) all-reduce(f32[]{:T(128)S(6)} %add.292, f32[2,4]{1,0:T(2,128)S(1)} %broadcast_select_fusion.2), channel_id=1, replica_groups=mesh['stream'=2,'dp'=16] {'stream','dp'}, use_global_device_ids=true, to_apply=%region_49.50 | all-reduce | flops 9 | bytes 72 | tf_op jit(solution)/shard_map/psum | solution.py:423
  1793.6 3.1 fusion.138
  (297 shorter events, 137.6 us)
Async XLA Ops:
  7.2 11.0 copy-start.63
  7.2 53.5 %copy-start.70 = (s32[1,32]{1,0:T(1,128)S(1)}, s32[1,32]{1,0:T(1,128)}, u32[]{:S(2)}) copy-start(s32[1,32]{1,0:T(1,128)} %param.36) | copy-start | bytes 388
  7.2 54.4 %copy-start.71 = (s32[1,32]{1,0:T(1,128)S(1)}, s32[1,32]{1,0:T(1,128)}, u32[]{:S(2)}) copy-start(s32[1,32]{1,0:T(1,128)} %param.37) | copy-start | bytes 388
  7.2 54.5 %copy-start.4 = (f32[1,512,768]{2,1,0:T(8,128)S(1)}, f32[1,512,768]{2,1,0:T(8,128)}, u32[]{:S(2)}) copy-start(f32[1,512,768]{2,1,0:T(8,128)} %param.34) | copy-start | bytes 4718596
  7.2 78.2 %all-gather.8.cloned.1.call-start = ((), (), s32[]{:S(2)}) async-start(), calls=%async_computation.7 | async-start | bytes 3760128 | tf_op jit(solution)/shard_map/all_gather | solution.py:187
  9.2 140.4 %all-gather.10.cloned.1.call-start = ((), (), s32[]{:S(2)}) async-start(), calls=%async_computation.8 | async-start | bytes 2506752 | tf_op jit(solution)/shard_map/all_gather | solution.py:188
  10.9 197.1 %all-gather.14.cloned.1.call-start = ((), (), s32[]{:S(2)}) async-start(), calls=%async_computation.10 | async-start | bytes 1253376 | tf_op jit(solution)/shard_map/all_gather | solution.py:189
  12.5 274.5 %all-gather.12.cloned.1.call-start = ((), (), s32[]{:S(2)}) async-start(), calls=%async_computation.9 | async-start | bytes 4595712 | tf_op jit(solution)/shard_map/all_gather | solution.py:190
  14.4 365.0 %all-gather.16.cloned.1.call-start = ((), (), s32[]{:S(2)}) async-start(), calls=%async_computation.11 | async-start | bytes 5013504 | tf_op jit(solution)/shard_map/all_gather | solution.py:191
  16.2 435.5 %all-gather.18.cloned.1.call-start = ((), (), s32[]{:S(2)}) async-start(), calls=%async_computation.12 | async-start | bytes 5013504 | tf_op jit(solution)/shard_map/all_gather | solution.py:192
  18.1 758.3 %reduce-scatter.14.cloned.1.call-start = ((), (), s32[]{:S(2)}) async-start(), calls=%async_computation.15 | async-start | bytes 2506752 | tf_op jit(solution)/shard_map/reduce_scatter | solution.py:387
  63.5 36.5 %copy-start.15 = (pred[512,512]{0,1:T(8,128)(4,1)}, pred[512,512]{0,1:T(8,128)(4,1)S(1)}, u32[]{:S(2)}) copy-start(pred[512,512]{0,1:T(8,128)(4,1)S(1)} %get-tuple-element.512) | copy-start | bytes 786436
  63.8 23.7 %copy-start.43 = (bf16[512,768]{1,0:T(8,128)(2,1)}, bf16[512,768]{1,0:T(8,128)(2,1)S(1)}, u32[]{:S(2)}) copy-start(bf16[512,768]{1,0:T(8,128)(2,1)S(1)} %fusion.102) | copy-start | bytes 2359300
  87.5 12.6 copy-start.10
  87.5 10.1 collective-permute-start
  91.2 8.9 copy-start.12
  91.2 7.6 collective-permute-start.1
  121.3 28.3 %copy-start.27 = (bf16[512,768]{0,1:T(8,128)(2,1)}, bf16[512,768]{0,1:T(8,128)(2,1)S(1)}, u32[]{:S(2)}) copy-start(bf16[512,768]{0,1:T(8,128)(2,1)S(1)} %get-tuple-element.203) | copy-start | bytes 2359300
  121.4 165.7 %copy-start.41 = (f32[1,12,512]{2,1,0:T(8,128)}, f32[1,12,512]{2,1,0:T(8,128)S(1)}, u32[]{:S(2)}) copy-start(f32[1,12,512]{2,1,0:T(8,128)S(1)} %get-tuple-element.193) | copy-start | bytes 73732
  287.4 29.4 %copy-start.31 = (bf16[512,768]{1,0:T(8,128)(2,1)}, bf16[512,768]{1,0:T(8,128)(2,1)S(1)}, u32[]{:S(2)}) copy-start(bf16[512,768]{1,0:T(8,128)(2,1)S(1)} %multiply_convert_fusion.5) | copy-start | bytes 2359300 | tf_op jit(solution)/shard_map/cond
  289.8 27.1 %copy-start.14 = (bf16[512,768]{1,0:T(8,128)(2,1)}, bf16[512,768]{1,0:T(8,128)(2,1)S(1)}, u32[]{:S(2)}) copy-start(bf16[512,768]{1,0:T(8,128)(2,1)S(1)} %convolution_convert_fusion.1) | copy-start | bytes 2359300 | tf_op jit(solution)/shard_map/cond
  316.9 8.6 copy-start
  379.4 90.3 %copy-start.61 = (f32[512]{0:T(512)}, f32[512]{0:T(512)S(1)}, u32[]{:S(2)}) copy-start(f32[512]{0:T(512)S(1)} %fusion.131) | copy-start | bytes 6148
  379.4 72.3 %copy-start.17 = (f32[1,512,768]{2,1,0:T(8,128)S(1)}, f32[1,512,768]{2,1,0:T(8,128)}, u32[]{:S(2)}) copy-start(f32[1,512,768]{2,1,0:T(8,128)} %param.38) | copy-start | bytes 4718596
  451.7 8.3 copy-start.72
  509.7 9.9 copy-start.49
  525.2 14.7 slice-start
  525.2 14.7 slice-start.1
  525.2 14.7 slice-start.2
  609.9 30.7 %copy-start.22 = (bf16[512,768]{1,0:T(8,128)(2,1)S(1)}, bf16[512,768]{1,0:T(8,128)(2,1)}, u32[]{:S(2)}) copy-start(bf16[512,768]{1,0:T(8,128)(2,1)} %convert_element_type.180) | copy-start | bytes 2359300 | tf_op jit(solution)/shard_map/cond
  609.9 30.7 %copy-start.32 = (bf16[512,768]{1,0:T(8,128)(2,1)S(1)}, bf16[512,768]{1,0:T(8,128)(2,1)}, u32[]{:S(2)}) copy-start(bf16[512,768]{1,0:T(8,128)(2,1)} %get-tuple-element.120) | copy-start | bytes 2359300 | tf_op jit(solution)/shard_map/cond
  649.4 269.9 %reduce-scatter.12.cloned.1.call-start = ((), (), s32[]{:S(2)}) async-start(), calls=%async_computation.14 | async-start | bytes 5013504 | tf_op jit(solution)/shard_map/reduce_scatter | solution.py:386
  651.1 6.7 copy-start.6
  657.8 417.2 %reduce-scatter.10.cloned.1.call-start = ((), (), s32[]{:S(2)}) async-start(), calls=%async_computation.13 | async-start | bytes 7520256 | tf_op jit(solution)/shard_map/reduce_scatter | solution.py:385
  670.6 6.7 copy-start.28
  670.9 7.6 copy-start.13
  679.7 13.6 slice-start.3
  679.7 13.6 slice-start.4
  679.7 13.6 slice-start.5
  693.4 7.1 copy-start.29
  712.3 7.9 copy-start.50
  712.3 9.9 collective-permute-start.2
  713.8 9.2 collective-permute-start.3
  736.5 508.2 %reduce-scatter.16.cloned.1.call-start = ((), (), s32[]{:S(2)}) async-start(), calls=%async_computation.16 | async-start | bytes 9191424 | tf_op jit(solution)/shard_map/reduce_scatter | solution.py:388
  745.9 500.8 %copy-start.21 = (f32[512,768]{1,0:T(8,128)S(1)}, f32[512,768]{1,0:T(8,128)}, u32[]{:S(2)}) copy-start(f32[512,768]{1,0:T(8,128)} %get-tuple-element.478) | copy-start | bytes 4718596
  745.9 500.8 %copy-start.59 = (f32[768]{0:T(1024)S(1)}, f32[768]{0:T(1024)}, u32[]{:S(2)}) copy-start(f32[768]{0:T(1024)} %dynamic-slice_reduce_fusion) | copy-start | bytes 9220
  746.0 500.8 %copy-start.62 = (f32[512]{0:T(512)S(1)}, f32[512]{0:T(512)}, u32[]{:S(2)}) copy-start(f32[512]{0:T(512)} %copy-done.61) | copy-start | bytes 6148
  746.0 624.8 %reduce-scatter.22.cloned.1.call-start = ((), (), s32[]{:S(2)}) async-start(), calls=%async_computation.19 | async-start | bytes 417792
  747.6 645.0 %all-reduce.4.cloned.1.call-start = ((), (), s32[]{:S(2)}) async-start(), calls=%async_computation.20 | async-start | bytes 1425408 | tf_op jit(solution)/shard_map/psum | solution.py:394
  1246.5 325.2 %reduce-scatter.18.cloned.1.call-start = ((), (), s32[]{:S(2)}) async-start(), calls=%async_computation.17 | async-start | bytes 10027008 | tf_op jit(solution)/shard_map/reduce_scatter | solution.py:389
  1255.1 491.9 %reduce-scatter.20.cloned.1.call-start = ((), (), s32[]{:S(2)}) async-start(), calls=%async_computation.18 | async-start | bytes 10027008 | tf_op jit(solution)/shard_map/reduce_scatter | solution.py:390
  1264.8 484.8 %copy-start.7 = (f32[512,768]{1,0:T(8,128)S(1)}, f32[512,768]{1,0:T(8,128)}, u32[]{:S(2)}) copy-start(f32[512,768]{1,0:T(8,128)} %copy-done.6) | copy-start | bytes 4718596
  1264.8 528.2 %copy-start.64 = (f32[4,48]{1,0:T(4,128)S(1)}, f32[4,48]{1,0:T(4,128)}, u32[]{:S(2)}) copy-start(f32[4,48]{1,0:T(4,128)} %param.45) | copy-start | bytes 2308
  1264.8 528.2 %copy-start.68 = (f32[4,48]{1,0:T(4,128)S(1)}, f32[4,48]{1,0:T(4,128)}, u32[]{:S(2)}) copy-start(f32[4,48]{1,0:T(4,128)} %param.58) | copy-start | bytes 2308
  1264.8 528.2 %copy-start.69 = (f32[4,48]{1,0:T(4,128)S(1)}, f32[4,48]{1,0:T(4,128)}, u32[]{:S(2)}) copy-start(f32[4,48]{1,0:T(4,128)} %param.59) | copy-start | bytes 2308
  1749.5 47.2 %copy-start.51 = (bf16[48,768]{1,0:T(8,128)(2,1)S(1)}, bf16[48,768]{1,0:T(8,128)(2,1)}, u32[]{:S(2)}) copy-start(bf16[48,768]{1,0:T(8,128)(2,1)} %get-tuple-element.445) | copy-start | bytes 221188
  1749.5 49.1 %copy-start.39 = (f32[2,48,768]{2,1,0:T(8,128)S(1)}, f32[2,48,768]{2,1,0:T(8,128)}, u32[]{:S(2)}) copy-start(f32[2,48,768]{2,1,0:T(8,128)} %param.40) | copy-start | bytes 884740
  1752.5 48.6 %copy-start.38 = (f32[3,48,768]{2,1,0:T(8,128)S(1)}, f32[3,48,768]{2,1,0:T(8,128)}, u32[]{:S(2)}) copy-start(f32[3,48,768]{2,1,0:T(8,128)} %param.39) | copy-start | bytes 1327108
  1752.5 48.6 %copy-start.40 = (bf16[3,48,768]{2,1,0:T(8,128)(2,1)S(1)}, bf16[3,48,768]{2,1,0:T(8,128)(2,1)}, u32[]{:S(2)}) copy-start(bf16[3,48,768]{2,1,0:T(8,128)(2,1)} %get-tuple-element.443) | copy-start | bytes 663556
  1793.6 10.0 copy-start.34
  1793.6 10.0 copy-start.37
  1793.6 10.0 copy-start.45
  1793.6 10.0 copy-start.46
  1798.7 6.6 copy-start.36
  (30 other events, 106.7 us)
Sparse Core Ops, SparseCore 0:
  11.3 74.0 all-gather.7
  88.7 60.8 all-gather.9
  153.0 54.9 all-gather.13
  211.1 75.9 all-gather.11
  290.2 79.0 all-gather.15
  372.6 79.0 all-gather.17
  649.5 126.7 reduce-scatter.13
  782.4 136.8 reduce-scatter.11
  924.7 150.2 reduce-scatter.9
  1080.5 164.1 reduce-scatter.15
  1250.6 120.1 reduce-scatter.21
  1374.4 18.1 all-reduce.3
  1399.3 172.3 reduce-scatter.17
  1577.2 169.7 reduce-scatter.19
where the time goes:
time: 1830 us; the launch traced here: 1810 us
  waiting for transfers between devices  1190 us (65%)
  matrix products  266 us (15%)
  local copies, waits for them, and re-layouts  146 us (8%)
  other arithmetic  90.7 us (5%)
  blocking collectives  84 us (5%)
  between operations  21.6 us (1%)
    reduce_scatter x1, waiting for transfers between devices, body(): lax.psum_scatter(grad_reduce[None], 'dp', scatter_dimension=1, tiled=True)  173 us
    reduce_scatter x1, waiting for transfers between devices, body(): lax.psum_scatter(grad_expand[None], 'dp', scatter_dimension=1, tiled=True)  169 us
    reduce_scatter x1, waiting for transfers between devices, body(): lax.psum_scatter(shared_grads[3], 'dp', scatter_dimension=1, tiled=True)  168 us
    reduce_scatter x1, waiting for transfers between devices, body(): lax.psum_scatter(shared_grads[0], 'dp', scatter_dimension=1, tiled=True)  154 us
    reduce_scatter x1, waiting for transfers between devices, body(): lax.psum_scatter(shared_grads[1], 'dp', scatter_dimension=1, tiled=True)  141 us
    unnamed x15, waiting for transfers between devices  101 us
    all_gather x1, waiting for transfers between devices, body(): lax.all_gather(to_half(cross_vision), 'dp', axis=1, tiled=True)  79.1 us
    all_gather x1, waiting for transfers between devices, body(): lax.all_gather(to_half(cross_query), 'dp', axis=0, tiled=True)  55.3 us
  transfers between devices with their start and end apart: 18, of which 13 were waited for; matrix products, arithmetic and copies ran while one was open for 15% of the time, Pallas kernels for 0%

commit v1 on v0

--- a/solution.py
+++ b/solution.py
@@ -1,6 +1,8 @@
 import jax
 import jax.numpy as jnp
 from jax import lax
+from jax.experimental import pallas as pl
+from jax.experimental.pallas import tpu as pltpu
 from jax.sharding import PartitionSpec as P
 
 HEADS = 12
@@ -152,6 +154,440 @@
         corrected_mean / (jnp.sqrt(corrected_square) + adam_floor) + decay * weight
     )
     return (fresh, mean_new, square_new)
+
+
+MESH = pl.DeviceIdType.MESH
+VMEM_LIMIT = 60 * 2**20
+
+
+def coordinates():
+    c = lax.axis_index("stream")
+    d = lax.axis_index("dp")
+    return c, d // 4, (d // 2) % 2, d % 2
+
+
+def device(c, z, y, x):
+    return (c, z * 4 + y * 2 + x)
+
+
+def meet(c, z, y, x):
+    barrier = pltpu.get_barrier_semaphore()
+    others = [device(1 - c, z, y, x), device(c, z, 1 - y, x), device(c, z, y, 1 - x)]
+    others += [device(c, (z + k) % 4, y, x) for k in (1, 2, 3)]
+    for other in others:
+        pl.semaphore_signal(barrier, inc=1, device_id=other, device_id_type=MESH)
+    pl.semaphore_wait(barrier, len(others))
+
+
+ORDERS = {
+    ("late", 0): ("z", "y", "x"),
+    ("late", 1): ("z", "x", "y"),
+    ("early", 0): ("x", "z", "y"),
+    ("early", 1): ("y", "z", "x"),
+}
+
+
+def gather_kernel(
+    first, vision, expand, reduce, gains,
+    all_first, all_vision, all_expand, all_reduce, all_gains,
+    send_sem, recv_sem, local_sem,
+):
+    c, z, y, x = coordinates()
+    half = expand.shape[0] // 2
+    low, high = pl.ds(0, half), pl.ds(half, half)
+    chunks = [
+        (gains, lambda *at: all_gains.at[at], "late", False),
+        (first.at[0], lambda *at: all_first.at[(c, 0) + at], "early", True),
+        (first.at[1], lambda *at: all_first.at[(c, 1) + at], "early", True),
+        (first.at[2], lambda *at: all_first.at[(c, 2) + at], "early", True),
+        (vision, lambda *at: all_vision.at[(c,) + at], "early", True),
+        (expand.at[low], lambda *at: all_expand.at[at + (low,)], "late", False),
+        (expand.at[high], lambda *at: all_expand.at[at + (high,)], "late", False),
+        (reduce.at[low], lambda *at: all_reduce.at[at + (low,)], "late", False),
+        (reduce.at[high], lambda *at: all_reduce.at[at + (high,)], "late", False),
+    ]
+    own = {"z": z, "y": y, "x": x}
+
+    def remote(source, target, index, where):
+        return pltpu.make_async_remote_copy(
+            src_ref=source, dst_ref=target, send_sem=send_sem.at[index],
+            recv_sem=recv_sem.at[index], device_id=where, device_id_type=MESH,
+        )
+
+    def sends(number, stage, core):
+        source, target, kind, _ = chunks[number]
+        order = ORDERS[kind, core]
+        done, axis = order[:stage], order[stage]
+        at = tuple(slice(None) if a in done else own[a] for a in "zyx")
+        block = target(*at)
+        here = source if stage == 0 else block
+        base = (number * 3 + stage) * 3
+        if axis == "z":
+            return [
+                remote(here, block, base + k - 1, device(c, (z + k) % 4, y, x)) for k in (1, 2, 3)
+            ]
+        where = device(c, z, 1 - y, x) if axis == "y" else device(c, z, y, 1 - x)
+        return [remote(here, block, base, where)]
+
+    def place(number):
+        source, target, _, _ = chunks[number]
+        return pltpu.make_async_copy(source, target(z, y, x), local_sem.at[number])
+
+    def across(number):
+        _, target, _, _ = chunks[number]
+        block = target(slice(None), slice(None), slice(None))
+        return remote(block, block, len(chunks) * 9 + number, device(1 - c, z, y, x))
+
+    def run(core):
+        count = len(chunks)
+        for tick in range(count + 3):
+            for stage in (3, 2, 1, 0):
+                number = tick - stage
+                if not 0 <= number < count:
+                    continue
+                if stage > 0:
+                    for copy in sends(number, stage - 1, core):
+                        copy.wait_recv()
+                if stage == 1:
+                    place(number).wait()
+                if stage < 3:
+                    for copy in sends(number, stage, core):
+                        copy.start()
+                    if stage == 0:
+                        place(number).start()
+                elif chunks[number][3]:
+                    across(number).start()
+        for number in range(count):
+            for stage in range(3):
+                for copy in sends(number, stage, core):
+                    copy.wait_send()
+            if chunks[number][3]:
+                across(number).wait()
+
+    meet(c, z, y, x)
+
+    @pl.when(c == 0)
+    def _():
+        run(0)
+
+    @pl.when(c == 1)
+    def _():
+        run(1)
+
+
+def gather_all(first, vision, expand, reduce, gains):
+    half = jnp.bfloat16
+    width = first.shape[-1]
+    shapes = [
+        (2, 3, 4, 2, 2) + first.shape[1:],
+        (2, 4, 2, 2) + vision.shape,
+        (4, 2, 2) + expand.shape,
+        (4, 2, 2) + reduce.shape,
+        (4, 2, 2) + gains.shape,
+    ]
+    count = 9
+    anywhere = pl.BlockSpec(memory_space=pl.ANY)
+    return pl.pallas_call(
+        gather_kernel,
+        out_shape=[jax.ShapeDtypeStruct(shape, half) for shape in shapes],
+        in_specs=[anywhere] * 5,
+        out_specs=[anywhere] * 5,
+        scratch_shapes=[
+            pltpu.SemaphoreType.DMA((count * 10,)),
+            pltpu.SemaphoreType.DMA((count * 10,)),
+            pltpu.SemaphoreType.DMA((count,)),
+        ],
+        compiler_params=pltpu.CompilerParams(
+            collective_id=0, has_side_effects=True, vmem_limit_bytes=VMEM_LIMIT
+        ),
+        name="gather_weights",
+    )(first, vision, expand, reduce, gains)
+
+
+def wide(block):
+    return block.astype(jnp.float32)
+
+
+def scatter_kernel(
+    part_first, part_vision, part_expand, part_reduce, part_gains, part_stats,
+    sum_first, sum_vision, sum_expand, sum_reduce, sum_gains, totals,
+    held_first, held_vision, held_expand, held_reduce,
+    pair_first, pair_vision,
+    got_a0, got_a1, got_a2, got_b0, got_b1, got_b2, got_c0, got_c1, got_c2,
+    gains_now, gains_got, gains_z, stats_now, stats_got, stats_z,
+    send_sem, recv_sem, local_sem,
+):
+    c, z, y, x = coordinates()
+    half = sum_expand.shape[0] // 2
+    low, high = pl.ds(0, half), pl.ds(half, half)
+    own = {"z": z, "y": y, "x": x}
+    chunks = []
+    for number, (held, total) in enumerate([(held_expand, sum_expand), (held_reduce, sum_reduce)]):
+        for part, rows in enumerate((low, high)):
+            slot = number * 2 + part
+            chunks.append((
+                lambda at, held=held, rows=rows: at + (rows,), held,
+                (got_a0.at[slot], got_a1.at[slot], got_a2.at[slot]), "late",
+                (total, (rows,)), None,
+            ))
+    for j in range(3):
+        chunks.append((
+            lambda at, j=j: (j,) + at, held_first,
+            (got_b0.at[j], got_b1.at[j], got_b2.at[j]), "early",
+            (sum_first, (c, j)), (pair_first, j),
+        ))
+    chunks.append((
+        lambda at: at, held_vision, (got_c0, got_c1, got_c2), "early",
+        (sum_vision, (c,)), (pair_vision, None),
+    ))
+    count = len(chunks)
+
+    def remote(source, target, index, where):
+        return pltpu.make_async_remote_copy(
+            src_ref=source, dst_ref=target, send_sem=send_sem.at[index],
+            recv_sem=recv_sem.at[index], device_id=where, device_id_type=MESH,
+        )
+
+    def load(number):
+        result = [
+            (part_expand.at[:, :, :, low], held_expand.at[:, :, :, low]),
+            (part_expand.at[:, :, :, high], held_expand.at[:, :, :, high]),
+            (part_reduce.at[:, :, :, low], held_reduce.at[:, :, :, low]),
+            (part_reduce.at[:, :, :, high], held_reduce.at[:, :, :, high]),
+        ]
+        result += [(part_first.at[c, j], held_first.at[j]) for j in range(3)]
+        result += [(part_vision.at[c], held_vision)]
+        source, target = result[number]
+        return pltpu.make_async_copy(source, target, local_sem.at[number])
+
+    def pair_copy(number):
+        buffer, j = chunks[number][5]
+        if j is None:
+            source, target = part_vision.at[1 - c], buffer
+        else:
+            source, target = part_first.at[1 - c, j], buffer.at[j]
+        return remote(source, target, count * 9 + number, device(1 - c, z, y, x))
+
+    def sends(number, stage, core):
+        address, held, got, kind, _, _ = chunks[number]
+        order = ORDERS[kind, core][::-1]
+        done, axis = order[:stage], order[stage]
+        base = (number * 3 + stage) * 3
+
+        def block(there):
+            at = tuple(
+                there if a == axis else own[a] if a in done else slice(None) for a in "zyx"
+            )
+            return held.at[address(at)]
+
+        if axis == "z":
+            return [
+                remote(
+                    block((z + k) % 4), got[stage].at[k - 1], base + k - 1,
+                    device(c, (z + k) % 4, y, x),
+                )
+                for k in (1, 2, 3)
+            ]
+        where = device(c, z, 1 - y, x) if axis == "y" else device(c, z, y, 1 - x)
+        return [remote(block(1 - own[axis]), got[stage], base, where)]
+
+    def absorb(number, stage, core):
+        address, held, got, kind, total, _ = chunks[number]
+        order = ORDERS[kind, core][::-1]
+        done, axis = order[: stage + 1], order[stage]
+        free = [a for a in "zyx" if a not in done]
+        sizes = [4 if a == "z" else 2 for a in free]
+        steps = 1
+        for size in sizes:
+            steps *= size
+
+        def step(i, carry):
+            index = {}
+            for a, size in reversed(list(zip(free, sizes))):
+                index[a] = i % size
+                i = i // size
+            at = address(tuple(index[a] if a in index else own[a] for a in "zyx"))
+            inner = tuple(index[a] for a in free)
+            value = wide(held[at])
+            if axis == "z":
+                for k in range(3):
+                    value = value + wide(got[stage][(k,) + inner])
+            else:
+                value = value + wide(got[stage][inner] if inner else got[stage][...])
+            if stage == 2:
+                target, where = total
+                target[where] = value
+            else:
+                held[at] = value.astype(jnp.bfloat16)
+            return carry
+
+        if steps == 1:
+            step(0, 0)
+        else:
+            lax.fori_loop(0, steps, step, 0)
+
+    def add_pair(number):
+        address, held, _, _, _, (buffer, j) = chunks[number]
+
+        def step(i, carry):
+            at = (i // 4, (i // 2) % 2, i % 2)
+            here = address(at)
+            value = wide(held[here]) + wide(buffer[at if j is None else (j,) + at])
+            held[here] = value.astype(jnp.bfloat16)
+            return carry
+
+        lax.fori_loop(0, 16, step, 0)
+
+    small_base = count * 10
+
+    def small(stage, now, got, got_z, base):
+        if stage < 3:
+            where = (device(1 - c, z, y, x), device(c, z, 1 - y, x), device(c, z, y, 1 - x))[stage]
+            return [remote(now.at[stage], got.at[stage], base + stage, where)]
+        return [
+            remote(now.at[3], got_z.at[z], base + 2 + k, device(c, (z + k) % 4, y, x))
+            for k in (1, 2, 3)
+        ]
+
+    def small_step(stage, now, got, got_z, base):
+        if stage > 0:
+            for copy in small(stage - 1, now, got, got_z, base):
+                copy.wait()
+            if stage < 4:
+                now[stage] = now[stage - 1] + got[stage - 1]
+            else:
+                got_z[z] = now[3]
+                now[4] = (got_z[0] + got_z[1]) + (got_z[2] + got_z[3])
+        if stage < 4:
+            for copy in small(stage, now, got, got_z, base):
+                copy.start()
+
+    gains_base, stats_base = small_base, small_base + 6
+
+    def run(core):
+        for tick in range(count + 3):
+            if tick < 5:
+                small_step(tick, gains_now, gains_got, gains_z, gains_base)
+            for stage in (3, 2, 1, 0):
+                number = tick - stage
+                if not 0 <= number < count:
+                    continue
+                if stage == 0:
+                    load(number).wait()
+                    if chunks[number][5] is not None:
+                        pair_copy(number).wait()
+                        add_pair(number)
+                else:
+                    for copy in sends(number, stage - 1, core):
+                        copy.wait_recv()
+                    absorb(number, stage - 1, core)
+                if stage < 3:
+                    for copy in sends(number, stage, core):
+                        copy.start()
+        for number in range(count):
+            for stage in range(3):
+                for copy in sends(number, stage, core):
+                    copy.wait_send()
+
+    meet(c, z, y, x)
+    for number in range(count):
+        load(number).start()
+    for number in range(count):
+        if chunks[number][5] is not None:
+            pair_copy(number).start()
+    gains_now[0] = part_gains[...]
+
+    @pl.when(c == 0)
+    def _():
+        run(0)
+
+    @pl.when(c == 1)
+    def _():
+        run(1)
+
+    back = [
+        remote(sum_first.at[c], sum_first.at[c], stats_base + 6, device(1 - c, z, y, x)),
+        remote(sum_vision.at[c], sum_vision.at[c], stats_base + 7, device(1 - c, z, y, x)),
+    ]
+    for copy in back:
+        copy.start()
+
+    def squares(block):
+        rows = block.shape[0]
+        return jnp.sum((block * block).reshape(rows // 8, 8, block.shape[1]), axis=0)
+
+    gains = gains_now[4]
+    sum_gains[...] = gains
+    count_gains = jnp.where((c == 0) & (z + y + x == 0), 1.0, 0.0)
+    mass = count_gains * (gains * gains)
+    for j in range(3):
+        mass = mass + squares(sum_first[c, j])
+    mass = mass + squares(sum_vision[c])
+    mass = mass + squares(sum_expand[...]) + squares(sum_reduce[...])
+    folded = mass[:, 0:128]
+    for k in range(1, mass.shape[1] // 128):
+        folded = folded + mass[:, k * 128 : (k + 1) * 128]
+    stats_now[0, 0:8] = folded
+    stats_now[0, 8:16] = part_stats[...]
+    for stage in range(5):
+        small_step(stage, stats_now, stats_got, stats_z, stats_base)
+    totals[...] = stats_now[4]
+    for copy in back:
+        copy.wait()
+
+
+def scatter_all(part_first, part_vision, part_expand, part_reduce, part_gains, part_stats):
+    rows_first, width = part_first.shape[-2:]
+    rows_vision = part_vision.shape[-2]
+    rows_feed = part_expand.shape[-2]
+    half_feed = rows_feed // 2
+    half, single = jnp.bfloat16, jnp.float32
+    anywhere = pl.BlockSpec(memory_space=pl.ANY)
+    vmem = pl.BlockSpec(memory_space=pltpu.VMEM)
+    count = 8
+
+    def late(rows):
+        return [(4, 2, rows, width), (4, rows, width), (3, rows, width)]
+
+    def early(rows):
+        return [(4, 2, rows, width), (3, 2, rows, width), (rows, width)]
+
+    scratch = [
+        pltpu.VMEM(part_first.shape[1:], half),
+        pltpu.VMEM(part_vision.shape[1:], half),
+        pltpu.VMEM(part_expand.shape, half),
+        pltpu.VMEM(part_reduce.shape, half),
+        pltpu.VMEM(part_first.shape[1:], half),
+        pltpu.VMEM(part_vision.shape[1:], half),
+    ]
+    scratch += [pltpu.VMEM((4,) + shape, half) for shape in late(half_feed)]
+    scratch += [pltpu.VMEM((3,) + shape, half) for shape in early(rows_first)]
+    scratch += [pltpu.VMEM(shape, half) for shape in early(rows_vision)]
+    for shape in (part_gains.shape, (16, 128)):
+        scratch += [pltpu.VMEM((number,) + shape, single) for number in (5, 3, 4)]
+    scratch += [
+        pltpu.SemaphoreType.DMA((count * 10 + 14,)),
+        pltpu.SemaphoreType.DMA((count * 10 + 14,)),
+        pltpu.SemaphoreType.DMA((count,)),
+    ]
+    return pl.pallas_call(
+        scatter_kernel,
+        out_shape=[
+            jax.ShapeDtypeStruct((2, 3, rows_first, width), single),
+            jax.ShapeDtypeStruct((2, rows_vision, width), single),
+            jax.ShapeDtypeStruct((rows_feed, width), single),
+            jax.ShapeDtypeStruct((rows_feed, width), single),
+            jax.ShapeDtypeStruct(part_gains.shape, single),
+            jax.ShapeDtypeStruct((16, 128), single),
+        ],
+        in_specs=[anywhere] * 4 + [vmem] * 2,
+        out_specs=[vmem] * 6,
+        scratch_shapes=scratch,
+        compiler_params=pltpu.CompilerParams(
+            collective_id=1, has_side_effects=True, vmem_limit_bytes=VMEM_LIMIT
+        ),
+        name="scatter_grads",
+    )(part_first, part_vision, part_expand, part_reduce, part_gains, part_stats)
 
 
 def body(
@@ -183,15 +619,42 @@
     second_gains,
 ):
     stream = lax.axis_index("stream")
-    full_project, full_output, full_query, full_vision, full_expand, full_reduce, full_gains = (
-        lax.all_gather(to_half(attn_project), "dp", axis=1, tiled=True),
-        lax.all_gather(to_half(attn_output), "dp", axis=1, tiled=True),
-        lax.all_gather(to_half(cross_query), "dp", axis=0, tiled=True),
-        lax.all_gather(to_half(cross_vision), "dp", axis=1, tiled=True),
-        lax.all_gather(to_half(feed_expand), "dp", axis=1, tiled=True),
-        lax.all_gather(to_half(feed_reduce), "dp", axis=1, tiled=True),
-        lax.all_gather(to_half(norm_gains), "dp", axis=1, tiled=True),
-    )
+    direct = lax.axis_size("dp") == 16
+    if direct:
+        halves = [
+            to_half(value)
+            for value in (attn_project, attn_output, cross_query, cross_vision, feed_expand[0], feed_reduce[0])
+        ]
+        project_half, output_half, query_half_weight, vision_half, expand_half, reduce_half = halves
+        first = jnp.where(
+            stream == 0, project_half, jnp.concatenate([output_half, query_half_weight[None]], axis=0)
+        )
+        vision_own = jnp.where(stream == 0, vision_half[0], vision_half[1])
+        gains_tile = jnp.pad(to_half(norm_gains), ((0, 12), (0, 80)))
+        all_first, all_vision, all_expand, all_reduce, all_gains = gather_all(
+            first, vision_own, expand_half, reduce_half, gains_tile
+        )
+        width = attn_project.shape[-1]
+        full_first = all_first.reshape(2, 3, width, width)
+        full_project = full_first[0]
+        full_output = full_first[1, :2]
+        full_query = full_first[1, 2]
+        full_vision = all_vision.reshape(2, -1, width)
+        full_expand = all_expand.reshape(1, -1, width)
+        full_reduce = all_reduce.reshape(1, -1, width)
+        full_gains = (
+            all_gains.reshape(16, 16, 128)[:, :4, : norm_gains.shape[1]].transpose(1, 0, 2).reshape(4, width)
+        )
+    else:
+        full_project, full_output, full_query, full_vision, full_expand, full_reduce, full_gains = (
+            lax.all_gather(to_half(attn_project), "dp", axis=1, tiled=True),
+            lax.all_gather(to_half(attn_output), "dp", axis=1, tiled=True),
+            lax.all_gather(to_half(cross_query), "dp", axis=0, tiled=True),
+            lax.all_gather(to_half(cross_vision), "dp", axis=1, tiled=True),
+            lax.all_gather(to_half(feed_expand), "dp", axis=1, tiled=True),
+            lax.all_gather(to_half(feed_reduce), "dp", axis=1, tiled=True),
+            lax.all_gather(to_half(norm_gains), "dp", axis=1, tiled=True),
+        )
     gain_rows = full_gains.astype(jnp.float32)
     gain_self = gain_rows[0]
     gain_cross = gain_rows[1]
@@ -373,42 +836,6 @@
         vision_term,
         gain_grads,
     )
-    (
-        parts_project,
-        parts_output,
-        parts_query,
-        parts_vision,
-        parts_expand,
-        parts_reduce,
-        parts_gains,
-    ) = (
-        lax.psum_scatter(shared_grads[0], "dp", scatter_dimension=1, tiled=True),
-        lax.psum_scatter(shared_grads[1], "dp", scatter_dimension=1, tiled=True),
-        lax.psum_scatter(shared_grads[2], "dp", scatter_dimension=0, tiled=True),
-        lax.psum_scatter(shared_grads[3], "dp", scatter_dimension=1, tiled=True),
-        lax.psum_scatter(grad_expand[None], "dp", scatter_dimension=1, tiled=True),
-        lax.psum_scatter(grad_reduce[None], "dp", scatter_dimension=1, tiled=True),
-        lax.psum_scatter(shared_grads[4], "dp", scatter_dimension=1, tiled=True),
-    )
-    sum_project, sum_output, sum_query, sum_vision, sum_gains = (
-        lax.psum(parts_project.astype(jnp.bfloat16), "stream").astype(jnp.float32),
-        lax.psum(parts_output.astype(jnp.bfloat16), "stream").astype(jnp.float32),
-        lax.psum(parts_query.astype(jnp.bfloat16), "stream").astype(jnp.float32),
-        lax.psum(parts_vision.astype(jnp.bfloat16), "stream").astype(jnp.float32),
-        lax.psum(parts_gains.astype(jnp.bfloat16), "stream").astype(jnp.float32),
-    )
-    shared_square = (
-        jnp.sum(sum_project * sum_project)
-        + jnp.sum(sum_output * sum_output)
-        + jnp.sum(sum_query * sum_query)
-        + jnp.sum(sum_vision * sum_vision)
-        + jnp.sum(sum_gains * sum_gains)
-    )
-    local_square = (
-        0.5 * shared_square
-        + jnp.sum(parts_expand * parts_expand)
-        + jnp.sum(parts_reduce * parts_reduce)
-    )
     stat_row = jnp.stack(
         [
             square_rows(source),
@@ -420,7 +847,67 @@
     stat_local = jnp.where(
         jnp.arange(2, dtype=jnp.int32)[:, None] == stream, stat_row[None, :], 0.0
     )
-    total_square, stat_sums = lax.psum((local_square, stat_local), ("stream", "dp"))
+    if direct:
+        width = grad_project.shape[-1]
+        rows = attn_project.shape[1]
+        part_first = to_half(
+            jnp.stack([grad_project, jnp.stack([grad_out_self, grad_out_cross, grad_cross_weight])])
+        ).reshape(2, 3, 4, 2, 2, rows, width)
+        part_vision = to_half(vision_term).reshape(2, 4, 2, 2, cross_vision.shape[1], width)
+        part_expand = to_half(grad_expand).reshape(4, 2, 2, feed_expand.shape[1], width)
+        part_reduce = to_half(grad_reduce).reshape(4, 2, 2, feed_reduce.shape[1], width)
+        part_stats = jnp.pad(stat_local.reshape(8, 1), ((0, 0), (0, 127)))
+        sum_first, sum_vision, sum_expand, sum_reduce, all_gain_sums, totals = scatter_all(
+            part_first, part_vision, part_expand, part_reduce, jnp.pad(gain_grads, ((0, 4), (0, 0))), part_stats
+        )
+        sum_project = sum_first[0]
+        sum_output = sum_first[1, :2]
+        sum_query = sum_first[1, 2]
+        parts_expand, parts_reduce = sum_expand[None], sum_reduce[None]
+        own_gains = norm_gains.shape[1]
+        sum_gains = lax.dynamic_slice_in_dim(
+            all_gain_sums[:4], lax.axis_index("dp") * own_gains, own_gains, axis=1
+        )
+        total_square = jnp.sum(totals[:8])
+        stat_sums = jnp.sum(totals[8:], axis=1).reshape(2, 4)
+    else:
+        (
+            parts_project,
+            parts_output,
+            parts_query,
+            parts_vision,
+            parts_expand,
+            parts_reduce,
+            parts_gains,
+        ) = (
+            lax.psum_scatter(shared_grads[0], "dp", scatter_dimension=1, tiled=True),
+            lax.psum_scatter(shared_grads[1], "dp", scatter_dimension=1, tiled=True),
+            lax.psum_scatter(shared_grads[2], "dp", scatter_dimension=0, tiled=True),
+            lax.psum_scatter(shared_grads[3], "dp", scatter_dimension=1, tiled=True),
+            lax.psum_scatter(grad_expand[None], "dp", scatter_dimension=1, tiled=True),
+            lax.psum_scatter(grad_reduce[None], "dp", scatter_dimension=1, tiled=True),
+            lax.psum_scatter(shared_grads[4], "dp", scatter_dimension=1, tiled=True),
+        )
+        sum_project, sum_output, sum_query, sum_vision, sum_gains = (
+            lax.psum(parts_project.astype(jnp.bfloat16), "stream").astype(jnp.float32),
+            lax.psum(parts_output.astype(jnp.bfloat16), "stream").astype(jnp.float32),
+            lax.psum(parts_query.astype(jnp.bfloat16), "stream").astype(jnp.float32),
+            lax.psum(parts_vision.astype(jnp.bfloat16), "stream").astype(jnp.float32),
+            lax.psum(parts_gains.astype(jnp.bfloat16), "stream").astype(jnp.float32),
+        )
+        shared_square = (
+            jnp.sum(sum_project * sum_project)
+            + jnp.sum(sum_output * sum_output)
+            + jnp.sum(sum_query * sum_query)
+            + jnp.sum(sum_vision * sum_vision)
+            + jnp.sum(sum_gains * sum_gains)
+        )
+        local_square = (
+            0.5 * shared_square
+            + jnp.sum(parts_expand * parts_expand)
+            + jnp.sum(parts_reduce * parts_reduce)
+        )
+        total_square, stat_sums = lax.psum((local_square, stat_local), ("stream", "dp"))
     grad_norm = jnp.sqrt(total_square)
     rms_values = jnp.sqrt(stat_sums / (row_count * lax.axis_size("dp")))
     factor = clip_norm / jnp.maximum(grad_norm, clip_norm)

time: 1830 us -> 885 us (0.48)
  waiting for transfers between devices: 1190 us -> 0.01 us
  Pallas kernels: 0 us -> 373 us
  blocking collectives: 84 us -> 0 us
  other arithmetic: 90.7 us -> 70.6 us
    reduce_scatter x6 -> x0, waiting for transfers between devices: 834 us -> none  [the longest x1 173 us: body(): lax.psum_scatter(grad_reduce[None], 'dp', scatter_dimension=1, tiled=True)]
    pallas_call x0 -> x2, Pallas kernels: none -> 373 us  [the longest x1 200 us: scatter_all(): pl.pallas_call(scatter_kernel, out_shape=[jax.ShapeDtypeStruct((2, 3, row...]
    all_gather x6 -> x0, waiting for transfers between devices: 237 us -> none  [the longest x1 79.1 us: body(): lax.all_gather(to_half(cross_vision), 'dp', axis=1, tiled=True)]
    unnamed x15 -> x0, waiting for transfers between devices: 101 us -> none
    all_gather x1 -> x0, blocking collectives: 42.4 us -> none  [body(): lax.all_gather(to_half(norm_gains), 'dp', axis=1, tiled=True)]
    psum x2 -> x0, blocking collectives: 41.6 us -> none  [the longest x1 39.2 us: body(): lax.psum((local_square, stat_local), ('stream', 'dp'))]
    convert_element_type x16 -> x14, other arithmetic: 39.2 us -> 32.5 us  [to_half(): return values.astype(jnp.bfloat16)]
  transfers between devices with their start and end apart: 18 -> 4, of which waited for: 13 -> 0; matrix products, arithmetic and copies ran while one was open for 15% -> 3% of each run, Pallas kernels for 0% -> 0%
where the time goes in v1:
time: 885 us; the launch traced here: 877 us
  Pallas kernels  373 us (42%)
  matrix products  254 us (29%)
  local copies, waits for them, and re-layouts  152 us (17%)
  other arithmetic  70.6 us (8%)
  loops' own time  16.9 us (2%)
    pallas_call x1, Pallas kernels, scatter_all(): pl.pallas_call(scatter_kernel, out_shape=[jax.ShapeDtypeStruct((2, 3, row...  200 us
    pallas_call x1, Pallas kernels, gather_all(): pl.pallas_call(gather_kernel, out_shape=[jax.ShapeDtypeStruct(shape, half...  173 us
    dot_general x10, matrix products, right_product(): lax.dot_general(left, right, (((1,), (1,)), ((), ())), preferred_element_...  45.1 us
    convert_element_type x14, other arithmetic, to_half(): return values.astype(jnp.bfloat16)  32.5 us
    another operation x28, local copies, waits for them, and re-layouts  31.4 us
    dot_general x1, matrix products, vision_grad(): jnp.einsum('inv,kind->kvd', feature_block, grad_pair, preferred_element_t...  30.4 us
    dot_general x2, matrix products, attend_back(): jnp.einsum('bqhd,bkhd->bhqk', grad_heads, value_heads, preferred_element_...  28.3 us
    dot_general x10, matrix products, left_product(): lax.dot_general(left, right, (((0,), (0,)), ((), ())), preferred_element_...  27.2 us
  transfers between devices with their start and end apart: 4, of which 0 were waited for; matrix products, arithmetic and copies ran while one was open for 3% of the time, Pallas kernels for 0%

profile of v1, /device:TPU:0, one launch (start us, length us, event | category | flops | bytes accessed | tf_op | source)
XLA Modules:
  0.0 877.2 jit_solution(18347686179812886949)
XLA Ops:
  9.6 172.8 %gather_weights.1 = (bf16[2,3,4,2,2,48,768]{6,5,4,3,2,1,0:T(8,128)(2,1)}, bf16[2,4,2,2,88,768]{5,4,3,2,1,0:T(8,128)(2,1)}, bf16[4,2,2,192,768]{4,3,2,1,0:T(8,128...) custom-call(bf16[3,48,768]{2,1,0:T(8,128)(2,1)} %maximum_select_fusion.first, ...), custom_call_target="tpu_custom_call" | custom-call | tf_op jit(solution)/shard_map/gather_weights/pallas_call | solution.py:290
  186.9 2.8 collective-permute-start.1
  197.5 2.4 slice_bitcast_fusion.3
  199.8 3.3 slice_bitcast_fusion.2
  203.1 2.4 pad_maximum_fusion.1
  205.5 2.6 pad_maximum_fusion
  208.1 25.0 %conditional.6 = (f32[1,12,512]{2,1,0:T(8,128)S(1)}, bf16[512,768]{0,1:T(8,128)(2,1)S(1)}) conditional(s32[]{:T(128)} %convert_element_type.235, (pred[512,1024]{0,1:T(8,128)(4,1)}, bf16[512,768]{1,0:T(8,128)(2,1)S(1)}, bf16[1024,768]{1,0:T(8,128)(2,1)}, bf16[1024,768]{1,0:T(8,128)(2,1)}) %tuple.70, (pred[512,512]{0,1:T(8,128)(4,1)S(1)}, ...), branch_computations={%region_4.7_spmd, %region_7.10_spmd} | conditional | flops 1686497280 | bytes 96927784 | solution.py:682
  218.5 3.2 fusion.6
  221.7 2.6 fusion.7
  226.5 6.6 fusion.9
  233.2 3.0 multiply_reduce_fusion.10
  236.2 88.5 %conditional.7 = (f32[512,768]{1,0:T(8,128)}, f32[16,12,32]{2,1,0:T(8,128)S(1)}, bf16[2,16,257,768]{3,2,1,0:T(8,128)(2,1)}, bf16[512,768]{1,0:T(8,128)(2,1)}, bf...) conditional(s32[]{:T(128)} %convert_element_type.235, () %tuple.72, ...), branch_computations={%region_10.11_spmd, %region_11.15_spmd} | conditional | flops 19421405184 | bytes 209458352 | solution.py:708
  239.0 2.7 reshape.608
  241.7 24.4 %fusion.31 = bf16[2,16,257,768]{3,2,1,0:T(8,128)(2,1)S(1)} fusion(bf16[2,1408,768,1]{2,1,3,0:T(8,128)(2,1)} %bitcast.431, bf16[16,257,1408]{2,0,1:T(8,128)(2,1)} %get-tuple-element.319), kind=kOutput, calls=%fused_computation.50 | convolution fusion | flops 17792262144 | bytes 28536832 | tf_op jit(solution)/shard_map/cond/branch_1_fun/inv,kvd->kind/dot_general | solution.py:137
  266.1 5.5 fusion.144
  271.7 3.0 copy-done
  274.7 11.2 %copy.139 = bf16[1,16,257,768]{2,3,1,0:T(8,128)(2,1)} copy(bf16[1,16,257,768]{3,2,1,0:T(8,128)(2,1)} %get-tuple-element.408) | data formatting | bytes 12632064 | tf_op jit(solution)/shard_map/cond/branch_1_fun/slice | solution.py:692
  285.9 6.2 multiply_reduce_fusion.2
  292.1 2.5 fusion.34
  295.7 11.2 %copy.138 = bf16[1,16,257,768]{2,3,1,0:T(8,128)(2,1)} copy(bf16[1,16,257,768]{3,2,1,0:T(8,128)(2,1)} %get-tuple-element.409) | data formatting | bytes 12632064 | tf_op jit(solution)/shard_map/cond/branch_1_fun/slice | solution.py:692
  306.8 8.3 fusion.39
  317.2 3.9 convert_element_type.179
  321.0 3.4 fusion.40
  327.7 19.4 %multiply_convert_fusion.9 = (bf16[512,3072]{1,0:T(8,128)(2,1)S(1)}, f32[512,3072]{1,0:T(8,128)}, f32[512,3072]{1,0:T(8,128)}) fusion(bf16[3072,768]{1,0:T(8,128)(2,1)S(1)} %bitcast.429, f32[512,768]{1,0:T(8,128)S(1)} %get-tuple-element.393, f32[768]{0:T(1024)S(1)} %copy-done.63, f32[512]{0:T(512)S(1)} %fusion.123), kind=kOutput, calls=%fused_computation.121 | convolution fusion | flops 2519334912 | bytes 22025216 | tf_op jit(solution)/shard_map/dot_general | solution.py:46
  347.1 8.2 fusion.83
  355.3 2.6 fusion.153
  357.9 4.7 multiply_reduce_fusion.9
  363.0 182.3 %conditional.16 = (f32[512,768]{1,0:T(8,128)}, f32[1,768]{1,0:T(1,128)}, bf16[2,4,2,2,88,768]{5,4,3,2,1,0:T(8,128)(2,1)}, bf16[1,1,4,2,2,48,768]{6,5,4,3,2,1,0:T(8,128)(2,1)}, bf16[1,1,4,2,2,48,768]{6,5,4,3,2,1,0:T(8,128)(2,1)}) conditional(s32[]{:T(128)} %convert_element_type.235, () %tuple.74, (bf16[512,768]{1,0:T(8,128)(2,1)}, ...), branch_computations={%region_17.18_spmd, %region_18.23_spmd} | conditional | flops 21257584640 | bytes 267592896 | solution.py:758
  363.3 21.2 %copy.164 = bf16[2,16,257,768]{2,3,1,0:T(8,128)(2,1)} copy(bf16[2,16,257,768]{3,2,1,0:T(8,128)(2,1)} %get-tuple-element.325) | data formatting | bytes 25264128 | tf_op jit(solution)/shard_map
  384.5 14.5 %fusion.145 = (bf16[1,16,257,768]{2,3,1,0:T(8,128)(2,1)}, bf16[1,16,257,768]{2,3,1,0:T(8,128)(2,1)}) fusion(bf16[2,16,257,768]{2,3,1,0:T(8,128)(2,1)} %copy.164), kind=kLoop, calls=%fused_computation.278 | loop fusion | bytes 25264128 | tf_op jit(solution)/shard_map/cond/branch_1_fun/slice | solution.py:733
  399.0 3.8 reshape.610
  402.7 9.9 %fusion.70 = f32[16,12,32,257]{3,2,1,0:T(8,128)} fusion(bf16[16,257,12,64]{1,3,2,0:T(8,128)(2,1)} %bitcast.366, bf16[16,32,12,64]{3,2,1,0:T(8,128)(2,1)} %reshape.610), kind=kOutput, calls=%fused_computation.100 | convolution fusion | flops 202113024 | bytes 13418496 | tf_op jit(solution)/shard_map/cond/branch_1_fun/bqhd,bkhd->bhqk/dot_general | solution.py:87
  414.4 3.8 reshape.611
  418.1 14.7 %multiply_reduce_fusion.4 = (f32[16,12,32]{2,1,0:T(8,128)S(1)}, f32[16,12,32,257]{3,2,1,0:T(8,128)}) fusion(f32[16,12,32,257]{3,2,1,0:T(8,128)} %fusion.70, f32[16,12,32]{2,1,0:T(8,128)S(1)} %get-tuple-element.119, bf16[16,257,12,64]{1,3,2,0:T(8,128)(2,1)} %bitcast.371, bf16[16,32,12,64]{3,2,1,0:T(8,128)(2,1)} %reshape.611), kind=kOutput, calls=%fused_computation.77 | convolution fusion | flops 208422912 | bytes 19783680 | tf_op jit(solution)/shard_map/cond/branch_1_fun/bqhd,bkhd->bhqk/dot_general | solution.py:113
  432.9 8.1 multiply_convert_fusion.7
  441.0 8.5 fusion.63
  451.5 3.9 convert_element_type.185
  455.6 2.5 multiply_reduce_fusion.5
  460.2 9.3 %multiply_convert_fusion.6 = bf16[16,12,257,64]{2,3,1,0:T(8,128)(2,1)} fusion(bf16[16,12,32,257]{3,2,1,0:T(8,128)(2,1)} %multiply_convert_fusion.7, bf16[16,32,12,64]{3,2,1,0:T(8,128)(2,1)} %reshape.610), kind=kOutput, calls=%fused_computation.69 | convolution fusion | flops 208429056 | bytes 10260480 | tf_op jit(solution)/shard_map/cond/branch_1_fun/bhqk,bqhd->bkhd/dot_general | solution.py:125
  469.5 11.6 %copy.147 = bf16[1,16,257,768]{3,2,1,0:T(8,128)(2,1)} copy(bf16[1,16,257,768]{2,3,1,0:T(8,128)(2,1)} %bitcast.373) | data formatting | bytes 12632064 | tf_op jit(solution)/shard_map/cond/branch_1_fun/stack;cond/branch_1_fun/reshape | solution.py:740
  481.0 10.8 %convolution_convert_fusion.2 = bf16[16,12,64,257]{3,2,1,0:T(8,128)(2,1)} fusion(f32[16,12,32,257]{3,2,1,0:T(8,128)} %fusion.70, f32[16,12,32]{2,1,0:T(8,128)S(1)} %get-tuple-element.119, bf16[16,32,12,64]{3,2,1,0:T(8,128)(2,1)} %reshape.611), kind=kOutput, calls=%fused_computation.80 | convolution fusion | flops 210008064 | bytes 13443072 | tf_op jit(solution)/shard_map/cond/branch_1_fun/bhqk,bqhd->bkhd/dot_general | solution.py:116
  491.8 11.4 %copy.148 = bf16[1,16,257,768]{3,2,1,0:T(8,128)(2,1)} copy(bf16[1,16,257,768]{2,3,1,0:T(8,128)(2,1)} %bitcast.372) | data formatting | bytes 12632064 | tf_op jit(solution)/shard_map/cond/branch_1_fun/stack;cond/branch_1_fun/reshape | solution.py:740
  503.2 30.4 %fusion.58 = bf16[2,1408,768]{1,2,0:T(8,128)(2,1)} fusion(bf16[16,257,1408]{2,0,1:T(8,128)(2,1)} %get-tuple-element.332, bf16[1,16,257,768]{3,2,1,0:T(8,128)(2,1)} %copy.148, bf16[1,16,257,768]{3,2,1,0:T(8,128)(2,1)} %copy.147), kind=kOutput, calls=%fused_computation.84 | convolution fusion | flops 17794424832 | bytes 28536832 | tf_op jit(solution)/shard_map/cond/branch_1_fun/inv,kind->kvd/dot_general | solution.py:144
  533.6 6.7 copy.149
  542.2 3.0 convolution_convert_fusion.4
  548.3 3.0 convolution_convert_fusion.10
  551.4 4.6 convolution_convert_fusion.7
  555.9 52.6 %conditional.17 = (bf16[512,768]{0,1:T(8,128)(2,1)}, bf16[512,768]{0,1:T(8,128)(2,1)}, bf16[512,768]{0,1:T(8,128)(2,1)}, bf16[512,768]{0,1:T(8,128)(2,1)}, bf16[512,768]{0,1:T(8,128)(2,1)}) conditional(s32[]{:T(128)} %convert_element_type.235, (pred[512,1024]{0,1:T(8,128)(4,1)}, bf16[512,768]{1,0:T(8,128)(2,1)}, bf16[1024,768]{1,0:T(8,128)(2,1)}, ...), branch_computations={%region_23.25_spmd, %region_25.27_spmd} | conditional | flops 4123256832 | bytes 274587776
  567.2 6.3 fusion.152
  575.9 13.6 %multiply_reduce_fusion.1 = (f32[12,512]{1,0:T(8,128)S(1)}, f32[12,512,512]{1,2,0:T(8,128)}) fusion(f32[12,512,512]{1,2,0:T(8,128)} %fusion.152, f32[12,512]{1,0:T(8,128)S(1)} %bitcast.419, pred[512,512]{0,1:T(8,128)(4,1)S(1)} %get-tuple-element.134, bf16[512,12,64]{0,2,1:T(8,128)(2,1)} %bitcast.396, bf16[512,12,64]{0,2,1:T(8,128)(2,1)} %bitcast.401), kind=kOutput, calls=%fused_computation.37 | convolution fusion | flops 418375680 | bytes 27049984 | tf_op jit(solution)/shard_map/cond/branch_1_fun/bqhd,bkhd->bhqk/dot_general | solution.py:113
  589.5 7.0 multiply_convert_fusion.2
  596.5 2.9 multiply_convert_fusion.3
  601.5 4.9 fusion.24
  608.6 2.5 fusion.155
  611.1 2.5 fusion.154
  622.0 4.3 fusion.148
  628.0 2.5 multiply_reduce_fusion.12
  630.5 3.4 fusion.158
  633.9 3.4 fusion.159
  638.5 2.7 pad_maximum_fusion.2
  648.6 2.7 add_convert_fusion.1
  652.2 5.1 maximum_maximum_fusion.part_first
  657.3 200.4 %scatter_grads.1 = (f32[2,3,48,768]{3,2,1,0:T(8,128)}, f32[2,88,768]{2,1,0:T(8,128)}, f32[192,768]{1,0:T(8,128)}, f32[192,768]{1,0:T(8,128)}, f32[8,768]{1,0:T(8,128)}, /*index=5*/f32[16,128]{1,0:T(8,128)}) custom-call(bf16[2,3,4,2,2,48,768]{6,5,4,3,2,1,0:T(8,128)(2,1)} %maximum_maximum_fusion.part_first, ...), custom_call_target="tpu_custom_call" | custom-call | tf_op jit(solution)/shard_map/scatter_grads/pallas_call | solution.py:573
  865.7 2.9 fusion.139
  (271 shorter events, 89.0 us)
Async XLA Ops:
  0.7 182.6 %copy-start.4 = (f32[1,512,768]{2,1,0:T(8,128)S(1)}, f32[1,512,768]{2,1,0:T(8,128)}, u32[]{:S(2)}) copy-start(f32[1,512,768]{2,1,0:T(8,128)} %param.34) | copy-start | bytes 4718596
  185.8 5.6 copy-start.21
  185.8 5.5 copy-start.39
  185.8 7.7 copy-start.41
  186.0 8.3 copy-start.73
  186.0 8.5 copy-start.75
  186.9 21.3 %copy-start.13 = (bf16[512,768]{1,0:T(8,128)(2,1)}, bf16[512,768]{1,0:T(8,128)(2,1)S(1)}, u32[]{:S(2)}) copy-start(bf16[512,768]{1,0:T(8,128)(2,1)S(1)} %convolution_convert_fusion.11) | copy-start | bytes 2359300
  186.9 16.2 %collective-permute-start.1 = (bf16[512,768]{1,0:T(8,128)(2,1)S(1)}, bf16[512,768]{1,0:T(8,128)(2,1)}, u32[]{:S(2)}, u32[]{:S(2)}) collective-permute-start(bf16[512,768]{1,0:T(8,128)(2,1)S(1)} %convolution_convert_fusion.11), channel_id=1, source_target_pairs={{0,16},{1,17},{2,18},{3,19},{4,20},{5,21},{6,22},{7,23},{8,24},{9,... | collective-permute-start | bytes 2359304 | tf_op jit(solution)/shard_map/ppermute | solution.py:28
  191.3 14.2 %collective-permute-start = (bf16[512,768]{1,0:T(8,128)(2,1)}, bf16[512,768]{1,0:T(8,128)(2,1)}, u32[]{:S(2)}, u32[]{:S(2)}) collective-permute-start(bf16[512,768]{1,0:T(8,128)(2,1)} %convolution_convert_fusion.12), channel_id=1, source_target_pairs={{0,16},{1,17},{2,18},{3,19},{4,20},{5,21},{6,22},{7,23},{8,24},{9,... | collective-permute-start | bytes 2359304 | tf_op jit(solution)/shard_map/ppermute | solution.py:28
  194.3 13.8 %copy-start.9 = (bf16[512,768]{1,0:T(8,128)(2,1)}, bf16[512,768]{1,0:T(8,128)(2,1)S(1)}, u32[]{:S(2)}) copy-start(bf16[512,768]{1,0:T(8,128)(2,1)S(1)} %convolution_convert_fusion.13) | copy-start | bytes 2359300
  195.3 12.8 %copy-start.16 = (pred[512,512]{0,1:T(8,128)(4,1)}, pred[512,512]{0,1:T(8,128)(4,1)S(1)}, u32[]{:S(2)}) copy-start(pred[512,512]{0,1:T(8,128)(4,1)S(1)} %get-tuple-element.430) | copy-start | bytes 786436
  221.7 4.5 copy-start.3
  236.6 29.5 %copy-start.45 = (bf16[512,768]{1,0:T(8,128)(2,1)}, bf16[512,768]{1,0:T(8,128)(2,1)S(1)}, u32[]{:S(2)}) copy-start(bf16[512,768]{1,0:T(8,128)(2,1)S(1)} %multiply_convert_fusion.5) | copy-start | bytes 2359300 | tf_op jit(solution)/shard_map/cond
  239.0 27.2 %copy-start.15 = (bf16[512,768]{1,0:T(8,128)(2,1)}, bf16[512,768]{1,0:T(8,128)(2,1)S(1)}, u32[]{:S(2)}) copy-start(bf16[512,768]{1,0:T(8,128)(2,1)S(1)} %convolution_convert_fusion.1) | copy-start | bytes 2359300 | tf_op jit(solution)/shard_map/cond
  266.1 8.6 copy-start
  326.5 36.1 %copy-start.19 = (f32[512,768]{1,0:T(8,128)}, f32[512,768]{1,0:T(8,128)S(1)}, u32[]{:S(2)}) copy-start(f32[512,768]{1,0:T(8,128)S(1)} %get-tuple-element.393) | copy-start | bytes 4718596
  327.6 19.4 %copy-start.36 = (f32[1,512,768]{2,1,0:T(8,128)S(1)}, f32[1,512,768]{2,1,0:T(8,128)}, u32[]{:S(2)}) copy-start(f32[1,512,768]{2,1,0:T(8,128)} %param.38) | copy-start | bytes 4718596
  327.7 19.4 %copy-start.76 = (bf16[4,2,2,192,768]{4,3,2,1,0:T(8,128)(2,1)S(1)}, bf16[4,2,2,192,768]{4,3,2,1,0:T(8,128)(2,1)}, u32[]{:S(2)}) copy-start(bf16[4,2,2,192,768]{4,3,2,1,0:T(8,128)(2,1)} %get-tuple-element.207) | copy-start | bytes 14155780
  347.1 10.9 %copy-start.78 = (bf16[512,3072]{1,0:T(8,128)(2,1)}, bf16[512,3072]{1,0:T(8,128)(2,1)S(1)}, u32[]{:S(2)}) copy-start(bf16[512,3072]{1,0:T(8,128)(2,1)S(1)} %get-tuple-element.390) | copy-start | bytes 9437188
  402.7 9.9 %copy-start.34 = (bf16[2,768,768]{2,1,0:T(8,128)(2,1)S(1)}, bf16[2,768,768]{2,1,0:T(8,128)(2,1)}, u32[]{:S(2)}) copy-start(bf16[2,768,768]{2,1,0:T(8,128)(2,1)} %get-tuple-element.121) | copy-start | bytes 7077892 | tf_op jit(solution)/shard_map/cond
  418.1 14.7 %slice-start = ((s8[9437184]{0:T(1024)(128)(4,1)}), s8[4194304]{0:T(1024)(128)(4,1)S(1)}, s32[]{:S(2)}) async-start(s8[9437184]{0:T(1024)(128)(4,1)} %bitcast.364), calls=%async_computation | async-start | bytes 8388608 | tf_op jit(solution)/shard_map/cond
  418.1 14.7 %slice-start.1 = ((s8[9437184]{0:T(1024)(128)(4,1)}), s8[4194304]{0:T(1024)(128)(4,1)S(1)}, s32[]{:S(2)}) async-start(s8[9437184]{0:T(1024)(128)(4,1)} %bitcast.364), calls=%async_computation.1 | async-start | bytes 8388608 | tf_op jit(solution)/shard_map/cond
  418.1 14.7 %slice-start.2 = ((s8[9437184]{0:T(1024)(128)(4,1)}), s8[1048576]{0:T(1024)(128)(4,1)S(1)}, s32[]{:S(2)}) async-start(s8[9437184]{0:T(1024)(128)(4,1)} %bitcast.364), calls=%async_computation.2 | async-start | bytes 2097152 | tf_op jit(solution)/shard_map/cond
  533.6 6.7 copy-start.46
  533.6 6.7 copy-start.47
  545.4 6.0 copy-start.17
  545.4 6.0 copy-start.20
  545.4 6.0 copy-start.43
  545.4 5.9 copy-start.81
  565.4 8.1 copy-start.28
  567.1 6.4 copy-start.10
  567.2 6.4 copy-start.30
  567.2 7.5 copy-start.14
  575.9 13.6 %slice-start.3 = ((s8[12582912]{0:T(1024)(128)(4,1)}), s8[4194304]{0:T(1024)(128)(4,1)S(1)}, s32[]{:S(2)}) async-start(s8[12582912]{0:T(1024)(128)(4,1)} %bitcast.368), calls=%async_computation.3 | async-start | bytes 8388608 | tf_op jit(solution)/shard_map/conditional.1
  575.9 13.6 %slice-start.4 = ((s8[12582912]{0:T(1024)(128)(4,1)}), s8[4194304]{0:T(1024)(128)(4,1)S(1)}, s32[]{:S(2)}) async-start(s8[12582912]{0:T(1024)(128)(4,1)} %bitcast.368), calls=%async_computation.4 | async-start | bytes 8388608 | tf_op jit(solution)/shard_map/conditional.1
  575.9 13.6 %slice-start.5 = ((s8[12582912]{0:T(1024)(128)(4,1)}), s8[4194304]{0:T(1024)(128)(4,1)S(1)}, s32[]{:S(2)}) async-start(s8[12582912]{0:T(1024)(128)(4,1)} %bitcast.368), calls=%async_computation.5 | async-start | bytes 8388608 | tf_op jit(solution)/shard_map/conditional.1
  589.5 7.0 copy-start.29
  608.5 5.1 copy-start.22
  608.5 9.6 %copy-start.72 = (f32[512]{0:T(512)S(1)}, f32[512]{0:T(512)}, u32[]{:S(2)}) copy-start(f32[512]{0:T(512)} %get-tuple-element.353) | copy-start | bytes 6148
  608.5 10.2 %copy-start.71 = (f32[512]{0:T(512)S(1)}, f32[512]{0:T(512)}, u32[]{:S(2)}) copy-start(f32[512]{0:T(512)} %get-tuple-element.354) | copy-start | bytes 6148
  608.5 10.8 %copy-start.65 = (f32[512]{0:T(512)S(1)}, f32[512]{0:T(512)}, u32[]{:S(2)}) copy-start(f32[512]{0:T(512)} %get-tuple-element.422) | copy-start | bytes 6148
  608.5 11.4 %copy-start.68 = (f32[768]{0:T(1024)S(1)}, f32[768]{0:T(1024)}, u32[]{:S(2)}) copy-start(f32[768]{0:T(1024)} %get-tuple-element.356) | copy-start | bytes 9220
  608.6 12.6 %copy-start.7 = (f32[512,768]{1,0:T(8,128)S(1)}, f32[512,768]{1,0:T(8,128)}, u32[]{:S(2)}) copy-start(f32[512,768]{1,0:T(8,128)} %copy-done.6) | copy-start | bytes 4718596
  608.6 12.6 %copy-start.27 = (bf16[512,768]{0,1:T(8,128)(2,1)S(1)}, bf16[512,768]{0,1:T(8,128)(2,1)}, u32[]{:S(2)}) copy-start(bf16[512,768]{0,1:T(8,128)(2,1)} %copy-done.26) | copy-start | bytes 2359300
  611.1 10.9 %copy-start.37 = (f32[1,512,768]{2,1,0:T(8,128)S(1)}, f32[1,512,768]{2,1,0:T(8,128)}, u32[]{:S(2)}) copy-start(f32[1,512,768]{2,1,0:T(8,128)} %param.38) | copy-start | bytes 4718596
  611.1 10.9 %copy-start.79 = (bf16[512,3072]{1,0:T(8,128)(2,1)S(1)}, bf16[512,3072]{1,0:T(8,128)(2,1)}, u32[]{:S(2)}) copy-start(bf16[512,3072]{1,0:T(8,128)(2,1)} %copy-done.78) | copy-start | bytes 9437188
  615.6 10.8 %collective-permute-start.2 = (bf16[512,768]{0,1:T(8,128)(2,1)}, bf16[512,768]{0,1:T(8,128)(2,1)S(1)}, u32[]{:S(2)}, u32[]{:S(2)}) collective-permute-start(bf16[512,768]{0,1:T(8,128)(2,1)} %get-tuple-element.218), channel_id=1, source_target_pairs={{16,0},{17,1},{18,2},{19,3},{20,4},{21,5},{22,6},{23,7},{24,8},{25... | collective-permute-start | bytes 2359304 | tf_op jit(solution)/shard_map/ppermute | solution.py:28
  616.9 10.3 %collective-permute-start.3 = (bf16[512,768]{0,1:T(8,128)(2,1)}, bf16[512,768]{0,1:T(8,128)(2,1)S(1)}, u32[]{:S(2)}, u32[]{:S(2)}) collective-permute-start(bf16[512,768]{0,1:T(8,128)(2,1)} %get-tuple-element.219), channel_id=1, source_target_pairs={{16,0},{17,1},{18,2},{19,3},{20,4},{21,5},{22,6},{23,7},{24,8},{25... | collective-permute-start | bytes 2359304 | tf_op jit(solution)/shard_map/ppermute | solution.py:28
  622.0 4.4 copy-start.40
  622.0 5.2 copy-start.58
  622.0 5.2 copy-start.60
  630.5 6.8 copy-start.62
  630.5 10.6 %copy-start.74 = (pred[2]{0:T(512)(128)(4,1)S(1)}, pred[2]{0:T(512)(128)(4,1)}, u32[]{:S(2)}) copy-start(pred[2]{0:T(512)(128)(4,1)} %iota_compare_fusion.4) | copy-start | bytes 10
  643.1 4.1 copy-start.64
  644.3 7.0 copy-start.12
  644.3 7.0 copy-start.25
  657.3 206.2 %copy-start.38 = (f32[2,48,768]{2,1,0:T(8,128)S(1)}, f32[2,48,768]{2,1,0:T(8,128)}, u32[]{:S(2)}) copy-start(f32[2,48,768]{2,1,0:T(8,128)} %param.40) | copy-start | bytes 884740
  857.8 10.9 %copy-start.8 = (f32[512,768]{1,0:T(8,128)S(1)}, f32[512,768]{1,0:T(8,128)}, u32[]{:S(2)}) copy-start(f32[512,768]{1,0:T(8,128)} %copy-done.6) | copy-start | bytes 4718596
  857.8 10.9 %copy-start.66 = (f32[512]{0:T(512)S(1)}, f32[512]{0:T(512)}, u32[]{:S(2)}) copy-start(f32[512]{0:T(512)} %get-tuple-element.429) | copy-start | bytes 6148
  861.4 7.3 copy-start.18
  865.7 4.5 copy-start.32
  865.7 4.5 copy-start.48
  865.7 4.6 copy-start.49
  865.7 4.6 copy-start.53
  (25 other events, 70.2 us)

commit v2 on v0

v2 whole, which is shorter than its diff:
```python
import functools

import jax
import jax.numpy as jnp
from jax import lax
from jax.experimental import pallas as pl
from jax.experimental.pallas import tpu as pltpu
from jax.sharding import PartitionSpec as P

HEADS = 12
HD = 64
NQ = 32
STEP = 10


epsilon = 1e-06
masked_value = -1e30
beta_first = 0.9
beta_second = 0.999
rate_matrix = 0.05
rate_gains = 1.0
decay_rate = 0.01
adam_floor = 1e-08
clip_norm = 1.0


def shifted(block, axis, distance):
    devices = range(lax.axis_size(axis))
    route = [(i - distance, i) for i in devices if i - distance in devices]
    return lax.ppermute(block, axis, route)


def to_half(values):
    return values.astype(jnp.bfloat16)


def product(left, right):
    return jnp.dot(left, right, preferred_element_type=jnp.float32)


def left_product(left, right):
    return lax.dot_general(
        left, right, (((0,), (0,)), ((), ())), preferred_element_type=jnp.float32
    )


def right_product(left, right):
    return lax.dot_general(
        left, right, (((1,), (1,)), ((), ())), preferred_element_type=jnp.float32
    )


def norm_rows(values, gain):
    return values * lax.rsqrt(jnp.mean(values * values, axis=-1, keepdims=True) + epsilon) * gain


def exact_gelu(values):
    return jax.nn.gelu(values, approximate=False)


def square_rows(values):
    return jnp.sum(jnp.mean(values * values, axis=-1))


def layout(lengths, owners, row_count, per_image):
    caption_ends = jnp.cumsum(lengths)
    caption_starts = caption_ends - lengths
    row_index = jnp.arange(row_count, dtype=jnp.int32)
    inside = (row_index[:, None] >= caption_starts[None, :]) & (
        row_index[:, None] < caption_ends[None, :]
    )
    caption = jnp.sum(
        jnp.where(inside, jnp.arange(lengths.shape[0], dtype=jnp.int32)[None, :], 0), axis=1
    )
    text_image = jnp.sum(jnp.where(inside, owners[None, :], 0), axis=1)
    query_image = row_index // per_image
    query_allow = query_image[:, None] == query_image[None, :]
    own_caption = (caption[:, None] == caption[None, :]) & (
        row_index[None, :] <= row_index[:, None]
    )
    text_allow = jnp.concatenate([text_image[:, None] == query_image[None, :], own_caption], axis=1)
    return (query_allow, text_allow)


def attention_scores(query_rows, key_rows, allowed):
    batch_count, query_count, width_all = query_rows.shape
    query_heads = query_rows.reshape(batch_count, query_count, HEADS, HD)
    key_heads = key_rows.reshape(batch_count, key_rows.shape[1], HEADS, HD)
    scores = jnp.einsum(
        "bqhd,bkhd->bhqk", query_heads, key_heads, preferred_element_type=jnp.float32
    ) * HD ** (-0.5)
    if allowed is not None:
        scores = jnp.where(allowed[:, None], scores, masked_value)
    return (scores, query_heads, key_heads)


def attend(query_rows, key_rows, value_rows, allowed):
    scores, query_heads, key_heads = attention_scores(query_rows, key_rows, allowed)
    value_heads = value_rows.reshape(key_heads.shape)
    row_max = jnp.max(scores, axis=-1, keepdims=True)
    weights = jnp.exp(scores - row_max)
    denominator = jnp.sum(weights, axis=-1, keepdims=True)
    probability = to_half(weights / denominator)
    context = jnp.einsum(
        "bhqk,bkhd->bqhd", probability, value_heads, preferred_element_type=jnp.float32
    )
    return (context.reshape(query_rows.shape), (row_max + jnp.log(denominator))[..., 0])


def attend_back(query_rows, key_rows, value_rows, allowed, log_total, grad_context):
    scores, query_heads, key_heads = attention_scores(query_rows, key_rows, allowed)
    value_heads = value_rows.reshape(key_heads.shape)
    probability = jnp.exp(scores - log_total[..., None])
    grad_heads = grad_context.reshape(query_heads.shape)
    grad_prob = jnp.einsum(
        "bqhd,bkhd->bhqk", grad_heads, value_heads, preferred_element_type=jnp.float32
    )
    grad_value = jnp.einsum(
        "bhqk,bqhd->bkhd", to_half(probability), grad_heads, preferred_element_type=jnp.float32
    )
    grad_score = to_half(
        probability * (grad_prob - jnp.sum(grad_prob * probability, axis=-1, keepdims=True))
    )
    grad_query = jnp.einsum(
        "bhqk,bkhd->bqhd", grad_score, key_heads, preferred_element_type=jnp.float32
    ) * HD ** (-0.5)
    grad_key = jnp.einsum(
        "bhqk,bqhd->bkhd", grad_score, query_heads, preferred_element_type=jnp.float32
    ) * HD ** (-0.5)
    return (
        grad_query.reshape(query_rows.shape),
        grad_key.reshape(key_rows.shape),
        grad_value.reshape(value_rows.shape),
    )


def project_vision(feature_block, vision_weights):
    return to_half(
        jnp.einsum(
            "inv,kvd->kind", feature_block, vision_weights, preferred_element_type=jnp.float32
        )
    )


def vision_grad(feature_block, grad_pair):
    return jnp.einsum("inv,kind->kvd", feature_block, grad_pair, preferred_element_type=jnp.float32)


def adam_step(weight, gradient, first, second, factor, rate, decay):
    clipped = gradient * factor
    mean_new = beta_first * first + (1.0 - beta_first) * clipped
    square_new = beta_second * second + (1.0 - beta_second) * clipped * clipped
    corrected_mean = mean_new / (1.0 - beta_first**STEP)
    corrected_square = square_new / (1.0 - beta_second**STEP)
    fresh = weight - rate * (
        corrected_mean / (jnp.sqrt(corrected_square) + adam_floor) + decay * weight
    )
    return (fresh, mean_new, square_new)


MESH = pl.DeviceIdType.MESH
VMEM_LIMIT = 60 * 2**20


def coordinates():
    c = lax.axis_index("stream")
    d = lax.axis_index("dp")
    return c, d // 4, (d // 2) % 2, d % 2


def device(c, z, y, x):
    return (c, z * 4 + y * 2 + x)


def meet(c, z, y, x):
    barrier = pltpu.get_barrier_semaphore()
    others = [device(1 - c, z, y, x), device(c, z, 1 - y, x), device(c, z, y, 1 - x)]
    others += [device(c, (z + k) % 4, y, x) for k in (1, 2, 3)]
    for other in others:
        pl.semaphore_signal(barrier, inc=1, device_id=other, device_id_type=MESH)
    pl.semaphore_wait(barrier, len(others))


ORDERS = {
    ("late", 0): ("z", "y", "x"),
    ("late", 1): ("z", "x", "y"),
    ("early", 0): ("x", "z", "y"),
    ("early", 1): ("y", "z", "x"),
    ("right", 0): ("y", "z", "x"),
    ("right", 1): ("y", "z", "x"),
    ("vision", 0): ("x", "z", "y"),
    ("vision", 1): ("x", "z", "y"),
}


PARTS = 4


def wide(block):
    return block.astype(jnp.float32)


def nn(left, right):
    return lax.dot_general(
        left, right, (((1,), (0,)), ((), ())), preferred_element_type=jnp.float32
    )


def nt(left, right):
    return lax.dot_general(
        left, right, (((1,), (1,)), ((), ())), preferred_element_type=jnp.float32
    )


def tn(left, right):
    return lax.dot_general(
        left, right, (((0,), (0,)), ((), ())), preferred_element_type=jnp.float32
    )


def span(index, size):
    return pl.ds(pl.multiple_of(index * size, size), size)


def loop(count, step):
    def body(index, carry):
        step(index)
        return carry

    lax.fori_loop(0, count, body, 0)


def row_sum(values):
    return jnp.sum(values, axis=0, keepdims=True)


def norm_back(values, gain, grad):
    scale = lax.rsqrt(jnp.mean(values * values, axis=-1, keepdims=True) + epsilon)
    unit = values * scale
    grad_unit = grad * gain
    mean = jnp.mean(grad_unit * unit, axis=-1, keepdims=True)
    return scale * (grad_unit - unit * mean), row_sum(grad * unit)


def lane_masks(rows):
    lane = lax.broadcasted_iota(jnp.int32, (rows, 2 * HD), 1)
    left = jnp.where(lane < HD, 1.0, 0.0)
    return to_half(left), to_half(1.0 - left)


def head_pair(block, masks):
    return jnp.concatenate([block * masks[0], block * masks[1]], axis=0)


def pair_join(both):
    rows = both.shape[0] // 2
    lane = lax.broadcasted_iota(jnp.int32, (rows, 2 * HD), 1)
    return jnp.where(lane < HD, both[:rows], both[rows:])


def diagonal(full, rows):
    lane = lax.broadcasted_iota(jnp.int32, (rows, 2 * HD), 1)
    tiles = []
    for t in range(HEADS // 2):
        tile = full[:, t * 2 * HD : (t + 1) * 2 * HD]
        left = tile[2 * t * rows : (2 * t + 1) * rows]
        right = tile[(2 * t + 1) * rows : (2 * t + 2) * rows]
        tiles.append(jnp.where(lane < HD, left, right))
    return jnp.concatenate(tiles, axis=1)


def head_mask(rows, width):
    row = lax.broadcasted_iota(jnp.int32, (HEADS * rows, width), 0) // rows
    lane = lax.broadcasted_iota(jnp.int32, (HEADS * rows, width), 1) // HD
    return to_half(jnp.where(row == lane, 1.0, 0.0))


def caption_layout(lengths, owners, row_count):
    count = lengths.shape[1]
    size = wide(lengths)
    owner = wide(owners)
    sub = lax.broadcasted_iota(jnp.int32, (count, count), 0)
    lane = lax.broadcasted_iota(jnp.int32, (count, count), 1)
    starts = jnp.sum(jnp.where(lane < sub, size, 0.0), axis=1, keepdims=True)
    owner_down = jnp.sum(jnp.where(lane == sub, owner, 0.0), axis=1, keepdims=True)
    row = wide(lax.broadcasted_iota(jnp.int32, (count, row_count), 1))
    begun = starts <= row
    start = jnp.max(jnp.where(begun, starts, 0.0), axis=0, keepdims=True)
    image = jnp.max(jnp.where(begun, owner_down, 0.0), axis=0, keepdims=True)
    return start, image


def text_bias(rb, start, image, far_rows, window, bias):
    begin = jnp.maximum(rb - 1, 0) * 128
    far = lax.broadcasted_iota(jnp.int32, (far_rows, 128), 0) // NQ
    far_bias = jnp.where(wide(far) == image, 0.0, masked_value)
    key = lax.broadcasted_iota(jnp.int32, (window, 128), 0) + begin
    row = lax.broadcasted_iota(jnp.int32, (window, 128), 1) + rb * 128
    seen = (wide(key) >= start) & (key <= row)
    own_bias = jnp.where(seen, 0.0, masked_value)
    bias[0:far_rows] = jnp.concatenate([far_bias, far_bias], axis=1)
    bias[far_rows : far_rows + window] = jnp.concatenate([own_bias, own_bias], axis=1)


def query_bias(bias):
    key = lax.broadcasted_iota(jnp.int32, (128, 256), 0) // NQ
    row = (lax.broadcasted_iota(jnp.int32, (128, 256), 1) % 128) // NQ
    bias[0:128] = jnp.where(key == row, 0.0, masked_value)


def forward_kernel(
    first, vision, expand, reduce, gains,
    hidden_in, out_grad_in, features, lengths, owners,
    out_result, out_grad_cross, part_expand, part_reduce, gain_feed_out, stats,
    keep_first, keep_gains, keep_normed, keep_query, keep_key, keep_value, keep_far_key, keep_far_value,
    keep_context, keep_after_self, keep_cross_query, keep_cross_context, keep_vision, keep_images, total_self, total_cross,
    all_first, raw_vision, all_vision, all_expand, all_reduce, all_gains, gain_rows,
    hidden, out_grad, images, vision_pair, normed, query, key, value, far_key, far_value, context, after_self,
    cross_query, cross_context, after_cross, normed_feed, grad_feed, sum_branch, sum_normed, bias, mask,
    layout_rows, send_sem, recv_sem, local_sem,
):
    c, z, y, x = coordinates()
    own = {"z": z, "y": y, "x": x}
    row_count, width = hidden.shape
    image_count = total_cross.shape[0]
    padded = vision_pair.shape[0] // image_count
    feature_rows = features.shape[0] // (2 * image_count)
    feature_width = features.shape[1]
    part_rows = expand.shape[0] // PARTS
    far_rows, window = far_key.shape[0], 256
    cross_rows = image_count * NQ

    chunks = [(gains, lambda *at: all_gains.at[at], "late", False, 1)]
    for j, kind in enumerate(("late", "early", "late")):
        chunks.append((first.at[j], lambda *at, j=j: all_first.at[(c, j) + at], kind, True, 1))
    chunks.append((vision, lambda *at: raw_vision.at[(c,) + at], "late", True, 2))
    for p in range(PARTS):
        rows = pl.ds(p * part_rows, part_rows)
        kinds = ("early", "late") if p % 2 == 0 else ("late", "early")
        for (source, whole), kind in zip(((expand, all_expand), (reduce, all_reduce)), kinds):
            target = lambda *at, p=p, whole=whole: whole.at[(p,) + at]
            chunks.append((source.at[rows], target, kind, False, 2))
    count = len(chunks)
    events = [
        (number + stage * chunk[4], -stage, number)
        for number, chunk in enumerate(chunks)
        for stage in range(4)
    ]

    def remote(source, target, index, where):
        return pltpu.make_async_remote_copy(
            src_ref=source, dst_ref=target, send_sem=send_sem.at[index],
            recv_sem=recv_sem.at[index], device_id=where, device_id_type=MESH,
        )

    def sends(number, stage, core):
        source, target, kind = chunks[number][:3]
        order = ORDERS[kind, core]
        done, axis = order[:stage], order[stage]
        at = tuple(slice(None) if a in done else own[a] for a in "zyx")
        block = target(*at)
        here = source if stage == 0 else block
        base = (number * 3 + stage) * 3
        if axis == "z":
            return [
                remote(here, block, base + k - 1, device(c, (z + k) % 4, y, x)) for k in (1, 2, 3)
            ]
        where = device(c, z, 1 - y, x) if axis == "y" else device(c, z, y, 1 - x)
        return [remote(here, block, base, where)]

    def place(number):
        source, target = chunks[number][:2]
        return pltpu.make_async_copy(source, target(z, y, x), local_sem.at[number])

    pair = device(1 - c, z, y, x)

    def across(number):
        target = chunks[number][1]
        block = target(slice(None), slice(None), slice(None))
        return remote(block, block, count * 9 + number, pair)

    def tick_core(tick, core):
        for when, negative, number in sorted(events):
            stage = -negative
            if when != tick:
                continue
            if stage > 0:
                for copy in sends(number, stage - 1, core):
                    copy.wait_recv()
            if stage == 1:
                place(number).wait()
            if stage < 3:
                for copy in sends(number, stage, core):
                    copy.start()
                if stage == 0:
                    place(number).start()
            elif chunks[number][3]:
                across(number).start()

    def both(step):
        @pl.when(c == 0)
        def _():
            step(0)

        @pl.when(c == 1)
        def _():
            step(1)

    def tick(number):
        both(lambda core: tick_core(number, core))

    def sent(number):
        def step(core):
            for stage in range(3):
                for copy in sends(number, stage, core):
                    copy.wait_send()

        both(step)

    swap_base = count * 10
    swaps = {
        "key": (key, far_key),
        "value": (value, far_value),
        "query": (cross_query.at[pl.ds(cross_rows, cross_rows)], cross_query.at[pl.ds(0, cross_rows)]),
        "context": (cross_context.at[pl.ds(0, cross_rows)], cross_context.at[pl.ds(cross_rows, cross_rows)]),
    }

    def swap(name):
        source, target = swaps[name]
        return remote(source, target, swap_base + list(swaps).index(name), pair)

    local_base = count
    loads = [
        (hidden_in, hidden),
        (out_grad_in, out_grad),
    ]
    step_rows = 2 * image_count * 32
    whole_steps = feature_rows // 32
    half_rows = whole_steps // 2 * step_rows
    for begin, size in ((0, half_rows), (half_rows, features.shape[0] - half_rows)):
        staged = vision_pair.at[pl.ds(0, size), pl.ds(0, feature_width)]
        loads.append((features.at[pl.ds(begin, size)], staged))
    keeps = {
        "first": (all_first, keep_first),
        "gains": (gain_rows, keep_gains),
        "normed": (normed, keep_normed),
        "query": (query, keep_query),
        "key": (key, keep_key),
        "value": (value, keep_value),
        "far_key": (far_key, keep_far_key),
        "far_value": (far_value, keep_far_value),
        "context": (context, keep_context),
        "after_self": (after_self, keep_after_self),
        "cross_query": (cross_query.at[pl.ds(0, cross_rows)], keep_cross_query),
        "cross_context": (cross_context, keep_cross_context),
        "vision": (vision_pair, keep_vision),
        "images": (images, keep_images),
        "result": (sum_branch, out_result),
        "grad_cross": (sum_normed, out_grad_cross),
    }
    for p in range(PARTS):
        keeps["expand", p] = (all_expand.at[p], part_expand.at[p])
        keeps["reduce", p] = (all_reduce.at[p], part_reduce.at[p])

    def load(k):
        source, target = loads[k]
        return pltpu.make_async_copy(source, target, local_sem.at[local_base + k])

    def keep(name):
        source, target = keeps[name]
        index = local_base + len(loads) + list(keeps).index(name)
        return pltpu.make_async_copy(source, target, local_sem.at[index])

    def weight(plane, j):
        return all_first[plane, j].reshape(width, width)

    def gain(k):
        return gain_rows[pl.ds(k, 1), :]

    def stat(k, amount):
        row = pl.ds(c * 4 + k, 1)
        stats[row, :] = stats[row, :] + amount


    def start():
        stats[...] = jnp.zeros_like(stats)
        mask[...] = head_mask(NQ, width)
        first_row, image = caption_layout(lengths[...], owners[...], row_count)
        layout_rows[0:1] = first_row
        layout_rows[1:2] = image

    def read_gains():
        total = jnp.zeros(gain_rows.shape, jnp.float32)
        per = width // 16
        for k in range(16):
            lane = lax.broadcasted_iota(jnp.int32, (128, width), 0)
            column = lax.broadcasted_iota(jnp.int32, (128, width), 1)
            pick = to_half(jnp.where((column == lane + k * per) & (lane < per), 1.0, 0.0))
            total = total + nn(all_gains[k // 4, (k // 2) % 2, k % 2], pick)
        gain_rows[...] = total

    def self_in():
        def step(i):
            rows = span(i, 256)
            source = hidden[rows, :]
            stat(0, row_sum(source * source))
            part = to_half(norm_rows(source, gain(0)))
            normed[rows, :] = part
            query[rows, :] = to_half(nn(part, weight(0, 0))) * jnp.bfloat16(HD**-0.5)
            key[rows, :] = to_half(nn(part, weight(0, 1)))
            value[rows, :] = to_half(nn(part, weight(0, 2)))

        loop(row_count // 256, step)

    def attend_pair(rb, t, parts):
        lanes, rows = span(t, 128), span(rb, 128)
        queries = head_pair(query[rows, lanes], lane_masks(128))
        scores, most = [], None
        for keys, _, where, _ in parts:
            score = nt(keys, queries) + bias[where, :]
            scores.append(score)
            top = jnp.max(score, axis=0, keepdims=True)
            most = top if most is None else jnp.maximum(most, top)
        weights = [jnp.exp(score - most) for score in scores]
        total = sum(row_sum(part) for part in weights)
        inverse = 1.0 / total
        result = sum(
            tn(to_half(part * inverse), values) for part, (_, values, _, _) in zip(weights, parts)
        )
        context[rows, lanes] = to_half(pair_join(result))
        total_self[rb, t] = most + jnp.log(total)

    def self_query():
        query_bias(bias)

        def step(i):
            rb, t = i // 6, i % 6
            rows, lanes = span(rb, 128), span(t, 128)
            attend_pair(rb, t, [(key[rows, lanes], value[rows, lanes], pl.ds(0, 128), None)])

        loop(row_count // 128 * 6, step)

    def self_text():
        def outer(rb):
            rows = span(rb, 128)
            text_bias(rb, layout_rows[0:1, rows], layout_rows[1:2, rows], far_rows, window, bias)
            near = pl.ds(pl.multiple_of(jnp.maximum(rb - 1, 0) * 128, 128), window)

            def inner(t):
                lanes = span(t, 128)
                attend_pair(rb, t, [
                    (far_key[:, lanes], far_value[:, lanes], pl.ds(0, far_rows), None),
                    (key[near, lanes], value[near, lanes], pl.ds(far_rows, window), None),
                ])

            loop(6, inner)

        loop(row_count // 128, outer)

    def self_out():
        def step(i):
            rows = span(i, 256)
            branch = nn(context[rows, :], weight(1, 0))
            stat(1, row_sum(branch * branch))
            after_self[rows, :] = hidden[rows, :] + branch

        loop(row_count // 256, step)

    def cross_in():
        def step(i):
            rows = span(i, 256)
            part = to_half(norm_rows(after_self[rows, :], gain(1)))
            result = to_half(nn(part, weight(1, 2))) * jnp.bfloat16(HD**-0.5)
            cross_query[rows, :] = result

        loop(row_count // 256, step)

    def pack_vision():
        def step(i):
            plane, z_at, y_at = i // 8, (i // 2) % 4, i % 2
            left = wide(raw_vision[plane, z_at, y_at, 0])
            right = wide(raw_vision[plane, z_at, y_at, 1])
            size = 2 * left.shape[0]
            all_vision[plane, span(z_at * 2 + y_at, size), :] = to_half(
                jnp.concatenate([left, right], axis=0)
            )

        loop(16, step)

    def sort_rows(begin, rows, base):
        size = rows // (2 * image_count)
        block = max(size, 16)
        out = lax.broadcasted_iota(jnp.int32, (image_count * block, rows), 0)
        column = lax.broadcasted_iota(jnp.int32, (image_count * block, rows), 1)
        source = (out % block) * (2 * image_count) + c * image_count + out // block
        pick = to_half(jnp.where((column == source) & (out % block < size), 1.0, 0.0))
        sorted_rows = to_half(nn(pick, vision_pair[begin, 0:feature_width]))
        for j in range(image_count):
            where = pl.ds(pl.multiple_of(j * padded + base, 16), block)
            images[where, :] = sorted_rows[j * block : (j + 1) * block]

    def sort_images(part):
        def step(i):
            sort_rows(span(i, step_rows), step_rows, 32 * (i + part * (whole_steps // 2)))

        loop(whole_steps // 2, step)
        if part == 1:
            rest = feature_rows % 32 * 2 * image_count
            sort_rows(pl.ds(whole_steps // 2 * step_rows, rest), rest, whole_steps * 32)

    def project_images(begin, end):
        def step(i):
            rows = pl.ds(pl.multiple_of((i + begin) * padded, 16), padded)
            image = images[rows, :]
            vision_pair[rows, 0:width] = to_half(nn(image, all_vision[0]))
            vision_pair[rows, width : 2 * width] = to_half(nn(image, all_vision[1]))

        loop(end - begin, step)

    def cross_attend(begin, end):
        def step(i):
            i = i + begin
            rows = pl.ds(pl.multiple_of(i * padded, 16), padded)
            own_rows = span(i, NQ)
            part = cross_query[own_rows, :]
            queries = jnp.concatenate([part] * HEADS, axis=0) * mask[...]
            score = nt(vision_pair[rows, 0:width], queries)
            key_row = lax.broadcasted_iota(jnp.int32, score.shape, 0)
            score = jnp.where(key_row < feature_rows, score, masked_value)
            most = jnp.max(score, axis=0, keepdims=True)
            weights = jnp.exp(score - most)
            total = row_sum(weights)
            total_cross[i] = most + jnp.log(total)
            full = tn(to_half(weights * (1.0 / total)), vision_pair[rows, width : 2 * width])
            cross_context[own_rows, :] = to_half(diagonal(full, NQ))

        loop(end - begin, step)

    def cross_out():
        def step(i):
            rows = span(i, 256)
            after_cross[rows, :] = after_self[rows, :] + nn(cross_context[rows, :], weight(1, 1))

        loop(row_count // 256, step)

    def feed_in():
        def step(i):
            rows = span(i, 128)
            normed_feed[rows, :] = to_half(norm_rows(after_cross[rows, :], gain(2 + c)))
            grad_feed[rows, :] = to_half(out_grad[rows, :])
            sum_branch[rows, :] = jnp.zeros((128, width), jnp.float32)
            sum_normed[rows, :] = jnp.zeros((128, width), jnp.float32)

        loop(row_count // 128, step)

    def feed_part(p):
        size = all_expand.shape[2] * all_expand.shape[3] * part_rows

        def step(s):
            at = pl.ds(2 * s, 2)
            shape = (2,) + all_expand.shape[2:]
            up = all_expand[p, at].reshape(2 * size, width)
            down = all_reduce[p, at].reshape(2 * size, width)
            before = nt(normed_feed[...], up)
            share = 0.5 * (1.0 + lax.erf(before * (0.5**0.5)))
            density = jnp.exp(before * before * -0.5) * (0.5 / jnp.pi) ** 0.5
            active = to_half(before * share)
            slope = share + before * density
            sum_branch[...] += nn(active, down)
            grad_before = to_half(nt(grad_feed[...], down) * slope)
            sum_normed[...] += nn(grad_before, up)
            all_reduce[p, at] = to_half(tn(active, grad_feed[...])).reshape(shape)
            all_expand[p, at] = to_half(tn(grad_before, normed_feed[...])).reshape(shape)

        loop(2, step)

    def feed_out():
        gain_feed_out[...] = jnp.zeros_like(gain_feed_out)

        def step(i):
            rows = span(i, 128)
            source = after_cross[rows, :]
            branch = sum_branch[rows, :]
            result = source + branch
            stat(2, row_sum(branch * branch))
            stat(3, row_sum(result * result))
            sum_branch[rows, :] = result
            back, gain_part = norm_back(source, gain(2 + c), sum_normed[rows, :])
            gain_feed_out[0:1, :] = gain_feed_out[0:1, :] + gain_part
            sum_normed[rows, :] = out_grad[rows, :] + back

        loop(row_count // 128, step)

    for k in range(3):
        load(k).start()
    meet(c, z, y, x)
    tick(0)
    start()
    tick(1)
    tick(2)
    load(2).wait()
    sort_images(0)
    load(3).start()
    tick(3)
    read_gains()
    keep("gains").start()
    tick(4)
    load(3).wait()
    sort_images(1)
    keep("images").start()
    tick(5)
    tick(6)
    for number in (1, 2, 3):
        across(number).wait_recv()
    load(0).wait()
    self_in()
    for name in ("normed", "query", "key", "value"):
        keep(name).start()

    @pl.when(c == 0)
    def _():
        swap("key").start()
        swap("value").start()

    tick(7)
    keep("first").start()

    @pl.when(c == 0)
    def _():
        self_query()

    @pl.when(c == 1)
    def _():
        swap("key").wait_recv()
        swap("value").wait_recv()
        self_text()
        keep("far_key").start()
        keep("far_value").start()

    tick(8)
    keep("context").start()
    self_out()
    keep("after_self").start()

    @pl.when(c == 0)
    def _():
        cross_in()
        swap("query").start()

    tick(9)
    tick(10)
    across(4).wait_recv()
    pack_vision()
    project_images(0, image_count // 2)
    tick(11)
    project_images(image_count // 2, image_count)
    keep("vision").start()
    tick(12)

    @pl.when(c == 1)
    def _():
        swap("query").wait_recv()

    cross_attend(0, image_count)
    tick(13)

    @pl.when(c == 1)
    def _():
        swap("context").start()
        after_cross[...] = after_self[...]

    @pl.when(c == 0)
    def _():
        swap("context").wait_recv()
        cross_out()

    keep("cross_query").start()
    keep("cross_context").start()
    load(1).wait()
    feed_in()
    for p in range(PARTS):
        sent(5 + 2 * p)
        sent(6 + 2 * p)
        feed_part(p)
        keep(("expand", p)).start()
        keep(("reduce", p)).start()
        for number in {0: (14,), 1: (15, 16), 2: (17, 18)}.get(p, ()):
            tick(number)
    feed_out()
    keep("result").start()
    keep("grad_cross").start()
    for number in range(5):
        sent(number)
    for number in range(1, 5):
        across(number).wait_send()

    @pl.when(c == 0)
    def _():
        swap("key").wait_send()
        swap("value").wait_send()
        swap("query").wait_send()

    @pl.when(c == 1)
    def _():
        swap("context").wait_send()

    for name in keeps:
        if name in ("far_key", "far_value"):

            @pl.when(c == 1)
            def _(name=name):
                keep(name).wait()

        else:
            keep(name).wait()


def forward_all(first, vision, expand, reduce, gains, hidden, out_grad, features, lengths, owners):
    half, single = jnp.bfloat16, jnp.float32
    row_count, width = hidden.shape
    image_count, feature_rows, feature_width = features.shape
    image_count = image_count // 2
    features = features.transpose(1, 0, 2).reshape(-1, feature_width)
    padded = -(-feature_rows // 16) * 16
    cross_rows = image_count * NQ
    part_rows = expand.shape[0] // PARTS
    anywhere = pl.BlockSpec(memory_space=pl.ANY)
    vmem = pl.BlockSpec(memory_space=pltpu.VMEM)
    rows_half = jax.ShapeDtypeStruct((row_count, width), half)
    rows_single = jax.ShapeDtypeStruct((row_count, width), single)
    all_first = (2,) + first.shape[:1] + (4, 2, 2) + first.shape[1:]
    all_feed = (PARTS, 4, 2, 2, part_rows, width)
    gain_shape = (16, width)
    pair_shape = (image_count * padded, 2 * width)
    outs = {
        "result": (rows_single, anywhere),
        "grad_cross": (rows_single, anywhere),
        "part_expand": (jax.ShapeDtypeStruct(all_feed, half), anywhere),
        "part_reduce": (jax.ShapeDtypeStruct(all_feed, half), anywhere),
        "gain_feed": (jax.ShapeDtypeStruct((8, width), single), vmem),
        "stats": (jax.ShapeDtypeStruct((8, width), single), vmem),
        "first": (jax.ShapeDtypeStruct(all_first, half), anywhere),
        "gains": (jax.ShapeDtypeStruct(gain_shape, single), anywhere),
        "normed": (rows_half, anywhere),
        "query": (rows_half, anywhere),
        "key": (rows_half, anywhere),
        "value": (rows_half, anywhere),
        "far_key": (rows_half, anywhere),
        "far_value": (rows_half, anywhere),
        "context": (rows_half, anywhere),
        "after_self": (rows_single, anywhere),
        "cross_query": (jax.ShapeDtypeStruct((cross_rows, width), half), anywhere),
        "cross_context": (rows_half, anywhere),
        "vision": (jax.ShapeDtypeStruct(pair_shape, half), anywhere),
        "images": (jax.ShapeDtypeStruct((image_count * padded, feature_width), half), anywhere),
        "total_self": (jax.ShapeDtypeStruct((row_count // 128, HEADS // 2, 1, 256), single), vmem),
        "total_cross": (jax.ShapeDtypeStruct((image_count, 1, HEADS * NQ), single), vmem),
    }
    halves = (row_count, width)
    scratch = [
        pltpu.VMEM(all_first, half),
        pltpu.VMEM((2, 4, 2, 2) + vision.shape, half),
        pltpu.VMEM((2, feature_width, width), half),
        pltpu.VMEM(all_feed, half),
        pltpu.VMEM(all_feed, half),
        pltpu.VMEM((4, 2, 2) + gains.shape, half),
        pltpu.VMEM(gain_shape, single),
        pltpu.VMEM(halves, single),
        pltpu.VMEM(halves, single),
        pltpu.VMEM((image_count * padded, feature_width), half),
        pltpu.VMEM(pair_shape, half),
    ]
    scratch += [pltpu.VMEM(halves, half)] * 7
    scratch += [
        pltpu.VMEM(halves, single),
        pltpu.VMEM(halves, half),
        pltpu.VMEM(halves, half),
        pltpu.VMEM(halves, single),
        pltpu.VMEM(halves, half),
        pltpu.VMEM(halves, half),
        pltpu.VMEM(halves, single),
        pltpu.VMEM(halves, single),
        pltpu.VMEM((row_count + 256, 256), single),
        pltpu.VMEM((HEADS * NQ, width), half),
        pltpu.VMEM((8, row_count), single),
        pltpu.SemaphoreType.DMA((13 * 10 + 4,)),
        pltpu.SemaphoreType.DMA((13 * 10 + 4,)),
        pltpu.SemaphoreType.DMA((13 + 4 + 16 + 2 * PARTS,)),
    ]
    values = pl.pallas_call(
        forward_kernel,
        out_shape=[shape for shape, _ in outs.values()],
        in_specs=[anywhere] * 8 + [vmem] * 2,
        out_specs=[spec for _, spec in outs.values()],
        scratch_shapes=scratch,
        compiler_params=pltpu.CompilerParams(
            collective_id=2, has_side_effects=True, vmem_limit_bytes=VMEM_LIMIT
        ),
        name="forward_layer",
    )(first, vision, expand, reduce, gains, hidden, out_grad, features, lengths, owners)
    return dict(zip(outs, values))


def add_events(chunks):
    return sorted(
        (number + stage * chunk["gap"] + chunk["begin"], -stage, number)
        for number, chunk in enumerate(chunks)
        for stage in range(4)
    )


def scatter_engine(chunks, send_sem, recv_sem):
    c, z, y, x = coordinates()
    own = {"z": z, "y": y, "x": x}
    events = add_events(chunks)

    def remote(source, target, index, where):
        return pltpu.make_async_remote_copy(
            src_ref=source, dst_ref=target, send_sem=send_sem.at[index],
            recv_sem=recv_sem.at[index], device_id=where, device_id_type=MESH,
        )

    def sends(number, stage, core):
        chunk = chunks[number]
        held, got = chunk["held"], chunk["got"][stage]
        order = ORDERS[chunk["kind"], core][::-1]
        done, axis = order[:stage], order[stage]
        base = (number * 3 + stage) * 3

        def block(there):
            return held.at[
                tuple(there if a == axis else own[a] if a in done else slice(None) for a in "zyx")
            ]

        if axis == "z":
            return [
                remote(
                    block((z + k) % 4), got.at[k - 1], base + k - 1, device(c, (z + k) % 4, y, x)
                )
                for k in (1, 2, 3)
            ]
        where = device(c, z, 1 - y, x) if axis == "y" else device(c, z, y, 1 - x)
        return [remote(block(1 - own[axis]), got, base, where)]

    def absorb(number, stage, core):
        chunk = chunks[number]
        held, got = chunk["held"], chunk["got"][stage]
        order = ORDERS[chunk["kind"], core][::-1]
        done, axis = order[: stage + 1], order[stage]
        free = [a for a in "zyx" if a not in done]
        sizes = [4 if a == "z" else 2 for a in free]
        steps = 1
        for size in sizes:
            steps *= size

        def step(i):
            index = {}
            for a, size in reversed(list(zip(free, sizes))):
                index[a] = i % size
                i = i // size
            at = tuple(index[a] if a in index else own[a] for a in "zyx")
            inner = tuple(index[a] for a in free)
            value = wide(held[at])
            if axis == "z":
                for k in range(3):
                    value = value + wide(got[(k,) + inner])
            else:
                value = value + wide(got[inner] if inner else got[...])
            if stage == 2:
                chunk["total"][...] = value
            else:
                held[at] = to_half(value)

        if steps == 1:
            step(0)
        else:
            loop(steps, step)

    def tick_core(now, core):
        for when, negative, number in events:
            stage = -negative
            if when != now:
                continue
            if stage == 0:
                chunks[number]["ready"]()
            else:
                for copy in sends(number, stage - 1, core):
                    copy.wait_recv()
                absorb(number, stage - 1, core)
            if stage < 3:
                for copy in sends(number, stage, core):
                    copy.start()

    def each_core(step):
        @pl.when(c == 0)
        def _():
            step(0)

        @pl.when(c == 1)
        def _():
            step(1)

    def tick(now):
        each_core(lambda core: tick_core(now, core))

    def wait_sent():
        def step(core):
            for number in range(len(chunks)):
                for stage in range(3):
                    for copy in sends(number, stage, core):
                        copy.wait_send()

        each_core(step)

    return tick, wait_sent, remote, events[-1][0]


def got_shapes(kind, rows, width):
    if kind == "late":
        return [(4, 2, rows, width), (4, rows, width), (3, rows, width)]
    return [(4, 2, rows, width), (3, 2, rows, width), (rows, width)]


FEED_KINDS = ("late", "early", "late", "late", "early", "late", "late", "early")


def backward_kernel(
    feature_rows,
    part_expand, part_reduce, grad_cross_in, hidden_in, after_self_in, first_in, gains_in,
    normed_in, query_in, key_in, value_in, far_key_in, far_value_in, context_in,
    cross_query_in, cross_context_in, vision_in, images_in, lengths, owners, total_self, total_cross, gain_feed,
    hidden_grad_out, part_first, part_vision, sum_expand, sum_reduce, gain_parts,
    held_expand, held_reduce, got_l0, got_l1, got_l2, got_e0, got_e1, got_e2,
    first, pair, images, grad_vision, cross_context, after_self, hidden, grad_after, grad_normed, gain_rows,
    cross_query, grad_context, grad_query, far_grad, bias, mask, sum_far_key, sum_far_value, sum_key, sum_value,
    layout_rows, send_sem, recv_sem, local_sem,
):
    c, z, y, x = coordinates()
    row_count, width = hidden.shape
    image_count = total_cross.shape[0]
    padded = pair.shape[0] // image_count
    feature_width = images.shape[1]
    cross_rows = image_count * NQ
    part_rows = held_expand.shape[-2]
    far_rows, window = row_count, 256
    scale = HD**-0.5
    other = device(1 - c, z, y, x)

    def shelf(buffer, number):
        at = pl.ds(number // 2 * row_count, row_count), pl.ds(number % 2 * width, width)
        return buffer.at[at[0], at[1]]

    names = ("normed", "query", "key", "value", "far_key", "far_value", "context", "grad_context")
    normed, query, key, value, far_key, far_value, context, grad_context_self = (
        shelf(pair, number) for number in range(len(names))
    )
    own_query, own_key, own_value = (shelf(images, 2 * number) for number in range(3))

    loads = {
        "expand": (part_expand, held_expand),
        "reduce": (part_reduce, held_reduce),
        "grad_cross": (grad_cross_in, grad_after),
        "first": (first_in, first),
        "gains": (gains_in, gain_rows),
        "cross_context": (cross_context_in, cross_context),
        "cross_query": (cross_query_in, cross_query),
        "vision": (vision_in, pair),
        "images": (images_in, images),
        "after_self": (after_self_in, after_self),
        "hidden": (hidden_in, hidden),
        "normed": (normed_in, normed),
        "query": (query_in, query),
        "key": (key_in, key),
        "value": (value_in, value),
        "far_key": (far_key_in, far_key),
        "far_value": (far_value_in, far_value),
        "context": (context_in, context),
        "out_hidden": (grad_after, hidden_grad_out),
        "out_first": (first, part_first),
        "out_vision": (grad_vision, part_vision),
    }

    def local(name):
        source, target = loads[name]
        return pltpu.make_async_copy(source, target, local_sem.at[list(loads).index(name)])

    chunks, slots = [], {"late": 0, "early": 0}
    for number, kind in enumerate(FEED_KINDS):
        p = number // 2
        held, total, name = (
            (held_expand, sum_expand, "expand"), (held_reduce, sum_reduce, "reduce")
        )[number % 2]
        slot = slots[kind]
        slots[kind] += 1
        got = (got_l0, got_l1, got_l2) if kind == "late" else (got_e0, got_e1, got_e2)
        chunks.append({
            "held": held.at[p], "got": [part.at[slot] for part in got], "kind": kind,
            "total": total.at[pl.ds(p * part_rows, part_rows)], "gap": 2, "begin": 0,
            "ready": (lambda name=name: local(name).wait()) if p == 0 else (lambda: None),
        })
    tick, wait_sent, remote, last = scatter_engine(chunks, send_sem, recv_sem)

    swap_base = len(chunks) * 9
    own_rows, other_rows = pl.ds(0, cross_rows), pl.ds(cross_rows, cross_rows)
    swaps = {
        "context": (grad_context.at[other_rows], grad_context.at[own_rows]),
        "query": (grad_query.at[own_rows], grad_query.at[other_rows]),
        "far_key": (far_grad.at[0], far_grad.at[0]),
        "far_value": (far_grad.at[1], far_grad.at[1]),
    }

    def swap(name):
        source, target = swaps[name]
        return remote(source, target, swap_base + list(swaps).index(name), other)

    def weight(plane, j):
        return first[plane, j].reshape(width, width)

    def gain(k):
        return gain_rows[pl.ds(k, 1), :]

    def store_weight_grad(plane, j, value):
        first[plane, j] = to_half(value).reshape(first.shape[2:])


    def start():
        gain_parts[...] = jnp.zeros_like(gain_parts)
        gain_parts[pl.ds(2 + c, 1), :] = gain_feed[0:1, :]
        mask[...] = head_mask(NQ, width)
        first_row, image = caption_layout(lengths[...], owners[...], row_count)
        layout_rows[0:1] = first_row
        layout_rows[1:2] = image

    def cross_out_back():
        def step(i):
            rows = span(i, 256)
            part = to_half(grad_after[rows, :])
            grad_query[rows, :] = part
            grad_context[rows, :] = to_half(nt(part, weight(1, 1)))

        loop(row_count // 256, step)
        store_weight_grad(1, 1, tn(cross_context[...], grad_query[...]))
        swap("context").start()

    def cross_back(begin, end):
        def step(i):
            i = i + begin
            rows = pl.ds(pl.multiple_of(i * padded, 16), padded)
            at = span(i, NQ)
            queries = jnp.concatenate([cross_query[at, :]] * HEADS, axis=0) * mask[...]
            grads = jnp.concatenate([grad_context[at, :]] * HEADS, axis=0) * mask[...]
            keys, values = pair[rows, 0:width], pair[rows, width : 2 * width]
            score = nt(keys, queries)
            key_row = lax.broadcasted_iota(jnp.int32, score.shape, 0)
            seen = key_row < feature_rows
            probability = jnp.exp(jnp.where(seen, score, masked_value) - total_cross[i])
            grad_prob = nt(values, grads)
            inner = row_sum(grad_prob * probability)
            grad_score = to_half(probability * (grad_prob - inner))
            full = tn(grad_score, keys)
            pair[rows, 0:width] = to_half(nn(grad_score, queries))
            pair[rows, width : 2 * width] = to_half(nn(to_half(probability), grads))
            grad_query[at, :] = to_half(diagonal(full, NQ) * scale)

        loop(end - begin, step)


    def vision_back(begin, end):
        def step(i):
            i = i + begin
            lanes = span(i, 128)
            both = to_half(tn(images[:, lanes], pair[...]))
            grad_vision[0, lanes, :] = both[:, 0:width]
            grad_vision[1, lanes, :] = both[:, width : 2 * width]

        loop(end - begin, step)

    def cross_in_back():
        def step(i):
            rows = span(i, 128)
            source = after_self[rows, :]
            grad = nt(grad_query[rows, :], weight(1, 2))
            back, part = norm_back(source, gain(1), grad)
            gain_parts[1:2, :] = gain_parts[1:2, :] + part
            grad_after[rows, :] = grad_after[rows, :] + back
            grad_context[rows, :] = to_half(norm_rows(source, gain(1)))

        loop(row_count // 128, step)
        store_weight_grad(1, 2, tn(grad_context[...], grad_query[...]))

    def self_out_back():
        def step(i):
            rows = span(i, 256)
            part = to_half(grad_after[rows, :])
            grad_context[rows, :] = part
            grad_context_self[rows, :] = to_half(nt(part, weight(1, 0)))

        loop(row_count // 256, step)
        store_weight_grad(1, 0, tn(context[...], grad_context[...]))

    def attend_pair_back(rb, t, parts):
        rows, lanes = span(rb, 128), span(t, 128)
        masks = lane_masks(128)
        queries = head_pair(query[rows, lanes], masks)
        grads = head_pair(grad_context_self[rows, lanes], masks)
        kept, inner = [], 0.0
        for keys, values, where in parts:
            score = nt(keys, queries) + wide(where)
            probability = jnp.exp(score - total_self[rb, t])
            grad_prob = nt(values, grads)
            inner = inner + row_sum(grad_prob * probability)
            kept.append((probability, grad_prob))
        result, back = [], 0.0
        for (keys, values, _), (probability, grad_prob) in zip(parts, kept):
            grad_score = to_half(probability * (grad_prob - inner))
            result.append((nn(grad_score, queries), nn(to_half(probability), grads)))
            back = back + tn(grad_score, keys)
        own_query[rows, lanes] = to_half(pair_join(back) * scale)
        return result

    def self_query_back(begin, end):
        def step(i):
            rb, t = i // 6, i % 6
            rows, lanes = span(rb, 128), span(t, 128)
            parts = [(key[rows, lanes], value[rows, lanes], bias[0, 0:128])]
            ((grad_key, grad_value),) = attend_pair_back(rb, t, parts)
            own_key[rows, lanes] = to_half(grad_key)
            own_value[rows, lanes] = to_half(grad_value)

        blocks = row_count // 128

        def shifted_step(i):
            step(i + begin * blocks)

        loop((end - begin) * blocks, shifted_step)

    def text_biases():
        def step(rb):
            rows = span(rb, 128)
            start_row, image = layout_rows[0:1, rows], layout_rows[1:2, rows]
            begin = jnp.maximum(rb - 1, 0) * 128
            far = lax.broadcasted_iota(jnp.int32, (far_rows, 128), 0) // NQ
            far_bias = jnp.where(wide(far) == image, 0.0, masked_value)
            key_row = lax.broadcasted_iota(jnp.int32, (window, 128), 0) + begin
            row = lax.broadcasted_iota(jnp.int32, (window, 128), 1) + rb * 128
            seen = (wide(key_row) >= start_row) & (key_row <= row)
            own_bias = jnp.where(seen, 0.0, masked_value)
            bias[rb, 0:far_rows] = to_half(jnp.concatenate([far_bias, far_bias], axis=1))
            bias[rb, far_rows : far_rows + window] = to_half(
                jnp.concatenate([own_bias, own_bias], axis=1)
            )

        loop(row_count // 128, step)

    def query_biases():
        key_row = lax.broadcasted_iota(jnp.int32, (128, 256), 0) // NQ
        row = (lax.broadcasted_iota(jnp.int32, (128, 256), 1) % 128) // NQ
        bias[0, 0:128] = to_half(jnp.where(key_row == row, 0.0, masked_value))

    def self_text_back(begin, end):
        def outer(t):
            t = t + begin
            lanes = span(t, 128)
            for total in (sum_far_key, sum_far_value, sum_key, sum_value):
                total[...] = jnp.zeros_like(total)

            def inner(rb):
                near = pl.ds(pl.multiple_of(jnp.maximum(rb - 1, 0) * 128, 128), window)
                parts = [
                    (far_key[:, lanes], far_value[:, lanes], bias[rb, 0:far_rows]),
                    (key[near, lanes], value[near, lanes], bias[rb, far_rows : far_rows + window]),
                ]
                far_part, near_part = attend_pair_back(rb, t, parts)
                sum_far_key[...] += far_part[0]
                sum_far_value[...] += far_part[1]
                sum_key[near, :] = sum_key[near, :] + near_part[0]
                sum_value[near, :] = sum_value[near, :] + near_part[1]

            loop(row_count // 128, inner)
            far_grad[0, :, lanes] = to_half(sum_far_key[...])
            far_grad[1, :, lanes] = to_half(sum_far_value[...])
            own_key[:, lanes] = to_half(sum_key[...])
            own_value[:, lanes] = to_half(sum_value[...])

        loop(end - begin, outer)

    def self_in_back():
        def step(i):
            rows = span(i, 256)
            grad = nt(own_query[rows, :], weight(0, 0))
            grad = grad + nt(own_key[rows, :], weight(0, 1))
            grad = grad + nt(own_value[rows, :], weight(0, 2))
            grad_normed[rows, :] = grad

        loop(row_count // 256, step)

    def far_in_back():
        def step(i):
            rows = span(i, 256)
            grad = nt(far_grad[0, rows, :], weight(0, 1)) + nt(far_grad[1, rows, :], weight(0, 2))
            grad_normed[rows, :] = grad_normed[rows, :] + grad

        loop(row_count // 256, step)

    def project_back(far):
        rows = normed[...]
        store_weight_grad(0, 0, tn(rows, own_query[...]))
        grad_key, grad_value = tn(rows, own_key[...]), tn(rows, own_value[...])
        if far:
            grad_key = grad_key + tn(rows, far_grad[0])
            grad_value = grad_value + tn(rows, far_grad[1])
        store_weight_grad(0, 1, grad_key)
        store_weight_grad(0, 2, grad_value)

    def hidden_back():
        def step(i):
            rows = span(i, 128)
            back, part = norm_back(hidden[rows, :], gain(0), grad_normed[rows, :])
            gain_parts[0:1, :] = gain_parts[0:1, :] + part
            grad_after[rows, :] = grad_after[rows, :] + back

        loop(row_count // 128, step)

    for name in ("expand", "reduce", "grad_cross", "first", "cross_context", "vision", "cross_query",
                 "images", "after_self", "gains", "hidden"):
        local(name).start()
    meet(c, z, y, x)
    tick(0)
    start()
    local("grad_cross").wait()
    local("first").wait()
    local("cross_context").wait()

    @pl.when(c == 0)
    def _():
        cross_out_back()

    @pl.when(c == 1)
    def _():
        first[1, 1] = jnp.zeros(first.shape[2:], jnp.bfloat16)
        first[1, 2] = jnp.zeros(first.shape[2:], jnp.bfloat16)
        swap("context").wait_recv()

    tick(1)
    local("vision").wait()
    local("cross_query").wait()
    quarter = image_count // 4
    for k in range(4):
        cross_back(k * quarter, (k + 1) * quarter)
        tick(2 + k)

    @pl.when(c == 1)
    def _():
        swap("query").start()

    local("images").wait()
    tiles = feature_width // 128
    vision_back(0, tiles // 2)
    tick(6)
    vision_back(tiles // 2, tiles)
    local("out_vision").start()
    for name in names[:-1]:
        local(name).start()
    tick(7)
    local("after_self").wait()
    local("gains").wait()

    @pl.when(c == 0)
    def _():
        swap("query").wait_recv()
        swap("context").wait_send()
        cross_in_back()

    for name in names[:-1]:
        local(name).wait()
    self_out_back()
    tick(8)

    @pl.when(c == 0)
    def _():
        query_biases()
        self_query_back(0, 6)

    @pl.when(c == 1)
    def _():
        text_biases()
        self_text_back(0, 2)

    tick(9)

    @pl.when(c == 1)
    def _():
        self_text_back(2, 4)

    tick(10)

    @pl.when(c == 1)
    def _():
        self_text_back(4, 6)
        swap("far_key").start()
        swap("far_value").start()

    tick(11)
    self_in_back()
    tick(12)

    @pl.when(c == 0)
    def _():
        swap("far_key").wait_recv()
        swap("far_value").wait_recv()
        far_in_back()
        project_back(True)

    @pl.when(c == 1)
    def _():
        project_back(False)

    tick(13)
    local("out_first").start()
    local("hidden").wait()
    hidden_back()
    local("out_hidden").start()
    assert last == 13
    wait_sent()

    @pl.when(c == 1)
    def _():
        swap("query").wait_send()
        swap("far_key").wait_send()
        swap("far_value").wait_send()

    for name in ("out_hidden", "out_first", "out_vision"):
        local(name).wait()


def backward_all(kept, hidden, lengths, owners, feature_rows):
    half, single = jnp.bfloat16, jnp.float32
    row_count, width = hidden.shape
    feature_width = kept["images"].shape[1]
    parts = kept["part_expand"].shape
    part_rows = parts[-2]
    cross_rows = kept["cross_query"].shape[0]
    anywhere = pl.BlockSpec(memory_space=pl.ANY)
    vmem = pl.BlockSpec(memory_space=pltpu.VMEM)
    rows_half, rows_single = pltpu.VMEM((row_count, width), half), pltpu.VMEM((row_count, width), single)
    outs = {
        "hidden_grad": (jax.ShapeDtypeStruct((row_count, width), single), anywhere),
        "first": (jax.ShapeDtypeStruct(kept["first"].shape, half), anywhere),
        "vision": (jax.ShapeDtypeStruct((2, feature_width, width), half), anywhere),
        "expand": (jax.ShapeDtypeStruct((PARTS * part_rows, width), single), vmem),
        "reduce": (jax.ShapeDtypeStruct((PARTS * part_rows, width), single), vmem),
        "gains": (jax.ShapeDtypeStruct((8, width), single), vmem),
    }
    scratch = [pltpu.VMEM(parts, half)] * 2
    for kind in ("late", "early"):
        number = FEED_KINDS.count(kind)
        scratch += [
            pltpu.VMEM((number,) + shape, half) for shape in got_shapes(kind, part_rows, width)
        ]
    scratch += [
        pltpu.VMEM(kept["first"].shape, half),
        pltpu.VMEM(kept["vision"].shape, half),
        pltpu.VMEM(kept["images"].shape, half),
        pltpu.VMEM((2, feature_width, width), half),
        rows_half,
        rows_single,
        rows_single,
        rows_single,
        rows_single,
        pltpu.VMEM((16, width), single),
        pltpu.VMEM((cross_rows, width), half),
        rows_half,
        rows_half,
        pltpu.VMEM((2, row_count, width), half),
        pltpu.VMEM((row_count // 128, row_count + 256, 256), half),
        pltpu.VMEM((HEADS * NQ, width), half),
    ]
    scratch += [pltpu.VMEM((row_count, 128), single)] * 4
    scratch += [
        pltpu.VMEM((8, row_count), single),
        pltpu.SemaphoreType.DMA((len(FEED_KINDS) * 9 + 4,)),
        pltpu.SemaphoreType.DMA((len(FEED_KINDS) * 9 + 4,)),
        pltpu.SemaphoreType.DMA((21,)),
    ]
    order = ("part_expand", "part_reduce", "grad_cross", None, "after_self", "first", "gains", "normed",
             "query", "key", "value", "far_key", "far_value", "context", "cross_query", "cross_context",
             "vision", "images")
    values = pl.pallas_call(
        functools.partial(backward_kernel, feature_rows),
        out_shape=[shape for shape, _ in outs.values()],
        in_specs=[anywhere] * len(order) + [vmem] * 5,
        out_specs=[spec for _, spec in outs.values()],
        scratch_shapes=scratch,
        compiler_params=pltpu.CompilerParams(
            collective_id=3, has_side_effects=True, vmem_limit_bytes=VMEM_LIMIT
        ),
        name="backward_layer",
    )(
        *[hidden if name is None else kept[name] for name in order],
        lengths, owners, kept["total_self"], kept["total_cross"], kept["gain_feed"],
    )
    return dict(zip(outs, values))


SHARED_KINDS = ("late", "early", "late", "late")


def reduce_kernel(
    part_first, part_vision, sum_expand, sum_reduce, part_gains, part_stats,
    sum_first, sum_vision, sum_gains, totals,
    held_first, held_vision, own_vision, pair_first, pair_vision,
    got_l0, got_l1, got_l2, got_e0, got_e1, got_e2, got_v0, got_v1, got_v2,
    gains_now, gains_got, gains_z, stats_now, stats_got, stats_z, send_sem, recv_sem, local_sem,
):
    c, z, y, x = coordinates()
    other = device(1 - c, z, y, x)
    rows_vision = held_vision.shape[-2]
    chunks, slots = [], {"late": 0, "early": 0}

    def load(k):
        if k == 3:
            return pltpu.make_async_copy(part_vision.at[c], own_vision, local_sem.at[k])
        return pltpu.make_async_copy(part_first.at[c, k], held_first.at[k], local_sem.at[k])

    def pair_copy(k):
        if k == 3:
            return remote(part_vision.at[1 - c], pair_vision, pair_base + k, other)
        return remote(part_first.at[1 - c, k], pair_first.at[k], pair_base + k, other)

    def ready_first(j):
        load(j).wait()
        pair_copy(j).wait()

        def step(i):
            at = (j, i // 4, (i // 2) % 2, i % 2)
            held_first[at] = to_half(wide(held_first[at]) + wide(pair_first[at]))

        loop(16, step)

    def ready_vision():
        load(3).wait()
        pair_copy(3).wait()

        def step(i):
            rows = span(i, 2 * rows_vision)
            value = wide(own_vision[rows, :]) + wide(pair_vision[rows, :])
            held_vision[i // 2, i % 2, 0] = to_half(value[:rows_vision])
            held_vision[i // 2, i % 2, 1] = to_half(value[rows_vision:])

        loop(8, step)

    for j in range(3):
        kind = SHARED_KINDS[j]
        slot = slots[kind]
        slots[kind] += 1
        got = (got_l0, got_l1, got_l2) if kind == "late" else (got_e0, got_e1, got_e2)
        chunks.append({
            "held": held_first.at[j], "got": [part.at[slot] for part in got], "kind": kind,
            "total": sum_first.at[c, j], "gap": 2, "begin": 0, "ready": lambda j=j: ready_first(j),
        })
    chunks.append({
        "held": held_vision, "got": [got_v0, got_v1, got_v2], "kind": SHARED_KINDS[3],
        "total": sum_vision.at[c], "gap": 2, "begin": 0, "ready": ready_vision,
    })
    tick, wait_sent, remote, last = scatter_engine(chunks, send_sem, recv_sem)
    pair_base = len(chunks) * 9
    gains_base, stats_base = pair_base + 4, pair_base + 10

    def small(stage, now, got, got_z, base):
        if stage < 3:
            where = (other, device(c, z, 1 - y, x), device(c, z, y, 1 - x))[stage]
            return [remote(now.at[stage], got.at[stage], base + stage, where)]
        return [
            remote(now.at[3], got_z.at[z], base + 2 + k, device(c, (z + k) % 4, y, x))
            for k in (1, 2, 3)
        ]

    def small_step(stage, now, got, got_z, base):
        if stage > 0:
            for copy in small(stage - 1, now, got, got_z, base):
                copy.wait()
            if stage < 4:
                now[stage] = now[stage - 1] + got[stage - 1]
            else:
                got_z[z] = now[3]
                now[4] = (got_z[0] + got_z[1]) + (got_z[2] + got_z[3])
        if stage < 4:
            for copy in small(stage, now, got, got_z, base):
                copy.start()

    def folded(values):
        total = values[:, 0:128]
        for k in range(1, values.shape[1] // 128):
            total = total + values[:, k * 128 : (k + 1) * 128]
        return total

    def squares(block):
        return jnp.sum((block * block).reshape(-1, 8, block.shape[1]), axis=0)

    for k in range(4):
        load(k).start()
    meet(c, z, y, x)
    for k in range(4):
        pair_copy(k).start()
    gains_now[0] = part_gains[...]
    for now in range(last + 1):
        if now < 5:
            small_step(now, gains_now, gains_got, gains_z, gains_base)
        tick(now)
    back = [
        remote(sum_first.at[c], sum_first.at[c], stats_base + 6, other),
        remote(sum_vision.at[c], sum_vision.at[c], stats_base + 7, other),
    ]
    for copy in back:
        copy.start()
    gains = gains_now[4]
    sum_gains[...] = gains
    mass = jnp.where((c == 0) & (z + y + x == 0), 1.0, 0.0) * (gains * gains)
    for j in range(3):
        mass = mass + squares(sum_first[c, j])
    mass = mass + squares(sum_vision[c])
    mass = mass + squares(sum_expand[...]) + squares(sum_reduce[...])
    stats_now[0, 0:8] = folded(mass)
    stats_now[0, 8:16] = folded(part_stats[...])
    for stage in range(5):
        small_step(stage, stats_now, stats_got, stats_z, stats_base)
    totals[...] = stats_now[4]
    for copy in back:
        copy.wait()
    wait_sent()


def reduce_all(part_first, part_vision, sum_expand, sum_reduce, part_gains, part_stats):
    half, single = jnp.bfloat16, jnp.float32
    rows_first, width = part_first.shape[-2:]
    feature_width = part_vision.shape[1]
    rows_vision = feature_width // 16
    anywhere = pl.BlockSpec(memory_space=pl.ANY)
    vmem = pl.BlockSpec(memory_space=pltpu.VMEM)
    scratch = [
        pltpu.VMEM(part_first.shape[1:], half),
        pltpu.VMEM((4, 2, 2, rows_vision, width), half),
        pltpu.VMEM((feature_width, width), half),
        pltpu.VMEM(part_first.shape[1:], half),
        pltpu.VMEM((feature_width, width), half),
    ]
    for kind in ("late", "early"):
        number = SHARED_KINDS[:3].count(kind)
        scratch += [
            pltpu.VMEM((number,) + shape, half) for shape in got_shapes(kind, rows_first, width)
        ]
    scratch += [pltpu.VMEM(shape, half) for shape in got_shapes(SHARED_KINDS[3], rows_vision, width)]
    for shape in (part_gains.shape, (16, 128)):
        scratch += [pltpu.VMEM((number,) + shape, single) for number in (5, 3, 4)]
    scratch += [
        pltpu.SemaphoreType.DMA((4 * 9 + 4 + 14,)),
        pltpu.SemaphoreType.DMA((4 * 9 + 4 + 14,)),
        pltpu.SemaphoreType.DMA((4,)),
    ]
    return pl.pallas_call(
        reduce_kernel,
        out_shape=[
            jax.ShapeDtypeStruct((2, 3, rows_first, width), single),
            jax.ShapeDtypeStruct((2, rows_vision, width), single),
            jax.ShapeDtypeStruct(part_gains.shape, single),
            jax.ShapeDtypeStruct((16, 128), single),
        ],
        in_specs=[anywhere] * 2 + [vmem] * 4,
        out_specs=[vmem] * 4,
        scratch_shapes=scratch,
        compiler_params=pltpu.CompilerParams(
            collective_id=4, has_side_effects=True, vmem_limit_bytes=VMEM_LIMIT
        ),
        name="reduce_grads",
    )(part_first, part_vision, sum_expand, sum_reduce, part_gains, part_stats)


def general_grads(
    hidden,
    features,
    caption_lengths,
    caption_image,
    out_grad,
    attn_project,
    attn_output,
    cross_query,
    cross_vision,
    feed_expand,
    feed_reduce,
    norm_gains,
):
    stream = lax.axis_index("stream")
    full_project, full_output, full_query, full_vision, full_expand, full_reduce, full_gains = (
        lax.all_gather(to_half(attn_project), "dp", axis=1, tiled=True),
        lax.all_gather(to_half(attn_output), "dp", axis=1, tiled=True),
        lax.all_gather(to_half(cross_query), "dp", axis=0, tiled=True),
        lax.all_gather(to_half(cross_vision), "dp", axis=1, tiled=True),
        lax.all_gather(to_half(feed_expand), "dp", axis=1, tiled=True),
        lax.all_gather(to_half(feed_reduce), "dp", axis=1, tiled=True),
        lax.all_gather(to_half(norm_gains), "dp", axis=1, tiled=True),
    )
    gain_rows = full_gains.astype(jnp.float32)
    gain_self = gain_rows[0]
    gain_cross = gain_rows[1]
    gain_feed = lax.dynamic_index_in_dim(gain_rows, 2 + stream, 0, keepdims=False)
    source = hidden[0]
    row_count = source.shape[0]
    feature_width = source.shape[1]
    image_count = features.shape[0]
    query_allow, text_allow = layout(caption_lengths[0], caption_image[0], row_count, NQ)
    normed_self = to_half(norm_rows(source, gain_self))
    query_half = to_half(product(normed_self, full_project[0]))
    key_half = to_half(product(normed_self, full_project[1]))
    value_half = to_half(product(normed_self, full_project[2]))
    empty_half = jnp.zeros((row_count, feature_width), jnp.bfloat16)
    far_key, far_value = shifted((key_half, value_half), "stream", 1)
    text_keys = jnp.concatenate([far_key, key_half], axis=0)
    text_values = jnp.concatenate([far_value, value_half], axis=0)

    def self_query():
        return attend(query_half[None], key_half[None], value_half[None], query_allow[None])

    def self_text():
        return attend(query_half[None], text_keys[None], text_values[None], text_allow[None])

    context_self, total_self = lax.cond(stream == 0, self_query, self_text)
    context_half = to_half(context_self[0])
    branch_self = product(context_half, full_output[0])
    after_self = source + branch_self

    def cross_on():
        normed_cross = to_half(norm_rows(after_self, gain_cross))
        cross_half = to_half(product(normed_cross, full_query))
        vision_pair = project_vision(features, full_vision)
        context_cross, total_cross = attend(
            cross_half.reshape(image_count, NQ, feature_width), vision_pair[0], vision_pair[1], None
        )
        context_cross_half = to_half(context_cross.reshape(row_count, feature_width))
        branch = product(context_cross_half, full_output[1])
        return (branch, total_cross, vision_pair, normed_cross, cross_half, context_cross_half)

    def cross_off():
        return (
            jnp.zeros((row_count, feature_width), jnp.float32),
            jnp.zeros((image_count, HEADS, NQ), jnp.float32),
            jnp.zeros((2, image_count, features.shape[1], feature_width), jnp.bfloat16),
            empty_half,
            empty_half,
            empty_half,
        )

    branch_cross, total_cross, vision_pair, normed_cross, cross_half, context_cross_half = lax.cond(
        stream == 0, cross_on, cross_off
    )
    after_cross = after_self + branch_cross
    normed_feed = to_half(norm_rows(after_cross, gain_feed))
    before = right_product(normed_feed, full_expand[0])
    active_half = to_half(exact_gelu(before))
    branch_feed = product(active_half, full_reduce[0])
    result = after_cross + branch_feed
    grad_result = out_grad[0]
    grad_feed_half = to_half(grad_result)
    grad_reduce = left_product(active_half, grad_feed_half)
    grad_active = right_product(grad_feed_half, full_reduce[0])
    grad_before = to_half(jax.vjp(exact_gelu, before)[1](grad_active)[0])
    grad_expand = left_product(grad_before, normed_feed)
    grad_normed_feed = product(grad_before, full_expand[0])
    feed_in, grad_gain_feed = jax.vjp(norm_rows, after_cross, gain_feed)[1](grad_normed_feed)
    grad_cross = grad_result + feed_in

    def cross_back_on():
        grad_branch_half = to_half(grad_cross)
        grad_out_cross = left_product(context_cross_half, grad_branch_half)
        grad_context = to_half(right_product(grad_branch_half, full_output[1]))
        grad_cq, grad_ck, grad_cv = attend_back(
            cross_half.reshape(image_count, NQ, feature_width),
            vision_pair[0],
            vision_pair[1],
            None,
            total_cross,
            grad_context.reshape(image_count, NQ, feature_width),
        )
        grad_cq_half = to_half(grad_cq.reshape(row_count, feature_width))
        grad_pair = to_half(jnp.stack([grad_ck, grad_cv]))
        grad_cross_weight = left_product(normed_cross, grad_cq_half)
        grad_normed_cross = right_product(grad_cq_half, full_query)
        cross_in, grad_gain_cross = jax.vjp(norm_rows, after_self, gain_cross)[1](grad_normed_cross)
        vision_term = vision_grad(features, grad_pair)
        return (cross_in, grad_gain_cross, grad_out_cross, grad_cross_weight, vision_term)

    def cross_back_off():
        square_zero = jnp.zeros((feature_width, feature_width), jnp.float32)
        vision_term = jnp.zeros((2, features.shape[2], feature_width), jnp.float32)
        return (
            jnp.zeros((row_count, feature_width), jnp.float32),
            jnp.zeros((feature_width,), jnp.float32),
            square_zero,
            square_zero,
            vision_term,
        )

    cross_in, grad_gain_cross, grad_out_cross, grad_cross_weight, vision_term = lax.cond(
        stream == 0, cross_back_on, cross_back_off
    )
    grad_after_self = grad_cross + cross_in
    grad_branch_half = to_half(grad_after_self)
    grad_out_self = left_product(context_half, grad_branch_half)
    grad_context_self = to_half(right_product(grad_branch_half, full_output[0]))

    def self_back_query():
        grad_sq, grad_sk, grad_sv = attend_back(
            query_half[None],
            key_half[None],
            value_half[None],
            query_allow[None],
            total_self,
            grad_context_self[None],
        )
        empty_rows = jnp.zeros((row_count, feature_width), jnp.float32)
        return (grad_sq[0], grad_sk[0], grad_sv[0], empty_rows, empty_rows)

    def self_back_text():
        grad_sq, grad_sk, grad_sv = attend_back(
            query_half[None],
            text_keys[None],
            text_values[None],
            text_allow[None],
            total_self,
            grad_context_self[None],
        )
        return (
            grad_sq[0],
            grad_sk[0, row_count:],
            grad_sv[0, row_count:],
            grad_sk[0, :row_count],
            grad_sv[0, :row_count],
        )

    own_query, own_key, own_value, far_grad_key, far_grad_value = lax.cond(
        stream == 0, self_back_query, self_back_text
    )
    own_query = to_half(own_query)
    own_key = to_half(own_key)
    own_value = to_half(own_value)
    far_key_half = to_half(far_grad_key)
    far_value_half = to_half(far_grad_value)
    grad_normed = (
        right_product(own_query, full_project[0])
        + right_product(own_key, full_project[1])
        + right_product(own_value, full_project[2])
    )
    grad_key_weight = left_product(normed_self, own_key)
    grad_value_weight = left_product(normed_self, own_value)
    back_key, back_value = shifted((far_key_half, far_value_half), "stream", -1)
    grad_normed = (
        grad_normed
        + right_product(back_key, full_project[1])
        + right_product(back_value, full_project[2])
    )
    grad_key_weight = grad_key_weight + left_product(normed_self, back_key)
    grad_value_weight = grad_value_weight + left_product(normed_self, back_value)
    grad_project = jnp.stack(
        [left_product(normed_self, own_query), grad_key_weight, grad_value_weight]
    )
    source_in, grad_gain_self = jax.vjp(norm_rows, source, gain_self)[1](grad_normed)
    hidden_grad = grad_after_self + source_in
    zero_row = jnp.zeros_like(grad_gain_feed)
    gain_grads = jnp.stack(
        [
            grad_gain_self,
            grad_gain_cross,
            jnp.where(stream == 0, grad_gain_feed, zero_row),
            jnp.where(stream == 1, grad_gain_feed, zero_row),
        ]
    )
    shared_grads = (
        grad_project,
        jnp.stack([grad_out_self, grad_out_cross]),
        grad_cross_weight,
        vision_term,
        gain_grads,
    )
    (
        parts_project,
        parts_output,
        parts_query,
        parts_vision,
        parts_expand,
        parts_reduce,
        parts_gains,
    ) = (
        lax.psum_scatter(shared_grads[0], "dp", scatter_dimension=1, tiled=True),
        lax.psum_scatter(shared_grads[1], "dp", scatter_dimension=1, tiled=True),
        lax.psum_scatter(shared_grads[2], "dp", scatter_dimension=0, tiled=True),
        lax.psum_scatter(shared_grads[3], "dp", scatter_dimension=1, tiled=True),
        lax.psum_scatter(grad_expand[None], "dp", scatter_dimension=1, tiled=True),
        lax.psum_scatter(grad_reduce[None], "dp", scatter_dimension=1, tiled=True),
        lax.psum_scatter(shared_grads[4], "dp", scatter_dimension=1, tiled=True),
    )
    sum_project, sum_output, sum_query, sum_vision, sum_gains = (
        lax.psum(parts_project.astype(jnp.bfloat16), "stream").astype(jnp.float32),
        lax.psum(parts_output.astype(jnp.bfloat16), "stream").astype(jnp.float32),
        lax.psum(parts_query.astype(jnp.bfloat16), "stream").astype(jnp.float32),
        lax.psum(parts_vision.astype(jnp.bfloat16), "stream").astype(jnp.float32),
        lax.psum(parts_gains.astype(jnp.bfloat16), "stream").astype(jnp.float32),
    )
    shared_square = (
        jnp.sum(sum_project * sum_project)
        + jnp.sum(sum_output * sum_output)
        + jnp.sum(sum_query * sum_query)
        + jnp.sum(sum_vision * sum_vision)
        + jnp.sum(sum_gains * sum_gains)
    )
    local_square = (
        0.5 * shared_square
        + jnp.sum(parts_expand * parts_expand)
        + jnp.sum(parts_reduce * parts_reduce)
    )
    stat_row = jnp.stack(
        [
            square_rows(source),
            square_rows(branch_self),
            square_rows(branch_feed),
            square_rows(result),
        ]
    )
    stat_local = jnp.where(
        jnp.arange(2, dtype=jnp.int32)[:, None] == stream, stat_row[None, :], 0.0
    )
    total_square, stat_sums = lax.psum((local_square, stat_local), ("stream", "dp"))
    return (
        result, hidden_grad, total_square, stat_sums, parts_expand, parts_reduce,
        (sum_project, sum_output, sum_query, sum_vision, sum_gains),
    )


def direct_grads(
    hidden,
    features,
    caption_lengths,
    caption_image,
    out_grad,
    attn_project,
    attn_output,
    cross_query,
    cross_vision,
    feed_expand,
    feed_reduce,
    norm_gains,
):
    stream = lax.axis_index("stream")
    width = attn_project.shape[-1]
    row_count = hidden.shape[1]
    output_half, query_half = to_half(attn_output), to_half(cross_query)
    first = jnp.where(
        stream == 0, to_half(attn_project), jnp.concatenate([output_half, query_half[None]], axis=0)
    )
    vision = to_half(lax.dynamic_index_in_dim(cross_vision, stream, 0, keepdims=False))
    gains = jnp.pad(to_half(norm_gains), ((0, 12), (0, 128 - norm_gains.shape[1])))
    kept = forward_all(
        first, vision, to_half(feed_expand[0]), to_half(feed_reduce[0]), gains,
        hidden[0], out_grad[0], features, caption_lengths, caption_image,
    )
    back = backward_all(kept, hidden[0], caption_lengths, caption_image, features.shape[1])
    sum_first, sum_vision, gain_sums, totals = reduce_all(
        back["first"], back["vision"], back["expand"], back["reduce"], back["gains"], kept["stats"]
    )
    own_gains = norm_gains.shape[1]
    begin = lax.axis_index("dp") * own_gains
    sum_gains = lax.dynamic_slice_in_dim(gain_sums[:4], begin, own_gains, axis=1)
    total_square = jnp.sum(totals[:8])
    stat_sums = jnp.sum(totals[8:], axis=1).reshape(2, 4) / width
    return (
        kept["result"], back["hidden_grad"], total_square, stat_sums,
        back["expand"][None], back["reduce"][None],
        (sum_first[0], sum_first[1, :2], sum_first[1, 2], sum_vision, sum_gains),
    )


def body(
    hidden,
    features,
    caption_lengths,
    caption_image,
    out_grad,
    attn_project,
    attn_output,
    cross_query,
    cross_vision,
    feed_expand,
    feed_reduce,
    norm_gains,
    first_project,
    second_project,
    first_output,
    second_output,
    first_query,
    second_query,
    first_vision,
    second_vision,
    first_expand,
    second_expand,
    first_reduce,
    second_reduce,
    first_gains,
    second_gains,
):
    grads = direct_grads if lax.axis_size("dp") == 16 else general_grads
    row_count = hidden.shape[1]
    result, hidden_grad, total_square, stat_sums, parts_expand, parts_reduce, shared = grads(
        hidden, features, caption_lengths, caption_image, out_grad, attn_project,
        attn_output, cross_query, cross_vision, feed_expand, feed_reduce, norm_gains,
    )
    sum_project, sum_output, sum_query, sum_vision, sum_gains = shared
    grad_norm = jnp.sqrt(total_square)
    rms_values = jnp.sqrt(stat_sums / (row_count * lax.axis_size("dp")))
    factor = clip_norm / jnp.maximum(grad_norm, clip_norm)
    clipped_gains = sum_gains * factor
    fresh_expand, mean_expand, square_expand = adam_step(
        feed_expand, parts_expand, first_expand, second_expand, factor, rate_matrix, decay_rate
    )
    fresh_reduce, mean_reduce, square_reduce = adam_step(
        feed_reduce, parts_reduce, first_reduce, second_reduce, factor, rate_matrix, decay_rate
    )
    weights_shared = (attn_project, attn_output, cross_query, cross_vision, norm_gains)
    firsts_shared = (first_project, first_output, first_query, first_vision, first_gains)
    seconds_shared = (second_project, second_output, second_query, second_vision, second_gains)
    summed_shared = (sum_project, sum_output, sum_query, sum_vision, sum_gains)
    updated = []
    for index in range(5):
        rate = rate_gains if index == 4 else rate_matrix
        decay = 0.0 if index == 4 else decay_rate
        weight = weights_shared[index]
        first = firsts_shared[index]
        second = seconds_shared[index]
        updated.append(adam_step(weight, summed_shared[index], first, second, factor, rate, decay))
    fresh_project, mean_project, square_project = updated[0]
    fresh_output, mean_output, square_output = updated[1]
    fresh_query, mean_query, square_query = updated[2]
    fresh_vision, mean_vision, square_vision = updated[3]
    fresh_gains, mean_gains, square_gains = updated[4]
    return (
        result[None],
        hidden_grad[None],
        grad_norm,
        rms_values,
        fresh_project,
        mean_project,
        square_project,
        fresh_output,
        mean_output,
        square_output,
        fresh_query,
        mean_query,
        square_query,
        fresh_vision,
        mean_vision,
        square_vision,
        fresh_expand,
        mean_expand,
        square_expand,
        fresh_reduce,
        mean_reduce,
        square_reduce,
        fresh_gains,
        mean_gains,
        square_gains,
        clipped_gains,
        to_half(fresh_project),
        to_half(fresh_output),
        to_half(fresh_query),
        to_half(fresh_vision),
        to_half(fresh_expand),
        to_half(fresh_reduce),
    )


def solution(mesh):
    return jax.shard_map(
        body,
        mesh=mesh,
        in_specs=(
            P("stream", "dp", None),
            P("dp", None, None),
            P("dp", None),
            P("dp", None),
            P("stream", "dp", None),
            P(None, "dp", None),
            P(None, "dp", None),
            P("dp", None),
            P(None, "dp", None),
            P("stream", "dp", None),
            P("stream", "dp", None),
            P(None, "dp"),
            P(None, "dp", None),
            P(None, "dp", None),
            P(None, "dp", None),
            P(None, "dp", None),
            P("dp", None),
            P("dp", None),
            P(None, "dp", None),
            P(None, "dp", None),
            P("stream", "dp", None),
            P("stream", "dp", None),
            P("stream", "dp", None),
            P("stream", "dp", None),
            P(None, "dp"),
            P(None, "dp"),
        ),
        out_specs=(
            P("stream", "dp", None),
            P("stream", "dp", None),
            P(),
            P(),
            P(None, "dp", None),
            P(None, "dp", None),
            P(None, "dp", None),
            P(None, "dp", None),
            P(None, "dp", None),
            P(None, "dp", None),
            P("dp", None),
            P("dp", None),
            P("dp", None),
            P(None, "dp", None),
            P(None, "dp", None),
            P(None, "dp", None),
            P("stream", "dp", None),
            P("stream", "dp", None),
            P("stream", "dp", None),
            P("stream", "dp", None),
            P("stream", "dp", None),
            P("stream", "dp", None),
            P(None, "dp"),
            P(None, "dp"),
            P(None, "dp"),
            P(None, "dp"),
            P(None, "dp", None),
            P(None, "dp", None),
            P("dp", None),
            P(None, "dp", None),
            P("stream", "dp", None),
            P("stream", "dp", None),
        ),
        check_vma=False,
    )
```

time: 1830 us -> 409 us (0.22)
  waiting for transfers between devices: 1190 us -> 0 us
  Pallas kernels: 0 us -> 373 us
  matrix products: 266 us -> 0 us
  local copies, waits for them, and re-layouts: 146 us -> 6.01 us
  blocking collectives: 84 us -> 0 us
  other arithmetic: 90.7 us -> 20.1 us
  between operations: 21.6 us -> 2.97 us
    reduce_scatter x6 -> x0, waiting for transfers between devices: 834 us -> none  [the longest x1 173 us: body(): lax.psum_scatter(grad_reduce[None], 'dp', scatter_dimension=1, tiled=True)]
    pallas_call x0 -> x3, Pallas kernels: none -> 373 us  [the longest x1 176 us: forward_all(): pl.pallas_call(forward_kernel, out_shape=[shape for shape, _ in outs.valu...]
    dot_general x44 -> x0, matrix products: 266 us -> none  [the longest x10 45.3 us: right_product(): lax.dot_general(left, right, (((1,), (1,)), ((), ())), preferred_element_...]
    all_gather x6 -> x0, waiting for transfers between devices: 237 us -> none  [the longest x1 79.1 us: body(): lax.all_gather(to_half(cross_vision), 'dp', axis=1, tiled=True)]
    unnamed x15 -> x0, waiting for transfers between devices: 101 us -> none
    all_gather x1 -> x0, blocking collectives: 42.4 us -> none  [body(): lax.all_gather(to_half(norm_gains), 'dp', axis=1, tiled=True)]
    slice x5 -> x1, local copies, waits for them, and re-layouts: 42.5 us -> 0.74 us  [direct_grads(): gain_sums[:4]]
    psum x2 -> x0, blocking collectives: 41.6 us -> none  [the longest x1 39.2 us: body(): lax.psum((local_square, stat_local), ('stream', 'dp'))]
  transfers between devices with their start and end apart: 18 -> 0, of which waited for: 13 -> 0; matrix products, arithmetic and copies ran while one was open for 15% -> 0% of each run, Pallas kernels for 0% -> 0%
where the time goes in v2:
time: 409 us; the launch traced here: 402 us
  Pallas kernels  373 us (91%)
  other arithmetic  20.1 us (5%)
  local copies, waits for them, and re-layouts  6.01 us (1%)
    pallas_call x1, Pallas kernels, forward_all(): pl.pallas_call(forward_kernel, out_shape=[shape for shape, _ in outs.valu...  176 us
    pallas_call x1, Pallas kernels, backward_all(): pl.pallas_call(functools.partial(backward_kernel, feature_rows), out_shap...  114 us
    pallas_call x1, Pallas kernels, reduce_all(): pl.pallas_call(reduce_kernel, out_shape=[jax.ShapeDtypeStruct((2, 3, rows...  82.9 us
    convert_element_type x9, other arithmetic, to_half(): return values.astype(jnp.bfloat16)  15.3 us

profile of v2, /device:TPU:0, one launch (start us, length us, event | category | flops | bytes accessed | tf_op | source)
XLA Modules:
  0.0 402.1 jit_solution(7013212781824047997)
XLA Ops:
  0.7 0.7 convert_element_type.56
  1.4 0.6 pad.4.gains
  2.0 0.9 convert_bitcast_fusion.2
  2.9 1.6 fusion.11.vision
  4.5 1.0 convert_element_type.48
  5.5 1.8 maximum_select_fusion.first
  7.3 2.1 convert_bitcast_fusion
  9.4 176.1 %forward_layer.1 = (f32[512,768]{1,0:T(8,128)}, f32[512,768]{1,0:T(8,128)}, bf16[4,4,2,2,48,768]{5,4,3,2,1,0:T(8,128)(2,1)}, bf16[4,4,2,2,48,768]{5,4,3,2,1,0:T(...) custom-call(bf16[3,48,768]{2,1,0:T(8,128)(2,1)} %maximum_select_fusi, ...), custom_call_target="tpu_custom_call" | custom-call | tf_op jit(solution)/shard_map/forward_layer/pallas_call | solution.py:890
  185.4 114.0 %backward_layer.1 = (f32[512,768]{1,0:T(8,128)}, bf16[2,3,4,2,2,48,768]{6,5,4,3,2,1,0:T(8,128)(2,1)}, bf16[2,1408,768]{2,1,0:T(8,128)(2,1)}, f32[192,768]{1,0:T(...) custom-call(bf16[4,4,2,2,48,768]{5,4,3,2,1,0:T(8,128)(2,1)} %get-tuple-element.65.part_expand, ...), custom_call_target="tpu_custom_call" | custom-call | tf_op jit(solution)/shard_map/backward_layer/pallas_call | solution.py:1488
  299.4 0.0 copy-start.18
  299.4 0.0 copy-start.19
  299.5 0.0 copy-start.20
  299.5 0.0 copy-start.13
  299.5 0.0 copy-start.7
  299.5 0.0 copy-start.4
  299.5 0.0 copy-start.17
  299.5 82.9 %reduce_grads.1 = (f32[2,3,48,768]{3,2,1,0:T(8,128)}, f32[2,88,768]{2,1,0:T(8,128)}, f32[8,768]{1,0:T(8,128)}, f32[16,128]{1,0:T(8,128)}) custom-call(bf16[2,3,4,2,2,48,768]{6,5,4,3,2,1,0:T(8,128)(2,1)} %get-tuple-element.86.part_first, bf16[2,1408,768]{2,1,0:T(8,128)(2,1)} %get-tuple-element.87.part_vision, f32[192,768]{1,0:T(8,128)} %get-tuple-element.88.sum_expand, ...), custom_call_target="tpu_custom_call" | custom-call | tf_op jit(solution)/shard_map/reduce_grads/pallas_call | solution.py:1660
  382.4 0.0 copy-start.8
  382.4 0.0 copy-start.14
  382.5 0.0 copy-start.15
  382.5 0.0 copy-start.16
  382.5 1.5 slice_reduce_fusion
  384.7 0.6 sqrt.32
  385.4 0.7 slice.23
  386.1 0.0 copy-done.18
  386.1 0.0 copy-done.19
  386.1 0.0 copy-done.20
  386.1 0.7 add_subtract_fusion
  386.8 0.0 copy-done.13
  386.8 1.9 fusion.19
  388.7 0.0 copy-done.7
  388.7 0.0 copy-start.1
  388.7 0.0 copy-start.2
  388.7 0.0 copy-start.9
  388.7 0.0 copy-start.10
  388.7 2.4 fusion.22
  391.1 0.0 copy-done.4
  391.1 0.0 copy-done.17
  391.1 2.5 fusion.25
  393.6 0.0 copy-start
  393.6 0.0 copy-start.3
  393.6 0.0 copy-start.11
  393.6 0.0 copy-start.12
  393.6 0.0 copy-done.8
  393.6 0.0 copy-done.14
  393.7 0.0 copy-done.15
  393.7 0.0 copy-done.16
  393.7 1.5 fusion.17
  395.2 0.0 copy-done.1
  395.2 0.0 copy-done.2
  395.2 0.0 copy-done.9
  395.2 0.0 copy-done.10
  395.2 0.0 copy-start.5
  395.2 1.6 fusion.13
  396.8 0.0 copy-start.6
  396.8 0.0 copy-done
  396.8 0.0 copy-done.3
  396.8 0.0 copy-done.11
  396.9 0.0 copy-done.12
  396.9 1.6 fusion.15
  398.5 0.0 copy-done.5
  398.5 1.1 copy.60
  399.6 0.0 copy-done.6
  399.6 1.1 copy.61
  (1 shorter events, 0.0 us)
Async XLA Ops:
  299.4 86.7 %copy-start.18 = (f32[4,48]{1,0:T(4,128)S(1)}, f32[4,48]{1,0:T(4,128)}, u32[]{:S(2)}) copy-start(f32[4,48]{1,0:T(4,128)} %param.37) | copy-start | bytes 2308
  299.4 86.7 %copy-start.19 = (f32[4,48]{1,0:T(4,128)S(1)}, f32[4,48]{1,0:T(4,128)}, u32[]{:S(2)}) copy-start(f32[4,48]{1,0:T(4,128)} %param.50) | copy-start | bytes 2308
  299.5 86.6 %copy-start.20 = (f32[4,48]{1,0:T(4,128)S(1)}, f32[4,48]{1,0:T(4,128)}, u32[]{:S(2)}) copy-start(f32[4,48]{1,0:T(4,128)} %param.51) | copy-start | bytes 2308
  299.5 87.3 %copy-start.13 = (f32[48,768]{1,0:T(8,128)S(1)}, f32[48,768]{1,0:T(8,128)}, u32[]{:S(2)}) copy-start(f32[48,768]{1,0:T(8,128)} %param.33) | copy-start | bytes 442372
  299.5 89.2 %copy-start.7 = (f32[2,48,768]{2,1,0:T(8,128)S(1)}, f32[2,48,768]{2,1,0:T(8,128)}, u32[]{:S(2)}) copy-start(f32[2,48,768]{2,1,0:T(8,128)} %param.32) | copy-start | bytes 884740
  299.5 91.6 %copy-start.4 = (f32[3,48,768]{2,1,0:T(8,128)S(1)}, f32[3,48,768]{2,1,0:T(8,128)}, u32[]{:S(2)}) copy-start(f32[3,48,768]{2,1,0:T(8,128)} %param.31) | copy-start | bytes 1327108
  299.5 91.6 %copy-start.17 = (f32[3,48,768]{2,1,0:T(8,128)S(1)}, f32[3,48,768]{2,1,0:T(8,128)}, u32[]{:S(2)}) copy-start(f32[3,48,768]{2,1,0:T(8,128)} %param.38) | copy-start | bytes 1327108
  382.4 11.2 %copy-start.8 = (f32[2,88,768]{2,1,0:T(8,128)S(1)}, f32[2,88,768]{2,1,0:T(8,128)}, u32[]{:S(2)}) copy-start(f32[2,88,768]{2,1,0:T(8,128)} %param.34) | copy-start | bytes 1622020
  382.4 11.2 %copy-start.14 = (f32[2,88,768]{2,1,0:T(8,128)S(1)}, f32[2,88,768]{2,1,0:T(8,128)}, u32[]{:S(2)}) copy-start(f32[2,88,768]{2,1,0:T(8,128)} %param.44) | copy-start | bytes 1622020
  382.5 11.2 %copy-start.15 = (f32[2,88,768]{2,1,0:T(8,128)S(1)}, f32[2,88,768]{2,1,0:T(8,128)}, u32[]{:S(2)}) copy-start(f32[2,88,768]{2,1,0:T(8,128)} %param.45) | copy-start | bytes 1622020
  382.5 11.2 %copy-start.16 = (f32[2,88,768]{2,1,0:T(8,128)S(1)}, f32[2,88,768]{2,1,0:T(8,128)}, u32[]{:S(2)}) copy-start(f32[2,88,768]{2,1,0:T(8,128)} %get-tuple-element.94) | copy-start | bytes 1622020
  388.7 6.5 %copy-start.1 = (f32[192,768]{1,0:T(8,128)S(1)}, f32[192,768]{1,0:T(8,128)}, u32[]{:S(2)}) copy-start(f32[192,768]{1,0:T(8,128)} %get-tuple-element.89.sum_reduce) | copy-start | bytes 1769476
  388.7 6.5 %copy-start.2 = (f32[1,192,768]{2,1,0:T(8,128)S(1)}, f32[1,192,768]{2,1,0:T(8,128)}, u32[]{:S(2)}) copy-start(f32[1,192,768]{2,1,0:T(8,128)} %param.36) | copy-start | bytes 1769476
  388.7 6.5 %copy-start.9 = (f32[1,192,768]{2,1,0:T(8,128)S(1)}, f32[1,192,768]{2,1,0:T(8,128)}, u32[]{:S(2)}) copy-start(f32[1,192,768]{2,1,0:T(8,128)} %param.48) | copy-start | bytes 1769476
  388.7 6.5 %copy-start.10 = (f32[1,192,768]{2,1,0:T(8,128)S(1)}, f32[1,192,768]{2,1,0:T(8,128)}, u32[]{:S(2)}) copy-start(f32[1,192,768]{2,1,0:T(8,128)} %param.49) | copy-start | bytes 1769476
  393.6 3.2 copy-start
  393.6 3.2 copy-start.3
  393.6 3.2 copy-start.11
  393.6 3.2 copy-start.12
  395.2 3.3 copy-start.5
  396.8 2.8 copy-start.6
